TPU v7x, 32 devices: a whole 2x2x4 slice. The times are simulated.
32 devices in a mesh: groups: 2 (over x), hi: 8 (over z, y), lo: 2 (over core).
Axes of the slice: x: 2, y: 2, z: 4, core: 2. Of those that a mesh axis runs over, the one named last changes fastest.
Arguments:
- vectors: float32 [64, 65536], P(None, ('groups', 'hi', 'lo')), parts along dimension 1, may hold values from -6 to 6
- tile_values: float32 [2048, 128, 128], P(('groups', 'hi', 'lo')), parts along dimension 0, may hold values from -0.25 to 0.25
- tile_cols: int32 [1024], P(('hi', 'lo')), may hold values from 0 to 15, as said below
- live_rows: int32 [16], P(('hi', 'lo')), may hold values from 512 to 2048
- boundary_map: int32 [32768], P(('hi', 'lo')), may hold values from -1 to 2047
- field_levels: int32 [8], P('groups'), parts along dimension 0, may hold values from -8 to 8
Outputs:
- filtered: float32 [64, 65536], P(None, ('groups', 'hi', 'lo')), parts along dimension 1
- correlation: float32 [128, 64], P('groups'), parts along dimension 0
- projected: float32 [128, 64], P('groups'), parts along dimension 0
There are 2 independent parts, one for each index of `groups`. A program takes and returns all parts, laid end to end along the dimension named above; an argument that names none is the same for every part. Nothing has to cross between parts.
Inputs may be any that keep to these rules, and one draw needn't show every extreme that they name: `tile_cols`: each row block's 4 column blocks are distinct.
All inputs are finite; a program needn't handle non-finite values.
Results may differ from a plain program's by a relative error of at most 0.0001.
Values sent between devices are 32-bit elements; how exact they have to be, the bound alone decides.
No kernel may reach another device: no remote copies, remote signals or barrier semaphores. Data moves between devices by JAX's collectives and lax.ppermute only.
A program may use at most 64 MiB of HBM per device.

v0:
```python
import functools

import jax
import jax.numpy as jnp
from jax import lax
from jax.experimental import pallas as pl
from jax.experimental.pallas import tpu as pltpu
from jax.sharding import PartitionSpec as P

HOP_SCALE = 0.5
ANISOTROPY = 1.0
FIELD_STEP = 0.25
HALF_WIDTH = 4.0
AXES = ("hi", "lo")
STEPS = 4
F32, BF16 = jnp.float32, jnp.bfloat16
SMEM = pl.BlockSpec(memory_space=pltpu.SMEM)
LIMIT = 32 * 1024 * 1024


def bit(number, place):
    return (number >> place) & 1


def halves(value):
    head = value.astype(BF16)
    return head, (value - head.astype(F32)).astype(BF16)


def stacked(value):
    return jnp.concatenate(halves(value), axis=0)


def product(left, right):
    rows, columns = left.shape[0] // 2, right.shape[0] // 2
    whole = lax.dot_general(left, right, (((1,), (1,)), ((), ())), preferred_element_type=F32)
    tails = whole[:rows, columns:] + whole[rows:, :columns] + whole[rows:, columns:]
    return whole[:rows, :columns] + tails


def coupling(config, bond):
    differ = bit(config, bond) ^ bit(config, bond + 1)
    return jnp.where(differ == 1, HOP_SCALE, 0.0)


def onsite_of(config, fields_ref):
    count = fields_ref.shape[0]
    spins = [bit(config, place).astype(F32) - 0.5 for place in range(count)]
    total = jnp.float32(0.0)
    for place in range(count):
        total += fields_ref[place].astype(F32) * FIELD_STEP * spins[place]
    for place in range(count - 1):
        total += ANISOTROPY * spins[place] * spins[place + 1]
    return total


def alive_of(live_ref, first, count):
    rows = lax.broadcasted_iota(jnp.int32, (1, count), 1) + first
    return (rows < live_ref[0]).astype(F32)


def own_block(block, config, cols_ref, fields_ref, field_ref, split_ref, flipped_ref, tiles_ref, map_ref):
    per_block, tile = tiles_ref.shape[1], tiles_ref.shape[2]
    span = pl.ds(pl.multiple_of(block * tile, tile), tile)
    picked = []
    for which in range(per_block):
        column = cols_ref[block * per_block + which]
        picked.append(split_ref[:, pl.ds(pl.multiple_of(column * tile, tile), tile)])
    weights = jnp.concatenate([tiles_ref[block, which] for which in range(per_block)], axis=1)
    total = product(jnp.concatenate(picked, axis=1), stacked(weights))
    total += onsite_of(config, fields_ref) * field_ref[:, span]
    targets = jnp.broadcast_to(map_ref[:, span], (8, tile))
    inside, outside = targets & (tile - 1), targets // tile
    outside = jnp.where(targets < 0, -1, outside)
    groups = []
    for group in range(field_ref.shape[0] // 8):
        found = jnp.zeros((8, tile), F32)
        for source in range(field_ref.shape[1] // tile):
            values = flipped_ref[group * 8 : group * 8 + 8, source * tile : (source + 1) * tile]
            moved = jnp.take_along_axis(values, inside, axis=1)
            found = jnp.where(outside == source, moved, found)
        groups.append(found)
    return span, total + HOP_SCALE * jnp.concatenate(groups, axis=0)


def own_kernel(place_ref, cols_ref, fields_ref, field_ref, flipped_ref, tiles_ref, map_ref, out_ref, split_ref):
    blocks = tiles_ref.shape[0] // STEPS
    split_ref[...] = stacked(field_ref[...])

    def body(step, carry):
        for row in range(blocks):
            span, total = own_block(
                step * blocks + row, place_ref[0], cols_ref, fields_ref, field_ref, split_ref, flipped_ref, tiles_ref, map_ref
            )
            out_ref[:, span] = total
        return carry

    lax.fori_loop(0, STEPS, body, 0)


def own_gram_kernel(
    place_ref, cols_ref, fields_ref, live_ref, field_ref, flipped_ref, tiles_ref, map_ref, out_ref, copy_ref, split_ref, sem
):
    blocks, tile = tiles_ref.shape[0] // STEPS, tiles_ref.shape[2]
    count, width = field_ref.shape[0], blocks * tile
    copy = pltpu.make_async_copy(field_ref, copy_ref, sem)
    copy.start()
    split_ref[...] = stacked(field_ref[...])
    out_ref[:, :count] = product(split_ref[...], split_ref[...])
    out_ref[:, count:] = jnp.zeros((count, count), F32)

    def body(step, carry):
        parts = []
        for row in range(blocks):
            block = step * blocks + row
            span, total = own_block(
                block, place_ref[0], cols_ref, fields_ref, field_ref, split_ref, flipped_ref, tiles_ref, map_ref
            )
            parts.append(alive_of(live_ref, block * tile, tile) * total)
        image = stacked(jnp.concatenate(parts, axis=1))
        span = pl.ds(pl.multiple_of(step * width, width), width)
        out_ref[:, count:] += product(split_ref[:, span], image)
        return carry

    lax.fori_loop(0, STEPS, body, 0)
    copy.wait()


def hop_sum(bonds, config, refs):
    total = coupling(config, 0) * refs[-1][...]
    total += coupling(config, 1) * jnp.concatenate([refs[-3][...], refs[-2][...]], axis=0)
    for bond, ref in zip(reversed(range(2, bonds)), refs):
        total += coupling(config, bond) * ref[...]
    return total


def store_halves(value, out_ref, first_ref, second_ref):
    middle = first_ref.shape[0]
    out_ref[...] = value
    first_ref[...] = value[:middle]
    second_ref[...] = value[middle:]


def start_kernel(live_ref, vectors_ref, out_ref, first_ref, second_ref):
    start = vectors_ref[...] * alive_of(live_ref, 0, vectors_ref.shape[1])
    store_halves(start, out_ref, first_ref, second_ref)


def combine_kernel(bonds, place_ref, live_ref, own_ref, *refs):
    hops, outs = refs[:-3], refs[-3:]
    total = own_ref[...] + hop_sum(bonds, place_ref[0], hops)
    store_halves(alive_of(live_ref, 0, total.shape[1]) * total * (1.0 / HALF_WIDTH), *outs)


def filter_kernel(bonds, place_ref, live_ref, own_ref, start_ref, *refs):
    hops, (kept_ref, sent_ref, lead_ref, rest_ref) = refs[:-4], refs[-4:]
    total = own_ref[...] + hop_sum(bonds, place_ref[0], hops)
    image = alive_of(live_ref, 0, total.shape[1]) * total * (1.0 / HALF_WIDTH)
    second = 2.0 * image - start_ref[...]
    kept_ref[...] = second
    lead_ref[...] = second[:, : lead_ref.shape[1]]
    rest_ref[...] = second[:, lead_ref.shape[1] :]
    width = sent_ref.shape[1]
    sent_ref[...] = jnp.where(place_ref[1] == 0, second[:, :width], second[:, width:])


def crossed_kernel(bonds, states, place_ref, own_ref, field_ref, *refs):
    hops, out_ref = refs[:-1], refs[-1]
    count = own_ref.shape[0]
    near = coupling(place_ref[0], 1) * hops[-1][...]
    theirs = jnp.where(place_ref[1] == 0, 0.0, near), jnp.where(place_ref[1] == 0, near, 0.0)
    theirs = jnp.concatenate(theirs, axis=1)
    for lead, rest in zip(hops, hops[bonds - 2 : -1]):
        theirs += HOP_SCALE * jnp.concatenate([lead[...], rest[...]], axis=1)
    crossed = product(stacked(field_ref[...]), stacked(theirs))
    out_ref[:, :count] = own_ref[:, :count] * (1.0 / states)
    projected = own_ref[:, count:] + crossed + crossed.T
    out_ref[:, count:] = projected * (1.0 / (HALF_WIDTH * states))


def local(vectors, tile_values, tile_cols, live_rows, boundary_map, field_levels):
    dev_count = lax.axis_size(AXES)
    bonds = dev_count.bit_length() - 2
    flip = (dev_count - 1) // 3
    position = lax.axis_index(AXES)
    parity = sum(bit(position, place) for place in range(0, bonds + 1, 2)) & 1
    place = jnp.stack([position ^ flip, parity]).astype(jnp.int32)
    vec_count, row_count = vectors.shape
    tile_size = tile_values.shape[1]
    block_count = row_count // tile_size
    per_block = tile_values.shape[0] // block_count
    tiles = tile_values.reshape(block_count, per_block, tile_size, tile_size)
    targets = boundary_map.reshape(1, row_count)
    params = pltpu.CompilerParams(vmem_limit_bytes=LIMIT)

    def coupled(here, bond):
        return bit(here ^ flip, bond) != bit(here ^ flip, bond + 1)

    def hop(value, bond):
        pairs = [(here, here ^ (3 << bond) if coupled(here, bond) else here) for here in range(dev_count)]
        return lax.ppermute(value, AXES, pairs)

    def one_way(value, bond, lead):
        pairs = []
        for here in range(dev_count):
            ahead = bit(here, bond) ^ bit(here, bond - 1) == lead
            if coupled(here, bond) and ahead:
                pairs.append((here, here ^ (3 << bond)))
            if bond == 2 and coupled(here, 0) and not ahead:
                pairs.append((here, here ^ 3))
        return lax.ppermute(value, AXES, pairs)

    def near(flipped):
        pairs = [(here, here ^ (1 if coupled(here, 0) else 2)) for here in range(dev_count)]
        return lax.ppermute(flipped, AXES, pairs)

    def exchange(value, mask):
        return lax.ppermute(value, AXES, [(source, source ^ mask) for source in range(dev_count)])

    inside = pl.BlockSpec(memory_space=pltpu.VMEM)
    own_cost = pl.CostEstimate(
        flops=8 * vec_count * row_count * per_block * tile_size,
        bytes_accessed=4 * tile_values.size + 12 * vec_count * row_count,
        transcendentals=0,
    )
    split = pltpu.VMEM((2 * vec_count, row_count), BF16)
    gram_shape = jax.ShapeDtypeStruct((vec_count, 2 * vec_count), F32)

    def rows_by(count, width):
        return jax.ShapeDtypeStruct((count, width), F32)

    full = rows_by(vec_count, row_count)

    def own_part(field, flipped):
        return pl.pallas_call(
            own_kernel,
            out_shape=full,
            in_specs=[SMEM] * 3 + [inside] * 4,
            out_specs=inside,
            scratch_shapes=[split],
            compiler_params=params,
            cost_estimate=own_cost,
            name="own",
        )(place, tile_cols, field_levels, field, flipped, tiles, targets)

    def own_gram(field, flipped):
        return pl.pallas_call(
            own_gram_kernel,
            out_shape=[gram_shape, full],
            in_specs=[SMEM] * 4 + [inside] * 4,
            out_specs=[inside, pl.BlockSpec(memory_space=pl.ANY)],
            scratch_shapes=[split, pltpu.SemaphoreType.DMA(())],
            compiler_params=params,
            cost_estimate=own_cost,
            name="own_gram",
        )(place, tile_cols, field_levels, live_rows, field, flipped, tiles, targets)

    three = [full, rows_by(vec_count // 2, row_count), rows_by(vec_count // 2, row_count)]

    def apply(field, first_half, second_half):
        legs = [(here, here ^ 2) for here in range(dev_count) if coupled(here, 1)]
        round_way = [(here, here ^ 4) for here in range(dev_count) if not coupled(here, 1)]
        flipped = exchange(field, 1)
        far = [hop(field, bond) for bond in reversed(range(2, bonds))]
        aside = lax.ppermute(lax.ppermute(second_half, AXES, legs), AXES, round_way)
        direct = hop(first_half, 1)
        closest = near(flipped)
        return own_part(field, flipped), far + [direct, aside, closest]

    start, *halves_of = pl.pallas_call(
        start_kernel,
        out_shape=three,
        in_specs=[SMEM, inside],
        out_specs=[inside] * 3,
        compiler_params=params,
        name="start",
    )(live_rows, vectors)
    own, hops = apply(start, *halves_of)
    first, *halves_of = pl.pallas_call(
        functools.partial(combine_kernel, bonds),
        out_shape=three,
        in_specs=[SMEM] * 2 + [inside] * (bonds + 2),
        out_specs=[inside] * 3,
        compiler_params=params,
        name="combine",
    )(place, live_rows, own, *hops)
    own, hops = apply(first, *halves_of)
    cut = row_count * 3 // 4
    kept, sent, lead, rest = pl.pallas_call(
        functools.partial(filter_kernel, bonds),
        out_shape=[full] + [rows_by(vec_count, width) for width in (row_count // 2, cut, row_count - cut)],
        in_specs=[SMEM] * 2 + [inside] * (bonds + 3),
        out_specs=[inside] * 4,
        compiler_params=params,
        name="filter",
    )(place, live_rows, own, start, *hops)
    flipped = exchange(kept, 1)
    hops = [one_way(lead, bond, 1) for bond in reversed(range(2, bonds))]
    flipped, sent, rest = lax.optimization_barrier((flipped, sent, rest))
    hops += [one_way(rest, bond, 0) for bond in reversed(range(2, bonds))]
    hops += [hop(sent, 1)]
    grams, second = own_gram(kept, flipped)
    sums = pl.pallas_call(
        functools.partial(crossed_kernel, bonds, dev_count * row_count),
        out_shape=gram_shape,
        in_specs=[SMEM] + [inside] * (2 * bonds - 1),
        out_specs=inside,
        compiler_params=params,
        name="crossed",
    )(place, grams, kept, *hops)
    sums = sums + exchange(sums, 1)
    for digit in range(1, bonds + 1, 2):
        near_mask, far_mask = 1 << digit, 2 << digit
        pair = sums + exchange(sums, near_mask)
        if far_mask < dev_count:
            pair = pair + (exchange(sums, far_mask) + exchange(sums, near_mask | far_mask))
        sums = pair
    return (second, sums[:, :vec_count], sums[:, vec_count:])


def solution(mesh):
    in_specs = (
        P(None, ("groups", "hi", "lo")),
        P(("groups", "hi", "lo"), None, None),
        P(("hi", "lo")),
        P(("hi", "lo")),
        P(("hi", "lo")),
        P("groups"),
    )
    out_specs = (P(None, ("groups", "hi", "lo")), P("groups", None), P("groups", None))
    return jax.shard_map(local, mesh=mesh, in_specs=in_specs, out_specs=out_specs, check_vma=False)
```

profile of v0, /device:TPU:0, one launch (start us, length us, event | category | flops | bytes accessed | tf_op | source)
XLA Modules:
  0.0 87.2 jit_solution(18355050314186475914)
XLA Ops:
  1.3 1.0 %copy-done.2 = f32[64,2048]{1,0:T(8,128)S(1)} copy-done((f32[64,2048]{1,0:T(8,128)S(1)}, f32[64,2048]{1,0:T(8,128)}, u32[]{:S(2)}) %copy-start.2) | copy-done | bytes 524312
  2.3 0.1 start.1
  2.4 0.5 collective-permute-start
  2.9 4.4 %collective-permute-start.3 = (f32[32,2048]{1,0:T(8,128)S(1)}, f32[32,2048]{1,0:T(8,128)S(1)}, u32[]{:S(2)}, u32[]{:S(2)}) collective-permute-start(f32[32,2048]{1,0:T(8,128)S(1)} %get-tuple-element.20), channel_id=1, source_target_pairs={{0,2},{1,3},{6,4},{7,5},{8,10},{9,11},{14,12},{15,13},{16,18},{17,... | collective-permute-start | bytes 786440 | tf_op jit(solution)/shard_map/ppermute | solution.py:265
  7.4 3.4 %collective-permute-start.1 = (f32[64,2048]{1,0:T(8,128)S(1)}, f32[64,2048]{1,0:T(8,128)S(1)}, u32[]{:S(2)}, u32[]{:S(2)}) collective-permute-start(f32[64,2048]{1,0:T(8,128)S(1)} %get-tuple-element.18.field_ref.start_ref), channel_id=1, source_target_pairs={{0,12},{1,13},{2,14},{3,15},{4,4},{5,5},{6,6},{7,7},{8,8},{9,9},{1... | collective-permute-start | bytes 1572872 | tf_op jit(solution)/shard_map/ppermute | solution.py:201
  10.8 0.2 collective-permute-start.5
  11.0 1.9 %collective-permute-start.2 = (f32[32,2048]{1,0:T(8,128)S(1)}, f32[32,2048]{1,0:T(8,128)S(1)}, u32[]{:S(2)}, u32[]{:S(2)}) collective-permute-start(f32[32,2048]{1,0:T(8,128)S(1)} %get-tuple-element.19), channel_id=1, source_target_pairs={{0,6},{1,7},{2,2},{3,3},{4,4},{5,5},{6,0},{7,1},{8,14},{9,15},{10,... | collective-permute-start | bytes 786440 | tf_op jit(solution)/shard_map/ppermute | solution.py:201
  12.9 0.7 collective-permute-done.3
  13.6 1.3 %collective-permute-start.4 = (f32[32,2048]{1,0:T(8,128)S(1)}, f32[32,2048]{1,0:T(8,128)S(1)}, u32[]{:S(2)}, u32[]{:S(2)}) collective-permute-start(f32[32,2048]{1,0:T(8,128)S(1)} %collective-permute-done.3), channel_id=1, source_target_pairs={{2,6},{3,7},{4,0},{5,1},{10,14},{11,15},{12,8},{13,9},{18,22},{19,... | collective-permute-start | bytes 786440 | tf_op jit(solution)/shard_map/ppermute | solution.py:265
  14.8 0.1 pad_add_fusion.place_ref
  14.9 2.2 %copy-done = f32[64,128,128]{2,1,0:T(8,128)S(1)} copy-done((f32[64,128,128]{2,1,0:T(8,128)S(1)}, f32[64,128,128]{2,1,0:T(8,128)}, u32[]{:S(2)}) %copy-start) | copy-done | bytes 4194328
  17.1 0.7 copy-done.3
  17.8 0.7 copy-done.4
  18.5 0.7 copy-done.5
  19.1 3.6 %own.2.own_ref = f32[64,2048]{1,0:T(8,128)S(1)} custom-call(s32[2]{0:T(128)S(1)} %pad_add_fusion.place_ref, s32[64]{0:T(128)S(1)} %copy-done.4, s32[4]{0:T(128)S(1)} %copy-done.5, f32[64,2048]{1,0:T(8,128)S(1)} %get-tuple-element.18.field_ref.start_ref, f32[64,2048]{1,0:T(8,128)S(1)} %collective-permute-done.flipped_ref, f32[16,4,128,128]{3,2,1,0:T(8,128)S(1)} %bitcast.4, ...), custom_call_target="tpu_custom_call" | custom-call | flops 536870912 | bytes 5767168 | tf_op jit(solution)/shard_map/own/pallas_call | solution.py:235
  22.7 7.9 %collective-permute-done.2.refs_1_ = f32[32,2048]{1,0:T(8,128)S(1)} collective-permute-done((f32[32,2048]{1,0:T(8,128)S(1)}, f32[32,2048]{1,0:T(8,128)S(1)}, u32[]{:S(2)}, u32[]{:S(2)}) %collective-permute-start.2) | collective-permute-done | bytes 262176 | tf_op jit(solution)/shard_map/ppermute | solution.py:201
  30.6 0.0 collective-permute-done.4.refs_2_
  30.7 0.7 combine.1
  31.4 0.2 collective-permute-start.6
  31.6 1.9 %collective-permute-start.7 = (f32[64,2048]{1,0:T(8,128)S(1)}, f32[64,2048]{1,0:T(8,128)S(1)}, u32[]{:S(2)}, u32[]{:S(2)}) collective-permute-start(f32[64,2048]{1,0:T(8,128)S(1)} %get-tuple-element.21.field_ref), channel_id=1, source_target_pairs={{0,12},{1,13},{2,14},{3,15},{4,4},{5,5},{6,6},{7,7},{8,8},{9,9},{1... | collective-permute-start | bytes 1572872 | tf_op jit(solution)/shard_map/ppermute | solution.py:201
  33.5 6.0 %collective-permute-start.9 = (f32[32,2048]{1,0:T(8,128)S(1)}, f32[32,2048]{1,0:T(8,128)S(1)}, u32[]{:S(2)}, u32[]{:S(2)}) collective-permute-start(f32[32,2048]{1,0:T(8,128)S(1)} %get-tuple-element.23), channel_id=1, source_target_pairs={{0,2},{1,3},{6,4},{7,5},{8,10},{9,11},{14,12},{15,13},{16,18},{17,... | collective-permute-start | bytes 786440 | tf_op jit(solution)/shard_map/ppermute | solution.py:265
  39.5 0.0 collective-permute-start.11
  39.5 1.9 %collective-permute-start.8 = (f32[32,2048]{1,0:T(8,128)S(1)}, f32[32,2048]{1,0:T(8,128)S(1)}, u32[]{:S(2)}, u32[]{:S(2)}) collective-permute-start(f32[32,2048]{1,0:T(8,128)S(1)} %get-tuple-element.22), channel_id=1, source_target_pairs={{0,6},{1,7},{2,2},{3,3},{4,4},{5,5},{6,0},{7,1},{8,14},{9,15},{10,... | collective-permute-start | bytes 786440 | tf_op jit(solution)/shard_map/ppermute | solution.py:201
  41.4 4.7 %collective-permute-done.9 = f32[32,2048]{1,0:T(8,128)S(1)} collective-permute-done((f32[32,2048]{1,0:T(8,128)S(1)}, f32[32,2048]{1,0:T(8,128)S(1)}, u32[]{:S(2)}, u32[]{:S(2)}) %collective-permute-start.9) | collective-permute-done | bytes 262176 | tf_op jit(solution)/shard_map/ppermute | solution.py:265
  46.1 1.3 %collective-permute-start.10 = (f32[32,2048]{1,0:T(8,128)S(1)}, f32[32,2048]{1,0:T(8,128)S(1)}, u32[]{:S(2)}, u32[]{:S(2)}) collective-permute-start(f32[32,2048]{1,0:T(8,128)S(1)} %collective-permute-done.9), channel_id=1, source_target_pairs={{2,6},{3,7},{4,0},{5,1},{10,14},{11,15},{12,8},{13,9},{18,22},{19,... | collective-permute-start | bytes 786440 | tf_op jit(solution)/shard_map/ppermute | solution.py:265
  47.4 3.6 %own.3.own_ref = f32[64,2048]{1,0:T(8,128)S(1)} custom-call(s32[2]{0:T(128)S(1)} %pad_add_fusion.place_ref, s32[64]{0:T(128)S(1)} %copy-done.4, s32[4]{0:T(128)S(1)} %copy-done.5, f32[64,2048]{1,0:T(8,128)S(1)} %get-tuple-element.21.field_ref, f32[64,2048]{1,0:T(8,128)S(1)} %collective-permute-done.6.flipped_ref, f32[16,4,128,128]{3,2,1,0:T(8,128)S(1)} %bitcast.5, ...), custom_call_target="tpu_custom_call" | custom-call | flops 536870912 | bytes 5767168 | tf_op jit(solution)/shard_map/own/pallas_call | solution.py:235
  51.0 4.1 %collective-permute-done.8.refs_1_ = f32[32,2048]{1,0:T(8,128)S(1)} collective-permute-done((f32[32,2048]{1,0:T(8,128)S(1)}, f32[32,2048]{1,0:T(8,128)S(1)}, u32[]{:S(2)}, u32[]{:S(2)}) %collective-permute-start.8) | collective-permute-done | bytes 262176 | tf_op jit(solution)/shard_map/ppermute | solution.py:201
  55.1 0.1 collective-permute-done.10.refs_2_
  55.2 0.0 collective-permute-done.11.refs_3_
  55.2 0.8 filter.1
  56.0 0.1 collective-permute-start.12
  56.1 1.9 %collective-permute-start.13 = (f32[64,1536]{1,0:T(8,128)S(1)}, f32[64,1536]{1,0:T(8,128)S(1)}, u32[]{:S(2)}, u32[]{:S(2)}) collective-permute-start(f32[64,1536]{1,0:T(8,128)S(1)} %get-tuple-element.30), channel_id=1, source_target_pairs={{0,3},{2,14},{3,15},{7,4},{8,11},{12,0},{13,1},{15,12},{16,19},{18... | collective-permute-start | bytes 1179656 | tf_op jit(solution)/shard_map/ppermute | solution.py:211
  58.0 0.0 collective-permute-done.12.flipped_ref
  58.0 3.5 %collective-permute-start.15 = (f32[64,1024]{1,0:T(8,128)S(1)}, f32[64,1024]{1,0:T(8,128)S(1)}, u32[]{:S(2)}, u32[]{:S(2)}) collective-permute-start(f32[64,1024]{1,0:T(8,128)S(1)} %get-tuple-element.32), channel_id=1, source_target_pairs={{0,6},{1,7},{2,2},{3,3},{4,4},{5,5},{6,0},{7,1},{8,14},{9,15},{10,... | collective-permute-start | bytes 786440 | tf_op jit(solution)/shard_map/ppermute | solution.py:201
  61.5 2.9 %collective-permute-start.14 = (f32[64,512]{1,0:T(8,128)S(1)}, f32[64,512]{1,0:T(8,128)S(1)}, u32[]{:S(2)}, u32[]{:S(2)}) collective-permute-start(f32[64,512]{1,0:T(8,128)S(1)} %get-tuple-element.31), channel_id=1, source_target_pairs={{0,12},{1,13},{3,0},{4,7},{11,8},{12,15},{14,2},{15,3},{16,28},{17... | collective-permute-start | bytes 393224 | tf_op jit(solution)/shard_map/ppermute | solution.py:211
  64.4 5.7 %own_gram.1 = (f32[64,128]{1,0:T(8,128)S(1)}, f32[64,2048]{1,0:T(8,128)}) custom-call(s32[2]{0:T(128)S(1)} %pad_add_fusion.place_ref, s32[64]{0:T(128)S(1)} %copy-done.4, s32[4]{0:T(128)S(1)} %copy-done.5, s32[1]{0:T(128)S(6)} %copy.9.live_ref, f32[64,2048]{1,0:T(8,128)S(1)} %get-tuple-element.24.field_ref, ...), custom_call_target="tpu_custom_call" | custom-call | flops 536870912 | bytes 5767168 | tf_op jit(solution)/shard_map/own_gram/pallas_call | solution.py:247
  70.2 1.1 %collective-permute-done.13.refs_0_ = f32[64,1536]{1,0:T(8,128)S(1)} collective-permute-done((f32[64,1536]{1,0:T(8,128)S(1)}, f32[64,1536]{1,0:T(8,128)S(1)}, u32[]{:S(2)}, u32[]{:S(2)}) %collective-permute-start.13) | collective-permute-done | bytes 393248 | tf_op jit(solution)/shard_map/ppermute | solution.py:211
  71.3 1.1 %crossed.1 = f32[64,128]{1,0:T(8,128)S(1)} custom-call(s32[2]{0:T(128)S(1)} %pad_add_fusion.place_ref, f32[64,128]{1,0:T(8,128)S(1)} %get-tuple-element.29.own_ref, f32[64,2048]{1,0:T(8,128)S(1)} %get-tuple-element.24.field_ref, f32[64,1536]{1,0:T(8,128)S(1)} %collective-permute-done.13.refs_0_, f32[64,512]{1,0:T(8,128)S(1)} %collective-permute-done.14.refs_1_, ...), custom_call_target="tpu_custom_call" | custom-call | tf_op jit(solution)/shard_map/crossed/pallas_call | solution.py:303
  72.4 0.1 collective-permute-start.16
  72.5 1.2 %collective-permute-done.16 = f32[64,128]{1,0:T(8,128)S(1)} collective-permute-done((f32[64,128]{1,0:T(8,128)S(1)}, f32[64,128]{1,0:T(8,128)S(1)}, u32[]{:S(2)}, u32[]{:S(2)}) %collective-permute-start.16) | collective-permute-done | bytes 32800 | tf_op jit(solution)/shard_map/ppermute | solution.py:218
  73.7 0.3 collective-permute-start.19
  74.1 3.5 %collective-permute-start.18 = (f32[64,128]{1,0:T(8,128)S(1)}, f32[64,128]{1,0:T(8,128)S(1)}, u32[]{:S(2)}, u32[]{:S(2)}) collective-permute-start(f32[64,128]{1,0:T(8,128)S(1)} %add.23), channel_id=1, source_target_pairs={{0,4},{1,5},{2,6},{3,7},{4,0},{5,1},{6,2},{7,3},{8,12},{9,13},{10,... | collective-permute-start | bytes 98312 | tf_op jit(solution)/shard_map/ppermute | solution.py:218
  77.6 1.1 %collective-permute-done.19 = f32[64,128]{1,0:T(8,128)S(1)} collective-permute-done((f32[64,128]{1,0:T(8,128)S(1)}, f32[64,128]{1,0:T(8,128)S(1)}, u32[]{:S(2)}, u32[]{:S(2)}) %collective-permute-start.19) | collective-permute-done | bytes 32800 | tf_op jit(solution)/shard_map/ppermute | solution.py:218
  78.7 1.2 %collective-permute-done.18 = f32[64,128]{1,0:T(8,128)S(1)} collective-permute-done((f32[64,128]{1,0:T(8,128)S(1)}, f32[64,128]{1,0:T(8,128)S(1)}, u32[]{:S(2)}, u32[]{:S(2)}) %collective-permute-start.18) | collective-permute-done | bytes 32800 | tf_op jit(solution)/shard_map/ppermute | solution.py:218
  79.8 1.7 %collective-permute-done.17 = f32[64,128]{1,0:T(8,128)S(1)} collective-permute-done((f32[64,128]{1,0:T(8,128)S(1)}, f32[64,128]{1,0:T(8,128)S(1)}, u32[]{:S(2)}, u32[]{:S(2)}) %collective-permute-start.17) | collective-permute-done | bytes 32800 | tf_op jit(solution)/shard_map/ppermute | solution.py:218
  81.5 1.3 %collective-permute-start.20 = (f32[64,128]{1,0:T(8,128)S(1)}, f32[64,128]{1,0:T(8,128)S(1)}, u32[]{:S(2)}, u32[]{:S(2)}) collective-permute-start(f32[64,128]{1,0:T(8,128)S(1)} %add_add_fusion), channel_id=1, source_target_pairs={{0,8},{1,9},{2,10},{3,11},{4,12},{5,13},{6,14},{7,15},{8,0},{9,1},... | collective-permute-start | bytes 98312 | tf_op jit(solution)/shard_map/ppermute | solution.py:218
  82.8 3.7 %collective-permute-done.20 = f32[64,128]{1,0:T(8,128)S(1)} collective-permute-done((f32[64,128]{1,0:T(8,128)S(1)}, f32[64,128]{1,0:T(8,128)S(1)}, u32[]{:S(2)}, u32[]{:S(2)}) %collective-permute-start.20) | collective-permute-done | bytes 32800 | tf_op jit(solution)/shard_map/ppermute | solution.py:218
  86.5 0.7 fusion
  (18 shorter events, 0.1 us)
Async XLA Ops:
  1.3 1.0 %copy-start.2 = (f32[64,2048]{1,0:T(8,128)S(1)}, f32[64,2048]{1,0:T(8,128)}, u32[]{:S(2)}) copy-start(f32[64,2048]{1,0:T(8,128)} %vectors_ref.1) | copy-start | bytes 1572868
  2.4 8.3 %collective-permute-start = (f32[64,2048]{1,0:T(8,128)S(1)}, f32[64,2048]{1,0:T(8,128)S(1)}, u32[]{:S(2)}, u32[]{:S(2)}) collective-permute-start(f32[64,2048]{1,0:T(8,128)S(1)} %get-tuple-element.18.field_ref.start_ref), channel_id=1, source_target_pairs={{0,1},{1,0},{2,3},{3,2},{4,5},{5,4},{6,7},{7,6},{8,9},{9,8},{10,11... | collective-permute-start | bytes 1572872 | tf_op jit(solution)/shard_map/ppermute | solution.py:218
  2.9 10.6 %collective-permute-start.3 = (f32[32,2048]{1,0:T(8,128)S(1)}, f32[32,2048]{1,0:T(8,128)S(1)}, u32[]{:S(2)}, u32[]{:S(2)}) collective-permute-start(f32[32,2048]{1,0:T(8,128)S(1)} %get-tuple-element.20), channel_id=1, source_target_pairs={{0,2},{1,3},{6,4},{7,5},{8,10},{9,11},{14,12},{15,13},{16,18},{17,... | collective-permute-start | bytes 786440 | tf_op jit(solution)/shard_map/ppermute | solution.py:265
  7.4 23.3 %collective-permute-start.1 = (f32[64,2048]{1,0:T(8,128)S(1)}, f32[64,2048]{1,0:T(8,128)S(1)}, u32[]{:S(2)}, u32[]{:S(2)}) collective-permute-start(f32[64,2048]{1,0:T(8,128)S(1)} %get-tuple-element.18.field_ref.start_ref), channel_id=1, source_target_pairs={{0,12},{1,13},{2,14},{3,15},{4,4},{5,5},{6,6},{7,7},{8,8},{9,9},{1... | collective-permute-start | bytes 1572872 | tf_op jit(solution)/shard_map/ppermute | solution.py:201
  10.8 19.9 %collective-permute-start.5 = (f32[64,2048]{1,0:T(8,128)S(1)}, f32[64,2048]{1,0:T(8,128)S(1)}, u32[]{:S(2)}, u32[]{:S(2)}) collective-permute-start(f32[64,2048]{1,0:T(8,128)S(1)} %collective-permute-done.flipped_ref), channel_id=1, source_target_pairs={{0,1},{1,3},{2,0},{3,2},{4,5},{5,7},{6,4},{7,6},{8,9},{9,11},{10,8... | collective-permute-start | bytes 1572872 | tf_op jit(solution)/shard_map/ppermute | solution.py:215
  11.0 19.7 %collective-permute-start.2 = (f32[32,2048]{1,0:T(8,128)S(1)}, f32[32,2048]{1,0:T(8,128)S(1)}, u32[]{:S(2)}, u32[]{:S(2)}) collective-permute-start(f32[32,2048]{1,0:T(8,128)S(1)} %get-tuple-element.19), channel_id=1, source_target_pairs={{0,6},{1,7},{2,2},{3,3},{4,4},{5,5},{6,0},{7,1},{8,14},{9,15},{10,... | collective-permute-start | bytes 786440 | tf_op jit(solution)/shard_map/ppermute | solution.py:201
  13.6 17.1 %collective-permute-start.4 = (f32[32,2048]{1,0:T(8,128)S(1)}, f32[32,2048]{1,0:T(8,128)S(1)}, u32[]{:S(2)}, u32[]{:S(2)}) collective-permute-start(f32[32,2048]{1,0:T(8,128)S(1)} %collective-permute-done.3), channel_id=1, source_target_pairs={{2,6},{3,7},{4,0},{5,1},{10,14},{11,15},{12,8},{13,9},{18,22},{19,... | collective-permute-start | bytes 786440 | tf_op jit(solution)/shard_map/ppermute | solution.py:265
  14.9 2.2 %copy-start = (f32[64,128,128]{2,1,0:T(8,128)S(1)}, f32[64,128,128]{2,1,0:T(8,128)}, u32[]{:S(2)}) copy-start(f32[64,128,128]{2,1,0:T(8,128)} %param.7) | copy-start | bytes 12582916
  17.1 0.7 copy-start.3
  17.8 0.7 copy-start.4
  18.5 0.7 copy-start.5
  19.1 28.3 %copy-start.1 = (f32[64,128,128]{2,1,0:T(8,128)S(1)}, f32[64,128,128]{2,1,0:T(8,128)}, u32[]{:S(2)}) copy-start(f32[64,128,128]{2,1,0:T(8,128)} %param.7) | copy-start | bytes 12582916
  31.4 8.1 %collective-permute-start.6 = (f32[64,2048]{1,0:T(8,128)S(1)}, f32[64,2048]{1,0:T(8,128)S(1)}, u32[]{:S(2)}, u32[]{:S(2)}) collective-permute-start(f32[64,2048]{1,0:T(8,128)S(1)} %get-tuple-element.21.field_ref), channel_id=1, source_target_pairs={{0,1},{1,0},{2,3},{3,2},{4,5},{5,4},{6,7},{7,6},{8,9},{9,8},{10,11... | collective-permute-start | bytes 1572872 | tf_op jit(solution)/shard_map/ppermute | solution.py:218
  31.6 23.6 %collective-permute-start.7 = (f32[64,2048]{1,0:T(8,128)S(1)}, f32[64,2048]{1,0:T(8,128)S(1)}, u32[]{:S(2)}, u32[]{:S(2)}) collective-permute-start(f32[64,2048]{1,0:T(8,128)S(1)} %get-tuple-element.21.field_ref), channel_id=1, source_target_pairs={{0,12},{1,13},{2,14},{3,15},{4,4},{5,5},{6,6},{7,7},{8,8},{9,9},{1... | collective-permute-start | bytes 1572872 | tf_op jit(solution)/shard_map/ppermute | solution.py:201
  33.5 12.6 %collective-permute-start.9 = (f32[32,2048]{1,0:T(8,128)S(1)}, f32[32,2048]{1,0:T(8,128)S(1)}, u32[]{:S(2)}, u32[]{:S(2)}) collective-permute-start(f32[32,2048]{1,0:T(8,128)S(1)} %get-tuple-element.23), channel_id=1, source_target_pairs={{0,2},{1,3},{6,4},{7,5},{8,10},{9,11},{14,12},{15,13},{16,18},{17,... | collective-permute-start | bytes 786440 | tf_op jit(solution)/shard_map/ppermute | solution.py:265
  39.5 15.8 %collective-permute-start.11 = (f32[64,2048]{1,0:T(8,128)S(1)}, f32[64,2048]{1,0:T(8,128)S(1)}, u32[]{:S(2)}, u32[]{:S(2)}) collective-permute-start(f32[64,2048]{1,0:T(8,128)S(1)} %collective-permute-done.6.flipped_ref), channel_id=1, source_target_pairs={{0,1},{1,3},{2,0},{3,2},{4,5},{5,7},{6,4},{7,6},{8,9},{9,11},{10,8... | collective-permute-start | bytes 1572872 | tf_op jit(solution)/shard_map/ppermute | solution.py:215
  39.5 15.6 %collective-permute-start.8 = (f32[32,2048]{1,0:T(8,128)S(1)}, f32[32,2048]{1,0:T(8,128)S(1)}, u32[]{:S(2)}, u32[]{:S(2)}) collective-permute-start(f32[32,2048]{1,0:T(8,128)S(1)} %get-tuple-element.22), channel_id=1, source_target_pairs={{0,6},{1,7},{2,2},{3,3},{4,4},{5,5},{6,0},{7,1},{8,14},{9,15},{10,... | collective-permute-start | bytes 786440 | tf_op jit(solution)/shard_map/ppermute | solution.py:201
  46.1 9.1 %collective-permute-start.10 = (f32[32,2048]{1,0:T(8,128)S(1)}, f32[32,2048]{1,0:T(8,128)S(1)}, u32[]{:S(2)}, u32[]{:S(2)}) collective-permute-start(f32[32,2048]{1,0:T(8,128)S(1)} %collective-permute-done.9), channel_id=1, source_target_pairs={{2,6},{3,7},{4,0},{5,1},{10,14},{11,15},{12,8},{13,9},{18,22},{19,... | collective-permute-start | bytes 786440 | tf_op jit(solution)/shard_map/ppermute | solution.py:265
  56.0 2.0 %collective-permute-start.12 = (f32[64,2048]{1,0:T(8,128)S(1)}, f32[64,2048]{1,0:T(8,128)S(1)}, u32[]{:S(2)}, u32[]{:S(2)}) collective-permute-start(f32[64,2048]{1,0:T(8,128)S(1)} %get-tuple-element.24.field_ref), channel_id=1, source_target_pairs={{0,1},{1,0},{2,3},{3,2},{4,5},{5,4},{6,7},{7,6},{8,9},{9,8},{10,11... | collective-permute-start | bytes 1572872 | tf_op jit(solution)/shard_map/ppermute | solution.py:218
  56.1 15.2 %collective-permute-start.13 = (f32[64,1536]{1,0:T(8,128)S(1)}, f32[64,1536]{1,0:T(8,128)S(1)}, u32[]{:S(2)}, u32[]{:S(2)}) collective-permute-start(f32[64,1536]{1,0:T(8,128)S(1)} %get-tuple-element.30), channel_id=1, source_target_pairs={{0,3},{2,14},{3,15},{7,4},{8,11},{12,0},{13,1},{15,12},{16,19},{18... | collective-permute-start | bytes 1179656 | tf_op jit(solution)/shard_map/ppermute | solution.py:211
  58.0 13.3 %collective-permute-start.15 = (f32[64,1024]{1,0:T(8,128)S(1)}, f32[64,1024]{1,0:T(8,128)S(1)}, u32[]{:S(2)}, u32[]{:S(2)}) collective-permute-start(f32[64,1024]{1,0:T(8,128)S(1)} %get-tuple-element.32), channel_id=1, source_target_pairs={{0,6},{1,7},{2,2},{3,3},{4,4},{5,5},{6,0},{7,1},{8,14},{9,15},{10,... | collective-permute-start | bytes 786440 | tf_op jit(solution)/shard_map/ppermute | solution.py:201
  61.5 9.8 %collective-permute-start.14 = (f32[64,512]{1,0:T(8,128)S(1)}, f32[64,512]{1,0:T(8,128)S(1)}, u32[]{:S(2)}, u32[]{:S(2)}) collective-permute-start(f32[64,512]{1,0:T(8,128)S(1)} %get-tuple-element.31), channel_id=1, source_target_pairs={{0,12},{1,13},{3,0},{4,7},{11,8},{12,15},{14,2},{15,3},{16,28},{17... | collective-permute-start | bytes 393224 | tf_op jit(solution)/shard_map/ppermute | solution.py:211
  72.4 1.3 %collective-permute-start.16 = (f32[64,128]{1,0:T(8,128)S(1)}, f32[64,128]{1,0:T(8,128)S(1)}, u32[]{:S(2)}, u32[]{:S(2)}) collective-permute-start(f32[64,128]{1,0:T(8,128)S(1)} %crossed.1), channel_id=1, source_target_pairs={{0,1},{1,0},{2,3},{3,2},{4,5},{5,4},{6,7},{7,6},{8,9},{9,8},{10,11... | collective-permute-start | bytes 98312 | tf_op jit(solution)/shard_map/ppermute | solution.py:218
  73.7 5.0 %collective-permute-start.19 = (f32[64,128]{1,0:T(8,128)S(1)}, f32[64,128]{1,0:T(8,128)S(1)}, u32[]{:S(2)}, u32[]{:S(2)}) collective-permute-start(f32[64,128]{1,0:T(8,128)S(1)} %add.23), channel_id=1, source_target_pairs={{0,6},{1,7},{2,4},{3,5},{4,2},{5,3},{6,0},{7,1},{8,14},{9,15},{10,... | collective-permute-start | bytes 98312 | tf_op jit(solution)/shard_map/ppermute | solution.py:218
  74.1 5.8 %collective-permute-start.18 = (f32[64,128]{1,0:T(8,128)S(1)}, f32[64,128]{1,0:T(8,128)S(1)}, u32[]{:S(2)}, u32[]{:S(2)}) collective-permute-start(f32[64,128]{1,0:T(8,128)S(1)} %add.23), channel_id=1, source_target_pairs={{0,4},{1,5},{2,6},{3,7},{4,0},{5,1},{6,2},{7,3},{8,12},{9,13},{10,... | collective-permute-start | bytes 98312 | tf_op jit(solution)/shard_map/ppermute | solution.py:218
  77.6 3.9 %collective-permute-start.17 = (f32[64,128]{1,0:T(8,128)S(1)}, f32[64,128]{1,0:T(8,128)S(1)}, u32[]{:S(2)}, u32[]{:S(2)}) collective-permute-start(f32[64,128]{1,0:T(8,128)S(1)} %add.23), channel_id=1, source_target_pairs={{0,2},{1,3},{2,0},{3,1},{4,6},{5,7},{6,4},{7,5},{8,10},{9,11},{10,... | collective-permute-start | bytes 98312 | tf_op jit(solution)/shard_map/ppermute | solution.py:218
  81.5 5.0 %collective-permute-start.20 = (f32[64,128]{1,0:T(8,128)S(1)}, f32[64,128]{1,0:T(8,128)S(1)}, u32[]{:S(2)}, u32[]{:S(2)}) collective-permute-start(f32[64,128]{1,0:T(8,128)S(1)} %add_add_fusion), channel_id=1, source_target_pairs={{0,8},{1,9},{2,10},{3,11},{4,12},{5,13},{6,14},{7,15},{8,0},{9,1},... | collective-permute-start | bytes 98312 | tf_op jit(solution)/shard_map/ppermute | solution.py:218
where the time goes:
time: 87.7 us; the launch traced here: 87.2 us
  starting transfers between devices  36.6 us (42%)
  waiting for transfers between devices  27.4 us (31%)
  Pallas kernels  15.6 us (18%)
  local copies, waits for them, and re-layouts  5.93 us (7%)
  between operations  1.5 us (2%)
    ppermute x4, starting transfers between devices, apply(): aside = lax.ppermute(lax.ppermute(second_half, AXES, legs), AXES, round_way)  13 us
    ppermute x5, starting transfers between devices, hop(): return lax.ppermute(value, AXES, pairs)  12.6 us
    ppermute x5, waiting for transfers between devices, hop(): return lax.ppermute(value, AXES, pairs)  12 us
    ppermute x8, waiting for transfers between devices, exchange(): lax.ppermute(value, AXES, [(source, source ^ mask) for source in range(de...  8.82 us
    pallas_call x2, Pallas kernels, own_part(): pl.pallas_call(own_kernel, out_shape=full, in_specs=[SMEM] * 3 + [inside]...  7.22 us
    ppermute x8, starting transfers between devices, exchange(): lax.ppermute(value, AXES, [(source, source ^ mask) for source in range(de...  5.99 us
    pallas_call x1, Pallas kernels, own_gram(): pl.pallas_call(own_gram_kernel, out_shape=[gram_shape, full], in_specs=[S...  5.71 us
    ppermute x4, waiting for transfers between devices, apply(): aside = lax.ppermute(lax.ppermute(second_half, AXES, legs), AXES, round_way)  5.45 us
  transfers between devices with their start and end apart: 21, of which 11 were waited for; matrix products, arithmetic and copies ran while one was open for 0% of the time, Pallas kernels for 15%

commit v1 on v0

--- a/solution.py
+++ b/solution.py
@@ -126,12 +126,16 @@
     copy.wait()
 
 
-def hop_sum(bonds, config, refs):
+def far_kernel(bonds, place_ref, own_ref, *refs):
+    total = own_ref[...]
+    for bond, ref in zip(reversed(range(2, bonds)), refs):
+        total += coupling(place_ref[0], bond) * ref[...]
+    refs[-1][...] = total
+
+
+def hop_sum(config, refs):
     total = coupling(config, 0) * refs[-1][...]
-    total += coupling(config, 1) * jnp.concatenate([refs[-3][...], refs[-2][...]], axis=0)
-    for bond, ref in zip(reversed(range(2, bonds)), refs):
-        total += coupling(config, bond) * ref[...]
-    return total
+    return total + coupling(config, 1) * jnp.concatenate([refs[0][...], refs[1][...]], axis=0)
 
 
 def store_halves(value, out_ref, first_ref, second_ref):
@@ -146,15 +150,15 @@
     store_halves(start, out_ref, first_ref, second_ref)
 
 
-def combine_kernel(bonds, place_ref, live_ref, own_ref, *refs):
+def combine_kernel(place_ref, live_ref, own_ref, *refs):
     hops, outs = refs[:-3], refs[-3:]
-    total = own_ref[...] + hop_sum(bonds, place_ref[0], hops)
+    total = own_ref[...] + hop_sum(place_ref[0], hops)
     store_halves(alive_of(live_ref, 0, total.shape[1]) * total * (1.0 / HALF_WIDTH), *outs)
 
 
-def filter_kernel(bonds, place_ref, live_ref, own_ref, start_ref, *refs):
+def filter_kernel(place_ref, live_ref, own_ref, start_ref, *refs):
     hops, (kept_ref, sent_ref, lead_ref, rest_ref) = refs[:-4], refs[-4:]
-    total = own_ref[...] + hop_sum(bonds, place_ref[0], hops)
+    total = own_ref[...] + hop_sum(place_ref[0], hops)
     image = alive_of(live_ref, 0, total.shape[1]) * total * (1.0 / HALF_WIDTH)
     second = 2.0 * image - start_ref[...]
     kept_ref[...] = second
@@ -265,7 +269,17 @@
         aside = lax.ppermute(lax.ppermute(second_half, AXES, legs), AXES, round_way)
         direct = hop(first_half, 1)
         closest = near(flipped)
-        return own_part(field, flipped), far + [direct, aside, closest]
+        total = pl.pallas_call(
+            functools.partial(far_kernel, bonds),
+            out_shape=full,
+            in_specs=[SMEM] + [inside] * (bonds - 1),
+            out_specs=inside,
+            input_output_aliases={1: 0},
+            compiler_params=params,
+            cost_estimate=pl.CostEstimate(flops=vec_count * row_count, bytes_accessed=12 * vec_count * row_count, transcendentals=0),
+            name="far",
+        )(place, own_part(field, flipped), *far)
+        return total, [direct, aside, closest]
 
     start, *halves_of = pl.pallas_call(
         start_kernel,
@@ -277,9 +291,9 @@
     )(live_rows, vectors)
     own, hops = apply(start, *halves_of)
     first, *halves_of = pl.pallas_call(
-        functools.partial(combine_kernel, bonds),
+        combine_kernel,
         out_shape=three,
-        in_specs=[SMEM] * 2 + [inside] * (bonds + 2),
+        in_specs=[SMEM] * 2 + [inside] * 4,
         out_specs=[inside] * 3,
         compiler_params=params,
         name="combine",
@@ -287,9 +301,9 @@
     own, hops = apply(first, *halves_of)
     cut = row_count * 3 // 4
     kept, sent, lead, rest = pl.pallas_call(
-        functools.partial(filter_kernel, bonds),
+        filter_kernel,
         out_shape=[full] + [rows_by(vec_count, width) for width in (row_count // 2, cut, row_count - cut)],
-        in_specs=[SMEM] * 2 + [inside] * (bonds + 3),
+        in_specs=[SMEM] * 2 + [inside] * 5,
         out_specs=[inside] * 4,
         compiler_params=params,
         name="filter",

time: 87.7 us -> 86.9 us (level)
  waiting for transfers between devices: 27.4 us -> 25.8 us
  Pallas kernels: 15.6 us -> 16.8 us
    ppermute x5, waiting for transfers between devices: 12 us -> 6.2 us  [hop(): return lax.ppermute(value, AXES, pairs)]
    ppermute x4, waiting for transfers between devices: 5.45 us -> 9.33 us  [apply(): aside = lax.ppermute(lax.ppermute(second_half, AXES, legs), AXES, round_way)]
    ppermute x4, starting transfers between devices: 13 us -> 10.7 us  [apply(): aside = lax.ppermute(lax.ppermute(second_half, AXES, legs), AXES, round_way)]
    ppermute x5, starting transfers between devices: 12.6 us -> 14.7 us  [hop(): return lax.ppermute(value, AXES, pairs)]
    ppermute x8, starting transfers between devices: 5.99 us -> 4.3 us  [exchange(): lax.ppermute(value, AXES, [(source, source ^ mask) for source in range(de...]
    ppermute x2, starting transfers between devices: 4.82 us -> 6.39 us  [one_way(): return lax.ppermute(value, AXES, pairs)]
    pallas_call x2 -> x4, Pallas kernels: 1.47 us -> 2.68 us  [the longest x2 1.27 us: apply(): pl.pallas_call(functools.partial(far_kernel, bonds), out_shape=full, in_s...]
  transfers between devices with their start and end apart: 21 -> 21, of which waited for: 11 -> 9; matrix products, arithmetic and copies ran while one was open for 0% -> 0% of each run, Pallas kernels for 15% -> 16%
where the time goes in v1:
time: 86.9 us; the launch traced here: 86.3 us
  starting transfers between devices  36.1 us (42%)
  waiting for transfers between devices  25.8 us (30%)
  Pallas kernels  16.8 us (19%)
  local copies, waits for them, and re-layouts  5.93 us (7%)
  between operations  1.57 us (2%)
    ppermute x5, starting transfers between devices, hop(): return lax.ppermute(value, AXES, pairs)  14.7 us
    ppermute x4, starting transfers between devices, apply(): aside = lax.ppermute(lax.ppermute(second_half, AXES, legs), AXES, round_way)  10.7 us
    ppermute x4, waiting for transfers between devices, apply(): aside = lax.ppermute(lax.ppermute(second_half, AXES, legs), AXES, round_way)  9.33 us
    ppermute x8, waiting for transfers between devices, exchange(): lax.ppermute(value, AXES, [(source, source ^ mask) for source in range(de...  9.13 us
    pallas_call x2, Pallas kernels, own_part(): pl.pallas_call(own_kernel, out_shape=full, in_specs=[SMEM] * 3 + [inside]...  7.21 us
    ppermute x2, starting transfers between devices, one_way(): return lax.ppermute(value, AXES, pairs)  6.39 us
    ppermute x5, waiting for transfers between devices, hop(): return lax.ppermute(value, AXES, pairs)  6.2 us
    pallas_call x1, Pallas kernels, own_gram(): pl.pallas_call(own_gram_kernel, out_shape=[gram_shape, full], in_specs=[S...  5.71 us
  transfers between devices with their start and end apart: 21, of which 9 were waited for; matrix products, arithmetic and copies ran while one was open for 0% of the time, Pallas kernels for 16%

profile of v1, /device:TPU:0, one launch (start us, length us, event | category | flops | bytes accessed | tf_op | source)
XLA Modules:
  0.0 86.3 jit_solution(1943821662177303265)
XLA Ops:
  1.3 1.0 %copy-done.2 = f32[64,2048]{1,0:T(8,128)S(1)} copy-done((f32[64,2048]{1,0:T(8,128)S(1)}, f32[64,2048]{1,0:T(8,128)}, u32[]{:S(2)}) %copy-start.2) | copy-done | bytes 524312
  2.3 0.1 start.1
  2.4 0.5 collective-permute-start
  2.9 6.5 %collective-permute-start.1 = (f32[64,2048]{1,0:T(8,128)S(1)}, f32[64,2048]{1,0:T(8,128)S(1)}, u32[]{:S(2)}, u32[]{:S(2)}) collective-permute-start(f32[64,2048]{1,0:T(8,128)S(1)} %get-tuple-element.18.field_ref.start_ref), channel_id=1, source_target_pairs={{0,12},{1,13},{2,14},{3,15},{4,4},{5,5},{6,6},{7,7},{8,8},{9,9},{1... | collective-permute-start | bytes 1572872 | tf_op jit(solution)/shard_map/ppermute | solution.py:205
  9.4 3.4 %collective-permute-start.3 = (f32[32,2048]{1,0:T(8,128)S(1)}, f32[32,2048]{1,0:T(8,128)S(1)}, u32[]{:S(2)}, u32[]{:S(2)}) collective-permute-start(f32[32,2048]{1,0:T(8,128)S(1)} %get-tuple-element.20), channel_id=1, source_target_pairs={{0,2},{1,3},{6,4},{7,5},{8,10},{9,11},{14,12},{15,13},{16,18},{17,... | collective-permute-start | bytes 786440 | tf_op jit(solution)/shard_map/ppermute | solution.py:269
  12.9 0.0 collective-permute-done.flipped_ref
  12.9 0.0 collective-permute-start.5
  12.9 1.9 %collective-permute-start.2 = (f32[32,2048]{1,0:T(8,128)S(1)}, f32[32,2048]{1,0:T(8,128)S(1)}, u32[]{:S(2)}, u32[]{:S(2)}) collective-permute-start(f32[32,2048]{1,0:T(8,128)S(1)} %get-tuple-element.19), channel_id=1, source_target_pairs={{0,6},{1,7},{2,2},{3,3},{4,4},{5,5},{6,0},{7,1},{8,14},{9,15},{10,... | collective-permute-start | bytes 786440 | tf_op jit(solution)/shard_map/ppermute | solution.py:205
  14.9 4.7 %collective-permute-done.3 = f32[32,2048]{1,0:T(8,128)S(1)} collective-permute-done((f32[32,2048]{1,0:T(8,128)S(1)}, f32[32,2048]{1,0:T(8,128)S(1)}, u32[]{:S(2)}, u32[]{:S(2)}) %collective-permute-start.3) | collective-permute-done | bytes 262176 | tf_op jit(solution)/shard_map/ppermute | solution.py:269
  19.5 1.3 %collective-permute-start.4 = (f32[32,2048]{1,0:T(8,128)S(1)}, f32[32,2048]{1,0:T(8,128)S(1)}, u32[]{:S(2)}, u32[]{:S(2)}) collective-permute-start(f32[32,2048]{1,0:T(8,128)S(1)} %collective-permute-done.3), channel_id=1, source_target_pairs={{2,6},{3,7},{4,0},{5,1},{10,14},{11,15},{12,8},{13,9},{18,22},{19,... | collective-permute-start | bytes 786440 | tf_op jit(solution)/shard_map/ppermute | solution.py:269
  20.8 0.1 pad_add_fusion.place_ref
  20.9 2.2 %copy-done = f32[64,128,128]{2,1,0:T(8,128)S(1)} copy-done((f32[64,128,128]{2,1,0:T(8,128)S(1)}, f32[64,128,128]{2,1,0:T(8,128)}, u32[]{:S(2)}) %copy-start) | copy-done | bytes 4194328
  23.1 0.7 copy-done.3
  23.8 0.7 copy-done.4
  24.4 0.7 copy-done.5
  25.1 3.6 %own.2.own_ref = f32[64,2048]{1,0:T(8,128)S(1)} custom-call(s32[2]{0:T(128)S(1)} %pad_add_fusion.place_ref, s32[64]{0:T(128)S(1)} %copy-done.4, s32[4]{0:T(128)S(1)} %copy-done.5, f32[64,2048]{1,0:T(8,128)S(1)} %get-tuple-element.18.field_ref.start_ref, f32[64,2048]{1,0:T(8,128)S(1)} %collective-permute-done.flipped_ref, f32[16,4,128,128]{3,2,1,0:T(8,128)S(1)} %bitcast.4, ...), custom_call_target="tpu_custom_call" | custom-call | flops 536870912 | bytes 5767168 | tf_op jit(solution)/shard_map/own/pallas_call | solution.py:239
  28.7 0.0 collective-permute-done.1.refs_0_
  28.7 0.6 far.2.own_ref
  29.3 0.0 collective-permute-done.2.refs_0_
  29.4 0.7 combine.1
  30.0 0.1 collective-permute-start.6
  30.1 2.5 %collective-permute-start.7 = (f32[64,2048]{1,0:T(8,128)S(1)}, f32[64,2048]{1,0:T(8,128)S(1)}, u32[]{:S(2)}, u32[]{:S(2)}) collective-permute-start(f32[64,2048]{1,0:T(8,128)S(1)} %get-tuple-element.21.field_ref), channel_id=1, source_target_pairs={{0,12},{1,13},{2,14},{3,15},{4,4},{5,5},{6,6},{7,7},{8,8},{9,9},{1... | collective-permute-start | bytes 1572872 | tf_op jit(solution)/shard_map/ppermute | solution.py:205
  32.6 4.7 %collective-permute-start.9 = (f32[32,2048]{1,0:T(8,128)S(1)}, f32[32,2048]{1,0:T(8,128)S(1)}, u32[]{:S(2)}, u32[]{:S(2)}) collective-permute-start(f32[32,2048]{1,0:T(8,128)S(1)} %get-tuple-element.23), channel_id=1, source_target_pairs={{0,2},{1,3},{6,4},{7,5},{8,10},{9,11},{14,12},{15,13},{16,18},{17,... | collective-permute-start | bytes 786440 | tf_op jit(solution)/shard_map/ppermute | solution.py:269
  37.3 0.0 collective-permute-start.11
  37.3 1.9 %collective-permute-start.8 = (f32[32,2048]{1,0:T(8,128)S(1)}, f32[32,2048]{1,0:T(8,128)S(1)}, u32[]{:S(2)}, u32[]{:S(2)}) collective-permute-start(f32[32,2048]{1,0:T(8,128)S(1)} %get-tuple-element.22), channel_id=1, source_target_pairs={{0,6},{1,7},{2,2},{3,3},{4,4},{5,5},{6,0},{7,1},{8,14},{9,15},{10,... | collective-permute-start | bytes 786440 | tf_op jit(solution)/shard_map/ppermute | solution.py:205
  39.2 4.7 %collective-permute-done.9 = f32[32,2048]{1,0:T(8,128)S(1)} collective-permute-done((f32[32,2048]{1,0:T(8,128)S(1)}, f32[32,2048]{1,0:T(8,128)S(1)}, u32[]{:S(2)}, u32[]{:S(2)}) %collective-permute-start.9) | collective-permute-done | bytes 262176 | tf_op jit(solution)/shard_map/ppermute | solution.py:269
  43.9 1.3 %collective-permute-start.10 = (f32[32,2048]{1,0:T(8,128)S(1)}, f32[32,2048]{1,0:T(8,128)S(1)}, u32[]{:S(2)}, u32[]{:S(2)}) collective-permute-start(f32[32,2048]{1,0:T(8,128)S(1)} %collective-permute-done.9), channel_id=1, source_target_pairs={{2,6},{3,7},{4,0},{5,1},{10,14},{11,15},{12,8},{13,9},{18,22},{19,... | collective-permute-start | bytes 786440 | tf_op jit(solution)/shard_map/ppermute | solution.py:269
  45.2 3.6 %own.3.own_ref = f32[64,2048]{1,0:T(8,128)S(1)} custom-call(s32[2]{0:T(128)S(1)} %pad_add_fusion.place_ref, s32[64]{0:T(128)S(1)} %copy-done.4, s32[4]{0:T(128)S(1)} %copy-done.5, f32[64,2048]{1,0:T(8,128)S(1)} %get-tuple-element.21.field_ref, f32[64,2048]{1,0:T(8,128)S(1)} %collective-permute-done.6.flipped_ref, f32[16,4,128,128]{3,2,1,0:T(8,128)S(1)} %bitcast.5, ...), custom_call_target="tpu_custom_call" | custom-call | flops 536870912 | bytes 5767168 | tf_op jit(solution)/shard_map/own/pallas_call | solution.py:239
  48.8 0.6 far.3.own_ref
  49.5 6.2 %collective-permute-done.8.refs_0_ = f32[32,2048]{1,0:T(8,128)S(1)} collective-permute-done((f32[32,2048]{1,0:T(8,128)S(1)}, f32[32,2048]{1,0:T(8,128)S(1)}, u32[]{:S(2)}, u32[]{:S(2)}) %collective-permute-start.8) | collective-permute-done | bytes 262176 | tf_op jit(solution)/shard_map/ppermute | solution.py:205
  55.7 0.7 filter.1
  56.4 0.1 collective-permute-start.12
  56.5 1.9 %collective-permute-start.13 = (f32[64,1536]{1,0:T(8,128)S(1)}, f32[64,1536]{1,0:T(8,128)S(1)}, u32[]{:S(2)}, u32[]{:S(2)}) collective-permute-start(f32[64,1536]{1,0:T(8,128)S(1)} %get-tuple-element.30), channel_id=1, source_target_pairs={{0,3},{2,14},{3,15},{7,4},{8,11},{12,0},{13,1},{15,12},{16,19},{18... | collective-permute-start | bytes 1179656 | tf_op jit(solution)/shard_map/ppermute | solution.py:215
  58.4 1.9 %collective-permute-start.15 = (f32[64,1024]{1,0:T(8,128)S(1)}, f32[64,1024]{1,0:T(8,128)S(1)}, u32[]{:S(2)}, u32[]{:S(2)}) collective-permute-start(f32[64,1024]{1,0:T(8,128)S(1)} %get-tuple-element.32), channel_id=1, source_target_pairs={{0,6},{1,7},{2,2},{3,3},{4,4},{5,5},{6,0},{7,1},{8,14},{9,15},{10,... | collective-permute-start | bytes 786440 | tf_op jit(solution)/shard_map/ppermute | solution.py:205
  60.4 4.5 %collective-permute-start.14 = (f32[64,512]{1,0:T(8,128)S(1)}, f32[64,512]{1,0:T(8,128)S(1)}, u32[]{:S(2)}, u32[]{:S(2)}) collective-permute-start(f32[64,512]{1,0:T(8,128)S(1)} %get-tuple-element.31), channel_id=1, source_target_pairs={{0,12},{1,13},{3,0},{4,7},{11,8},{12,15},{14,2},{15,3},{16,28},{17... | collective-permute-start | bytes 393224 | tf_op jit(solution)/shard_map/ppermute | solution.py:215
  64.9 5.7 %own_gram.1 = (f32[64,128]{1,0:T(8,128)S(1)}, f32[64,2048]{1,0:T(8,128)}) custom-call(s32[2]{0:T(128)S(1)} %pad_add_fusion.place_ref, s32[64]{0:T(128)S(1)} %copy-done.4, s32[4]{0:T(128)S(1)} %copy-done.5, s32[1]{0:T(128)S(6)} %copy.13.live_ref, f32[64,2048]{1,0:T(8,128)S(1)} %get-tuple-element.24.field_ref, ...), custom_call_target="tpu_custom_call" | custom-call | flops 536870912 | bytes 5767168 | tf_op jit(solution)/shard_map/own_gram/pallas_call | solution.py:251
  70.6 1.1 %collective-permute-done.13.refs_0_ = f32[64,1536]{1,0:T(8,128)S(1)} collective-permute-done((f32[64,1536]{1,0:T(8,128)S(1)}, f32[64,1536]{1,0:T(8,128)S(1)}, u32[]{:S(2)}, u32[]{:S(2)}) %collective-permute-start.13) | collective-permute-done | bytes 393248 | tf_op jit(solution)/shard_map/ppermute | solution.py:215
  71.7 1.1 %crossed.1 = f32[64,128]{1,0:T(8,128)S(1)} custom-call(s32[2]{0:T(128)S(1)} %pad_add_fusion.place_ref, f32[64,128]{1,0:T(8,128)S(1)} %get-tuple-element.29.own_ref, f32[64,2048]{1,0:T(8,128)S(1)} %get-tuple-element.24.field_ref, f32[64,1536]{1,0:T(8,128)S(1)} %collective-permute-done.13.refs_0_, f32[64,512]{1,0:T(8,128)S(1)} %collective-permute-done.14.refs_1_, ...), custom_call_target="tpu_custom_call" | custom-call | tf_op jit(solution)/shard_map/crossed/pallas_call | solution.py:317
  72.9 0.1 collective-permute-start.16
  72.9 1.2 %collective-permute-done.16 = f32[64,128]{1,0:T(8,128)S(1)} collective-permute-done((f32[64,128]{1,0:T(8,128)S(1)}, f32[64,128]{1,0:T(8,128)S(1)}, u32[]{:S(2)}, u32[]{:S(2)}) %collective-permute-start.16) | collective-permute-done | bytes 32800 | tf_op jit(solution)/shard_map/ppermute | solution.py:222
  74.1 2.7 %collective-permute-start.18 = (f32[64,128]{1,0:T(8,128)S(1)}, f32[64,128]{1,0:T(8,128)S(1)}, u32[]{:S(2)}, u32[]{:S(2)}) collective-permute-start(f32[64,128]{1,0:T(8,128)S(1)} %add.23), channel_id=1, source_target_pairs={{0,4},{1,5},{2,6},{3,7},{4,0},{5,1},{6,2},{7,3},{8,12},{9,13},{10,... | collective-permute-start | bytes 98312 | tf_op jit(solution)/shard_map/ppermute | solution.py:222
  76.8 0.8 collective-permute-start.17
  77.6 1.3 %collective-permute-done.19 = f32[64,128]{1,0:T(8,128)S(1)} collective-permute-done((f32[64,128]{1,0:T(8,128)S(1)}, f32[64,128]{1,0:T(8,128)S(1)}, u32[]{:S(2)}, u32[]{:S(2)}) %collective-permute-start.19) | collective-permute-done | bytes 32800 | tf_op jit(solution)/shard_map/ppermute | solution.py:222
  78.9 0.1 collective-permute-done.18
  79.1 1.7 %collective-permute-done.17 = f32[64,128]{1,0:T(8,128)S(1)} collective-permute-done((f32[64,128]{1,0:T(8,128)S(1)}, f32[64,128]{1,0:T(8,128)S(1)}, u32[]{:S(2)}, u32[]{:S(2)}) %collective-permute-start.17) | collective-permute-done | bytes 32800 | tf_op jit(solution)/shard_map/ppermute | solution.py:222
  80.8 0.1 collective-permute-start.20
  80.8 4.8 %collective-permute-done.20 = f32[64,128]{1,0:T(8,128)S(1)} collective-permute-done((f32[64,128]{1,0:T(8,128)S(1)}, f32[64,128]{1,0:T(8,128)S(1)}, u32[]{:S(2)}, u32[]{:S(2)}) %collective-permute-start.20) | collective-permute-done | bytes 32800 | tf_op jit(solution)/shard_map/ppermute | solution.py:222
  85.6 0.7 fusion
  (20 shorter events, 0.1 us)
Async XLA Ops:
  1.3 1.0 %copy-start.2 = (f32[64,2048]{1,0:T(8,128)S(1)}, f32[64,2048]{1,0:T(8,128)}, u32[]{:S(2)}) copy-start(f32[64,2048]{1,0:T(8,128)} %vectors_ref.1) | copy-start | bytes 1572868
  2.4 10.5 %collective-permute-start = (f32[64,2048]{1,0:T(8,128)S(1)}, f32[64,2048]{1,0:T(8,128)S(1)}, u32[]{:S(2)}, u32[]{:S(2)}) collective-permute-start(f32[64,2048]{1,0:T(8,128)S(1)} %get-tuple-element.18.field_ref.start_ref), channel_id=1, source_target_pairs={{0,1},{1,0},{2,3},{3,2},{4,5},{5,4},{6,7},{7,6},{8,9},{9,8},{10,11... | collective-permute-start | bytes 1572872 | tf_op jit(solution)/shard_map/ppermute | solution.py:222
  2.9 25.8 %collective-permute-start.1 = (f32[64,2048]{1,0:T(8,128)S(1)}, f32[64,2048]{1,0:T(8,128)S(1)}, u32[]{:S(2)}, u32[]{:S(2)}) collective-permute-start(f32[64,2048]{1,0:T(8,128)S(1)} %get-tuple-element.18.field_ref.start_ref), channel_id=1, source_target_pairs={{0,12},{1,13},{2,14},{3,15},{4,4},{5,5},{6,6},{7,7},{8,8},{9,9},{1... | collective-permute-start | bytes 1572872 | tf_op jit(solution)/shard_map/ppermute | solution.py:205
  9.4 10.1 %collective-permute-start.3 = (f32[32,2048]{1,0:T(8,128)S(1)}, f32[32,2048]{1,0:T(8,128)S(1)}, u32[]{:S(2)}, u32[]{:S(2)}) collective-permute-start(f32[32,2048]{1,0:T(8,128)S(1)} %get-tuple-element.20), channel_id=1, source_target_pairs={{0,2},{1,3},{6,4},{7,5},{8,10},{9,11},{14,12},{15,13},{16,18},{17,... | collective-permute-start | bytes 786440 | tf_op jit(solution)/shard_map/ppermute | solution.py:269
  12.9 16.5 %collective-permute-start.5 = (f32[64,2048]{1,0:T(8,128)S(1)}, f32[64,2048]{1,0:T(8,128)S(1)}, u32[]{:S(2)}, u32[]{:S(2)}) collective-permute-start(f32[64,2048]{1,0:T(8,128)S(1)} %collective-permute-done.flipped_ref), channel_id=1, source_target_pairs={{0,1},{1,3},{2,0},{3,2},{4,5},{5,7},{6,4},{7,6},{8,9},{9,11},{10,8... | collective-permute-start | bytes 1572872 | tf_op jit(solution)/shard_map/ppermute | solution.py:219
  12.9 16.4 %collective-permute-start.2 = (f32[32,2048]{1,0:T(8,128)S(1)}, f32[32,2048]{1,0:T(8,128)S(1)}, u32[]{:S(2)}, u32[]{:S(2)}) collective-permute-start(f32[32,2048]{1,0:T(8,128)S(1)} %get-tuple-element.19), channel_id=1, source_target_pairs={{0,6},{1,7},{2,2},{3,3},{4,4},{5,5},{6,0},{7,1},{8,14},{9,15},{10,... | collective-permute-start | bytes 786440 | tf_op jit(solution)/shard_map/ppermute | solution.py:205
  19.5 9.8 %collective-permute-start.4 = (f32[32,2048]{1,0:T(8,128)S(1)}, f32[32,2048]{1,0:T(8,128)S(1)}, u32[]{:S(2)}, u32[]{:S(2)}) collective-permute-start(f32[32,2048]{1,0:T(8,128)S(1)} %collective-permute-done.3), channel_id=1, source_target_pairs={{2,6},{3,7},{4,0},{5,1},{10,14},{11,15},{12,8},{13,9},{18,22},{19,... | collective-permute-start | bytes 786440 | tf_op jit(solution)/shard_map/ppermute | solution.py:269
  20.9 2.2 %copy-start = (f32[64,128,128]{2,1,0:T(8,128)S(1)}, f32[64,128,128]{2,1,0:T(8,128)}, u32[]{:S(2)}) copy-start(f32[64,128,128]{2,1,0:T(8,128)} %param.7) | copy-start | bytes 12582916
  23.1 0.7 copy-start.3
  23.8 0.7 copy-start.4
  24.4 0.7 copy-start.5
  25.1 20.1 %copy-start.1 = (f32[64,128,128]{2,1,0:T(8,128)S(1)}, f32[64,128,128]{2,1,0:T(8,128)}, u32[]{:S(2)}) copy-start(f32[64,128,128]{2,1,0:T(8,128)} %param.7) | copy-start | bytes 12582916
  30.0 7.2 %collective-permute-start.6 = (f32[64,2048]{1,0:T(8,128)S(1)}, f32[64,2048]{1,0:T(8,128)S(1)}, u32[]{:S(2)}, u32[]{:S(2)}) collective-permute-start(f32[64,2048]{1,0:T(8,128)S(1)} %get-tuple-element.21.field_ref), channel_id=1, source_target_pairs={{0,1},{1,0},{2,3},{3,2},{4,5},{5,4},{6,7},{7,6},{8,9},{9,8},{10,11... | collective-permute-start | bytes 1572872 | tf_op jit(solution)/shard_map/ppermute | solution.py:222
  30.1 18.7 %collective-permute-start.7 = (f32[64,2048]{1,0:T(8,128)S(1)}, f32[64,2048]{1,0:T(8,128)S(1)}, u32[]{:S(2)}, u32[]{:S(2)}) collective-permute-start(f32[64,2048]{1,0:T(8,128)S(1)} %get-tuple-element.21.field_ref), channel_id=1, source_target_pairs={{0,12},{1,13},{2,14},{3,15},{4,4},{5,5},{6,6},{7,7},{8,8},{9,9},{1... | collective-permute-start | bytes 1572872 | tf_op jit(solution)/shard_map/ppermute | solution.py:205
  32.6 11.3 %collective-permute-start.9 = (f32[32,2048]{1,0:T(8,128)S(1)}, f32[32,2048]{1,0:T(8,128)S(1)}, u32[]{:S(2)}, u32[]{:S(2)}) collective-permute-start(f32[32,2048]{1,0:T(8,128)S(1)} %get-tuple-element.23), channel_id=1, source_target_pairs={{0,2},{1,3},{6,4},{7,5},{8,10},{9,11},{14,12},{15,13},{16,18},{17,... | collective-permute-start | bytes 786440 | tf_op jit(solution)/shard_map/ppermute | solution.py:269
  37.3 18.4 %collective-permute-start.11 = (f32[64,2048]{1,0:T(8,128)S(1)}, f32[64,2048]{1,0:T(8,128)S(1)}, u32[]{:S(2)}, u32[]{:S(2)}) collective-permute-start(f32[64,2048]{1,0:T(8,128)S(1)} %collective-permute-done.6.flipped_ref), channel_id=1, source_target_pairs={{0,1},{1,3},{2,0},{3,2},{4,5},{5,7},{6,4},{7,6},{8,9},{9,11},{10,8... | collective-permute-start | bytes 1572872 | tf_op jit(solution)/shard_map/ppermute | solution.py:219
  37.3 18.4 %collective-permute-start.8 = (f32[32,2048]{1,0:T(8,128)S(1)}, f32[32,2048]{1,0:T(8,128)S(1)}, u32[]{:S(2)}, u32[]{:S(2)}) collective-permute-start(f32[32,2048]{1,0:T(8,128)S(1)} %get-tuple-element.22), channel_id=1, source_target_pairs={{0,6},{1,7},{2,2},{3,3},{4,4},{5,5},{6,0},{7,1},{8,14},{9,15},{10,... | collective-permute-start | bytes 786440 | tf_op jit(solution)/shard_map/ppermute | solution.py:205
  43.9 11.8 %collective-permute-start.10 = (f32[32,2048]{1,0:T(8,128)S(1)}, f32[32,2048]{1,0:T(8,128)S(1)}, u32[]{:S(2)}, u32[]{:S(2)}) collective-permute-start(f32[32,2048]{1,0:T(8,128)S(1)} %collective-permute-done.9), channel_id=1, source_target_pairs={{2,6},{3,7},{4,0},{5,1},{10,14},{11,15},{12,8},{13,9},{18,22},{19,... | collective-permute-start | bytes 786440 | tf_op jit(solution)/shard_map/ppermute | solution.py:269
  56.4 2.0 %collective-permute-start.12 = (f32[64,2048]{1,0:T(8,128)S(1)}, f32[64,2048]{1,0:T(8,128)S(1)}, u32[]{:S(2)}, u32[]{:S(2)}) collective-permute-start(f32[64,2048]{1,0:T(8,128)S(1)} %get-tuple-element.24.field_ref), channel_id=1, source_target_pairs={{0,1},{1,0},{2,3},{3,2},{4,5},{5,4},{6,7},{7,6},{8,9},{9,8},{10,11... | collective-permute-start | bytes 1572872 | tf_op jit(solution)/shard_map/ppermute | solution.py:222
  56.5 15.2 %collective-permute-start.13 = (f32[64,1536]{1,0:T(8,128)S(1)}, f32[64,1536]{1,0:T(8,128)S(1)}, u32[]{:S(2)}, u32[]{:S(2)}) collective-permute-start(f32[64,1536]{1,0:T(8,128)S(1)} %get-tuple-element.30), channel_id=1, source_target_pairs={{0,3},{2,14},{3,15},{7,4},{8,11},{12,0},{13,1},{15,12},{16,19},{18... | collective-permute-start | bytes 1179656 | tf_op jit(solution)/shard_map/ppermute | solution.py:215
  58.4 13.3 %collective-permute-start.15 = (f32[64,1024]{1,0:T(8,128)S(1)}, f32[64,1024]{1,0:T(8,128)S(1)}, u32[]{:S(2)}, u32[]{:S(2)}) collective-permute-start(f32[64,1024]{1,0:T(8,128)S(1)} %get-tuple-element.32), channel_id=1, source_target_pairs={{0,6},{1,7},{2,2},{3,3},{4,4},{5,5},{6,0},{7,1},{8,14},{9,15},{10,... | collective-permute-start | bytes 786440 | tf_op jit(solution)/shard_map/ppermute | solution.py:205
  60.4 11.3 %collective-permute-start.14 = (f32[64,512]{1,0:T(8,128)S(1)}, f32[64,512]{1,0:T(8,128)S(1)}, u32[]{:S(2)}, u32[]{:S(2)}) collective-permute-start(f32[64,512]{1,0:T(8,128)S(1)} %get-tuple-element.31), channel_id=1, source_target_pairs={{0,12},{1,13},{3,0},{4,7},{11,8},{12,15},{14,2},{15,3},{16,28},{17... | collective-permute-start | bytes 393224 | tf_op jit(solution)/shard_map/ppermute | solution.py:215
  72.9 1.3 %collective-permute-start.16 = (f32[64,128]{1,0:T(8,128)S(1)}, f32[64,128]{1,0:T(8,128)S(1)}, u32[]{:S(2)}, u32[]{:S(2)}) collective-permute-start(f32[64,128]{1,0:T(8,128)S(1)} %crossed.1), channel_id=1, source_target_pairs={{0,1},{1,0},{2,3},{3,2},{4,5},{5,4},{6,7},{7,6},{8,9},{9,8},{10,11... | collective-permute-start | bytes 98312 | tf_op jit(solution)/shard_map/ppermute | solution.py:222
  74.1 4.8 %collective-permute-start.19 = (f32[64,128]{1,0:T(8,128)S(1)}, f32[64,128]{1,0:T(8,128)S(1)}, u32[]{:S(2)}, u32[]{:S(2)}) collective-permute-start(f32[64,128]{1,0:T(8,128)S(1)} %add.23), channel_id=1, source_target_pairs={{0,6},{1,7},{2,4},{3,5},{4,2},{5,3},{6,0},{7,1},{8,14},{9,15},{10,... | collective-permute-start | bytes 98312 | tf_op jit(solution)/shard_map/ppermute | solution.py:222
  74.1 4.9 %collective-permute-start.18 = (f32[64,128]{1,0:T(8,128)S(1)}, f32[64,128]{1,0:T(8,128)S(1)}, u32[]{:S(2)}, u32[]{:S(2)}) collective-permute-start(f32[64,128]{1,0:T(8,128)S(1)} %add.23), channel_id=1, source_target_pairs={{0,4},{1,5},{2,6},{3,7},{4,0},{5,1},{6,2},{7,3},{8,12},{9,13},{10,... | collective-permute-start | bytes 98312 | tf_op jit(solution)/shard_map/ppermute | solution.py:222
  76.8 3.9 %collective-permute-start.17 = (f32[64,128]{1,0:T(8,128)S(1)}, f32[64,128]{1,0:T(8,128)S(1)}, u32[]{:S(2)}, u32[]{:S(2)}) collective-permute-start(f32[64,128]{1,0:T(8,128)S(1)} %add.23), channel_id=1, source_target_pairs={{0,2},{1,3},{2,0},{3,1},{4,6},{5,7},{6,4},{7,5},{8,10},{9,11},{10,... | collective-permute-start | bytes 98312 | tf_op jit(solution)/shard_map/ppermute | solution.py:222
  80.8 4.9 %collective-permute-start.20 = (f32[64,128]{1,0:T(8,128)S(1)}, f32[64,128]{1,0:T(8,128)S(1)}, u32[]{:S(2)}, u32[]{:S(2)}) collective-permute-start(f32[64,128]{1,0:T(8,128)S(1)} %add_add_fusion), channel_id=1, source_target_pairs={{0,8},{1,9},{2,10},{3,11},{4,12},{5,13},{6,14},{7,15},{8,0},{9,1},... | collective-permute-start | bytes 98312 | tf_op jit(solution)/shard_map/ppermute | solution.py:222

commit v2 on v1

--- a/solution.py
+++ b/solution.py
@@ -16,6 +16,20 @@
 F32, BF16 = jnp.float32, jnp.bfloat16
 SMEM = pl.BlockSpec(memory_space=pltpu.SMEM)
 LIMIT = 32 * 1024 * 1024
+FIRST_LIMIT = 50 * 1024 * 1024
+
+
+class Part:
+    def __init__(self, ref, begin, count):
+        self.ref, self.begin, self.shape = ref, begin, (count,)
+
+    def __getitem__(self, index):
+        return self.ref[self.begin + index]
+
+
+def parts_of(table_ref, field_count):
+    fields = Part(table_ref, 2, field_count)
+    return table_ref, Part(table_ref, 2 + field_count, table_ref.shape[0] - 2 - field_count), fields
 
 
 def bit(number, place):
@@ -83,7 +97,29 @@
     return span, total + HOP_SCALE * jnp.concatenate(groups, axis=0)
 
 
-def own_kernel(place_ref, cols_ref, fields_ref, field_ref, flipped_ref, tiles_ref, map_ref, out_ref, split_ref):
+def first_own_kernel(
+    field_count, table_ref, field_ref, flipped_ref, far_tiles, map_ref, out_ref, split_ref, tiles_ref, sems
+):
+    place_ref, cols_ref, fields_ref = parts_of(table_ref, field_count)
+    blocks = tiles_ref.shape[0] // STEPS
+    fetched = []
+    for step in range(STEPS):
+        span = pl.ds(step * blocks, blocks)
+        fetched.append(pltpu.make_async_copy(far_tiles.at[span], tiles_ref.at[span], sems.at[step]))
+    for copy in fetched:
+        copy.start()
+    split_ref[...] = stacked(field_ref[...])
+    for step in range(STEPS):
+        fetched[step].wait()
+        for row in range(blocks):
+            span, total = own_block(
+                step * blocks + row, place_ref[0], cols_ref, fields_ref, field_ref, split_ref, flipped_ref, tiles_ref, map_ref
+            )
+            out_ref[:, span] = total
+
+
+def own_kernel(field_count, table_ref, field_ref, flipped_ref, tiles_ref, map_ref, out_ref, split_ref):
+    place_ref, cols_ref, fields_ref = parts_of(table_ref, field_count)
     blocks = tiles_ref.shape[0] // STEPS
     split_ref[...] = stacked(field_ref[...])
 
@@ -99,8 +135,9 @@
 
 
 def own_gram_kernel(
-    place_ref, cols_ref, fields_ref, live_ref, field_ref, flipped_ref, tiles_ref, map_ref, out_ref, copy_ref, split_ref, sem
+    field_count, table_ref, live_ref, field_ref, flipped_ref, tiles_ref, map_ref, out_ref, copy_ref, split_ref, sem
 ):
+    place_ref, cols_ref, fields_ref = parts_of(table_ref, field_count)
     blocks, tile = tiles_ref.shape[0] // STEPS, tiles_ref.shape[2]
     count, width = field_ref.shape[0], blocks * tile
     copy = pltpu.make_async_copy(field_ref, copy_ref, sem)
@@ -189,6 +226,7 @@
     position = lax.axis_index(AXES)
     parity = sum(bit(position, place) for place in range(0, bonds + 1, 2)) & 1
     place = jnp.stack([position ^ flip, parity]).astype(jnp.int32)
+    table = jnp.concatenate([place, field_levels, tile_cols])
     vec_count, row_count = vectors.shape
     tile_size = tile_values.shape[1]
     block_count = row_count // tile_size
@@ -235,33 +273,49 @@
 
     full = rows_by(vec_count, row_count)
 
+    def first_own_part(field, flipped):
+        return pl.pallas_call(
+            functools.partial(first_own_kernel, bonds + 1),
+            out_shape=full,
+            in_specs=[SMEM] + [inside] * 2 + [pl.BlockSpec(memory_space=pl.ANY), inside],
+            out_specs=inside,
+            scratch_shapes=[
+                split,
+                pltpu.VMEM(tiles.shape, F32),
+                pltpu.SemaphoreType.DMA((STEPS,)),
+            ],
+            compiler_params=pltpu.CompilerParams(vmem_limit_bytes=FIRST_LIMIT),
+            cost_estimate=own_cost,
+            name="first_own",
+        )(table, field, flipped, tiles, targets)
+
     def own_part(field, flipped):
         return pl.pallas_call(
-            own_kernel,
+            functools.partial(own_kernel, bonds + 1),
             out_shape=full,
-            in_specs=[SMEM] * 3 + [inside] * 4,
+            in_specs=[SMEM] + [inside] * 4,
             out_specs=inside,
             scratch_shapes=[split],
             compiler_params=params,
             cost_estimate=own_cost,
             name="own",
-        )(place, tile_cols, field_levels, field, flipped, tiles, targets)
+        )(table, field, flipped, tiles, targets)
 
     def own_gram(field, flipped):
         return pl.pallas_call(
-            own_gram_kernel,
+            functools.partial(own_gram_kernel, bonds + 1),
             out_shape=[gram_shape, full],
-            in_specs=[SMEM] * 4 + [inside] * 4,
+            in_specs=[SMEM] * 2 + [inside] * 4,
             out_specs=[inside, pl.BlockSpec(memory_space=pl.ANY)],
             scratch_shapes=[split, pltpu.SemaphoreType.DMA(())],
             compiler_params=params,
             cost_estimate=own_cost,
             name="own_gram",
-        )(place, tile_cols, field_levels, live_rows, field, flipped, tiles, targets)
+        )(table, live_rows, field, flipped, tiles, targets)
 
     three = [full, rows_by(vec_count // 2, row_count), rows_by(vec_count // 2, row_count)]
 
-    def apply(field, first_half, second_half):
+    def apply(own, field, first_half, second_half):
         legs = [(here, here ^ 2) for here in range(dev_count) if coupled(here, 1)]
         round_way = [(here, here ^ 4) for here in range(dev_count) if not coupled(here, 1)]
         flipped = exchange(field, 1)
@@ -278,7 +332,7 @@
             compiler_params=params,
             cost_estimate=pl.CostEstimate(flops=vec_count * row_count, bytes_accessed=12 * vec_count * row_count, transcendentals=0),
             name="far",
-        )(place, own_part(field, flipped), *far)
+        )(table, own(field, flipped), *far)
         return total, [direct, aside, closest]
 
     start, *halves_of = pl.pallas_call(
@@ -289,7 +343,7 @@
         compiler_params=params,
         name="start",
     )(live_rows, vectors)
-    own, hops = apply(start, *halves_of)
+    own, hops = apply(first_own_part, start, *halves_of)
     first, *halves_of = pl.pallas_call(
         combine_kernel,
         out_shape=three,
@@ -297,8 +351,8 @@
         out_specs=[inside] * 3,
         compiler_params=params,
         name="combine",
-    )(place, live_rows, own, *hops)
-    own, hops = apply(first, *halves_of)
+    )(table, live_rows, own, *hops)
+    own, hops = apply(own_part, first, *halves_of)
     cut = row_count * 3 // 4
     kept, sent, lead, rest = pl.pallas_call(
         filter_kernel,
@@ -307,7 +361,7 @@
         out_specs=[inside] * 4,
         compiler_params=params,
         name="filter",
-    )(place, live_rows, own, start, *hops)
+    )(table, live_rows, own, start, *hops)
     flipped = exchange(kept, 1)
     hops = [one_way(lead, bond, 1) for bond in reversed(range(2, bonds))]
     flipped, sent, rest = lax.optimization_barrier((flipped, sent, rest))
@@ -321,7 +375,7 @@
         out_specs=inside,
         compiler_params=params,
         name="crossed",
-    )(place, grams, kept, *hops)
+    )(table, grams, kept, *hops)
     sums = sums + exchange(sums, 1)
     for digit in range(1, bonds + 1, 2):
         near_mask, far_mask = 1 << digit, 2 << digit

time: 86.9 us -> 85.5 us (0.984)
  local copies, waits for them, and re-layouts: 5.93 us -> 2.43 us
  starting transfers between devices: 36.1 us -> 38.1 us
  waiting for transfers between devices: 25.8 us -> 23.9 us
  Pallas kernels: 16.8 us -> 18.2 us
    unnamed x12 -> x6, local copies, waits for them, and re-layouts: 5.23 us -> 1.74 us
    pallas_call x3, Pallas kernels: 12.9 us -> 14.3 us  [the longest x1 5.68 us: own_gram(): pl.pallas_call(functools.partial(own_gram_kernel, bonds + 1), out_shape=[...]
    ppermute x4, starting transfers between devices: 10.7 us -> 12 us  [apply(): aside = lax.ppermute(lax.ppermute(second_half, AXES, legs), AXES, round_way)]
    ppermute x8, starting transfers between devices: 4.3 us -> 5.51 us  [exchange(): lax.ppermute(value, AXES, [(source, source ^ mask) for source in range(de...]
    ppermute x8, waiting for transfers between devices: 9.13 us -> 8.04 us  [exchange(): lax.ppermute(value, AXES, [(source, source ^ mask) for source in range(de...]
  transfers between devices with their start and end apart: 21 -> 21, of which waited for: 9 -> 10; matrix products, arithmetic and copies ran while one was open for 0% -> 1% of each run, Pallas kernels for 16% -> 18%
where the time goes in v2:
time: 85.5 us; the launch traced here: 85 us
  starting transfers between devices  38.1 us (45%)
  waiting for transfers between devices  23.9 us (28%)
  Pallas kernels  18.2 us (21%)
  local copies, waits for them, and re-layouts  2.43 us (3%)
  between operations  1.53 us (2%)
    ppermute x5, starting transfers between devices, hop(): return lax.ppermute(value, AXES, pairs)  14.6 us
    ppermute x4, starting transfers between devices, apply(): aside = lax.ppermute(lax.ppermute(second_half, AXES, legs), AXES, round_way)  12 us
    ppermute x4, waiting for transfers between devices, apply(): aside = lax.ppermute(lax.ppermute(second_half, AXES, legs), AXES, round_way)  9.33 us
    ppermute x8, waiting for transfers between devices, exchange(): lax.ppermute(value, AXES, [(source, source ^ mask) for source in range(de...  8.04 us
    ppermute x2, starting transfers between devices, one_way(): return lax.ppermute(value, AXES, pairs)  5.97 us
    pallas_call x1, Pallas kernels, own_gram(): pl.pallas_call(functools.partial(own_gram_kernel, bonds + 1), out_shape=[...  5.68 us
    ppermute x8, starting transfers between devices, exchange(): lax.ppermute(value, AXES, [(source, source ^ mask) for source in range(de...  5.51 us
    ppermute x5, waiting for transfers between devices, hop(): return lax.ppermute(value, AXES, pairs)  5.4 us
  transfers between devices with their start and end apart: 21, of which 10 were waited for; matrix products, arithmetic and copies ran while one was open for 1% of the time, Pallas kernels for 18%

profile of v2, /device:TPU:0, one launch (start us, length us, event | category | flops | bytes accessed | tf_op | source)
XLA Modules:
  0.0 85.0 jit_solution(14366568939614211034)
XLA Ops:
  1.3 1.0 %copy-done.1 = f32[64,2048]{1,0:T(8,128)S(1)} copy-done((f32[64,2048]{1,0:T(8,128)S(1)}, f32[64,2048]{1,0:T(8,128)}, u32[]{:S(2)}) %copy-start.1) | copy-done | bytes 524312
  2.3 0.1 start.1
  2.4 0.5 collective-permute-start
  2.9 6.5 %collective-permute-start.1 = (f32[64,2048]{1,0:T(8,128)S(1)}, f32[64,2048]{1,0:T(8,128)S(1)}, u32[]{:S(2)}, u32[]{:S(2)}) collective-permute-start(f32[64,2048]{1,0:T(8,128)S(1)} %get-tuple-element.18.field_ref.start_ref), channel_id=1, source_target_pairs={{0,12},{1,13},{2,14},{3,15},{4,4},{5,5},{6,6},{7,7},{8,8},{9,9},{1... | collective-permute-start | bytes 1572872 | tf_op jit(solution)/shard_map/ppermute | solution.py:243
  9.4 3.4 %collective-permute-start.3 = (f32[32,2048]{1,0:T(8,128)S(1)}, f32[32,2048]{1,0:T(8,128)S(1)}, u32[]{:S(2)}, u32[]{:S(2)}) collective-permute-start(f32[32,2048]{1,0:T(8,128)S(1)} %get-tuple-element.20), channel_id=1, source_target_pairs={{0,2},{1,3},{6,4},{7,5},{8,10},{9,11},{14,12},{15,13},{16,18},{17,... | collective-permute-start | bytes 786440 | tf_op jit(solution)/shard_map/ppermute | solution.py:323
  12.9 0.0 collective-permute-start.5
  12.9 1.9 %collective-permute-start.2 = (f32[32,2048]{1,0:T(8,128)S(1)}, f32[32,2048]{1,0:T(8,128)S(1)}, u32[]{:S(2)}, u32[]{:S(2)}) collective-permute-start(f32[32,2048]{1,0:T(8,128)S(1)} %get-tuple-element.19), channel_id=1, source_target_pairs={{0,6},{1,7},{2,2},{3,3},{4,4},{5,5},{6,0},{7,1},{8,14},{9,15},{10,... | collective-permute-start | bytes 786440 | tf_op jit(solution)/shard_map/ppermute | solution.py:243
  14.9 4.7 %collective-permute-done.3 = f32[32,2048]{1,0:T(8,128)S(1)} collective-permute-done((f32[32,2048]{1,0:T(8,128)S(1)}, f32[32,2048]{1,0:T(8,128)S(1)}, u32[]{:S(2)}, u32[]{:S(2)}) %collective-permute-start.3) | collective-permute-done | bytes 262176 | tf_op jit(solution)/shard_map/ppermute | solution.py:323
  19.5 1.3 %collective-permute-start.4 = (f32[32,2048]{1,0:T(8,128)S(1)}, f32[32,2048]{1,0:T(8,128)S(1)}, u32[]{:S(2)}, u32[]{:S(2)}) collective-permute-start(f32[32,2048]{1,0:T(8,128)S(1)} %collective-permute-done.3), channel_id=1, source_target_pairs={{2,6},{3,7},{4,0},{5,1},{10,14},{11,15},{12,8},{13,9},{18,22},{19,... | collective-permute-start | bytes 786440 | tf_op jit(solution)/shard_map/ppermute | solution.py:323
  20.8 0.8 pad_add_fusion.table_ref.place_ref
  21.6 0.7 copy-done.2
  22.3 4.9 %first_own.1.own_ref = f32[64,2048]{1,0:T(8,128)S(1)} custom-call(s32[70]{0:T(128)S(1)} %pad_add_fusion.table_ref.place_ref, f32[64,2048]{1,0:T(8,128)S(1)} %get-tuple-element.18.field_ref.start_ref, f32[64,2048]{1,0:T(8,128)S(1)} %collective-permute-done.flipped_ref, f32[16,4,128,128]{3,2,1,0:T(8,128)} %bitcast.4, s32[1,2048]{1,0:T(1,128)S(1)} %bitcast.7), custom_call_target="tpu_custom_call" | custom-call | flops 536870912 | bytes 5767168 | tf_op jit(solution)/shard_map/first_own/pallas_call | solution.py:277
  27.2 0.6 far.2.own_ref
  27.9 0.7 collective-permute-done.2.refs_0_
  28.6 0.0 collective-permute-done.4.refs_1_
  28.6 0.0 collective-permute-done.5.refs_2_
  28.6 0.7 combine.1
  29.3 0.1 collective-permute-start.6
  29.3 1.9 %collective-permute-start.7 = (f32[64,2048]{1,0:T(8,128)S(1)}, f32[64,2048]{1,0:T(8,128)S(1)}, u32[]{:S(2)}, u32[]{:S(2)}) collective-permute-start(f32[64,2048]{1,0:T(8,128)S(1)} %get-tuple-element.21.field_ref), channel_id=1, source_target_pairs={{0,12},{1,13},{2,14},{3,15},{4,4},{5,5},{6,6},{7,7},{8,8},{9,9},{1... | collective-permute-start | bytes 1572872 | tf_op jit(solution)/shard_map/ppermute | solution.py:243
  31.3 6.0 %collective-permute-start.9 = (f32[32,2048]{1,0:T(8,128)S(1)}, f32[32,2048]{1,0:T(8,128)S(1)}, u32[]{:S(2)}, u32[]{:S(2)}) collective-permute-start(f32[32,2048]{1,0:T(8,128)S(1)} %get-tuple-element.23), channel_id=1, source_target_pairs={{0,2},{1,3},{6,4},{7,5},{8,10},{9,11},{14,12},{15,13},{16,18},{17,... | collective-permute-start | bytes 786440 | tf_op jit(solution)/shard_map/ppermute | solution.py:323
  37.3 0.0 collective-permute-done.6.flipped_ref
  37.3 0.0 collective-permute-start.11
  37.3 1.9 %collective-permute-start.8 = (f32[32,2048]{1,0:T(8,128)S(1)}, f32[32,2048]{1,0:T(8,128)S(1)}, u32[]{:S(2)}, u32[]{:S(2)}) collective-permute-start(f32[32,2048]{1,0:T(8,128)S(1)} %get-tuple-element.22), channel_id=1, source_target_pairs={{0,6},{1,7},{2,2},{3,3},{4,4},{5,5},{6,0},{7,1},{8,14},{9,15},{10,... | collective-permute-start | bytes 786440 | tf_op jit(solution)/shard_map/ppermute | solution.py:243
  39.2 4.7 %collective-permute-done.9 = f32[32,2048]{1,0:T(8,128)S(1)} collective-permute-done((f32[32,2048]{1,0:T(8,128)S(1)}, f32[32,2048]{1,0:T(8,128)S(1)}, u32[]{:S(2)}, u32[]{:S(2)}) %collective-permute-start.9) | collective-permute-done | bytes 262176 | tf_op jit(solution)/shard_map/ppermute | solution.py:323
  43.9 1.3 %collective-permute-start.10 = (f32[32,2048]{1,0:T(8,128)S(1)}, f32[32,2048]{1,0:T(8,128)S(1)}, u32[]{:S(2)}, u32[]{:S(2)}) collective-permute-start(f32[32,2048]{1,0:T(8,128)S(1)} %collective-permute-done.9), channel_id=1, source_target_pairs={{2,6},{3,7},{4,0},{5,1},{10,14},{11,15},{12,8},{13,9},{18,22},{19,... | collective-permute-start | bytes 786440 | tf_op jit(solution)/shard_map/ppermute | solution.py:323
  45.2 3.7 %own.1.own_ref = f32[64,2048]{1,0:T(8,128)S(1)} custom-call(s32[70]{0:T(128)S(1)} %pad_add_fusion.table_ref.place_ref, f32[64,2048]{1,0:T(8,128)S(1)} %get-tuple-element.21.field_ref, f32[64,2048]{1,0:T(8,128)S(1)} %collective-permute-done.6.flipped_ref, f32[16,4,128,128]{3,2,1,0:T(8,128)S(1)} %bitcast.5, s32[1,2048]{1,0:T(1,128)S(1)} %bitcast.8), custom_call_target="tpu_custom_call" | custom-call | flops 536870912 | bytes 5767168 | tf_op jit(solution)/shard_map/own/pallas_call | solution.py:293
  48.9 0.0 collective-permute-done.7.refs_0_
  48.9 0.6 far.3.own_ref
  49.5 4.7 %collective-permute-done.8.refs_0_ = f32[32,2048]{1,0:T(8,128)S(1)} collective-permute-done((f32[32,2048]{1,0:T(8,128)S(1)}, f32[32,2048]{1,0:T(8,128)S(1)}, u32[]{:S(2)}, u32[]{:S(2)}) %collective-permute-start.8) | collective-permute-done | bytes 262176 | tf_op jit(solution)/shard_map/ppermute | solution.py:243
  54.2 0.0 collective-permute-done.10.refs_1_
  54.2 0.7 filter.1
  55.0 0.1 collective-permute-start.12
  55.0 1.9 %collective-permute-start.13 = (f32[64,1536]{1,0:T(8,128)S(1)}, f32[64,1536]{1,0:T(8,128)S(1)}, u32[]{:S(2)}, u32[]{:S(2)}) collective-permute-start(f32[64,1536]{1,0:T(8,128)S(1)} %get-tuple-element.30), channel_id=1, source_target_pairs={{0,3},{2,14},{3,15},{7,4},{8,11},{12,0},{13,1},{15,12},{16,19},{18... | collective-permute-start | bytes 1179656 | tf_op jit(solution)/shard_map/ppermute | solution.py:253
  57.0 2.3 %collective-permute-start.15 = (f32[64,1024]{1,0:T(8,128)S(1)}, f32[64,1024]{1,0:T(8,128)S(1)}, u32[]{:S(2)}, u32[]{:S(2)}) collective-permute-start(f32[64,1024]{1,0:T(8,128)S(1)} %get-tuple-element.32), channel_id=1, source_target_pairs={{0,6},{1,7},{2,2},{3,3},{4,4},{5,5},{6,0},{7,1},{8,14},{9,15},{10,... | collective-permute-start | bytes 786440 | tf_op jit(solution)/shard_map/ppermute | solution.py:243
  59.3 4.1 %collective-permute-start.14 = (f32[64,512]{1,0:T(8,128)S(1)}, f32[64,512]{1,0:T(8,128)S(1)}, u32[]{:S(2)}, u32[]{:S(2)}) collective-permute-start(f32[64,512]{1,0:T(8,128)S(1)} %get-tuple-element.31), channel_id=1, source_target_pairs={{0,12},{1,13},{3,0},{4,7},{11,8},{12,15},{14,2},{15,3},{16,28},{17... | collective-permute-start | bytes 393224 | tf_op jit(solution)/shard_map/ppermute | solution.py:253
  63.4 5.7 %own_gram.1 = (f32[64,128]{1,0:T(8,128)S(1)}, f32[64,2048]{1,0:T(8,128)}) custom-call(s32[70]{0:T(128)S(1)} %pad_add_fusion.table_ref.place_ref, s32[1]{0:T(128)S(6)} %copy.13.live_ref, f32[64,2048]{1,0:T(8,128)S(1)} %get-tuple-element.24.field_ref, f32[64,2048]{1,0:T(8,128)S(1)} %collective-permute-done.12.flipped_ref, f32[16,4,128,128]{3,2,1,0:T(8,128)S(1)} %bitcast.6, ...), custom_call_target="tpu_custom_call" | custom-call | flops 536870912 | bytes 5767168 | tf_op jit(solution)/shard_map/own_gram/pallas_call | solution.py:305
  69.1 1.2 %collective-permute-done.13.refs_0_ = f32[64,1536]{1,0:T(8,128)S(1)} collective-permute-done((f32[64,1536]{1,0:T(8,128)S(1)}, f32[64,1536]{1,0:T(8,128)S(1)}, u32[]{:S(2)}, u32[]{:S(2)}) %collective-permute-start.13) | collective-permute-done | bytes 393248 | tf_op jit(solution)/shard_map/ppermute | solution.py:253
  70.2 1.1 %crossed.1 = f32[64,128]{1,0:T(8,128)S(1)} custom-call(s32[70]{0:T(128)S(1)} %pad_add_fusion.table_ref.place_ref, f32[64,128]{1,0:T(8,128)S(1)} %get-tuple-element.29.own_ref, f32[64,2048]{1,0:T(8,128)S(1)} %get-tuple-element.24.field_ref, f32[64,1536]{1,0:T(8,128)S(1)} %collective-permute-done.13.refs_0_, f32[64,512]{1,0:T(8,128)S(1)} %collective-permute-done.14.refs_1_, ...), custom_call_target="tpu_custom_call" | custom-call | tf_op jit(solution)/shard_map/crossed/pallas_call | solution.py:371
  71.4 0.1 collective-permute-start.16
  71.5 1.2 %collective-permute-done.16 = f32[64,128]{1,0:T(8,128)S(1)} collective-permute-done((f32[64,128]{1,0:T(8,128)S(1)}, f32[64,128]{1,0:T(8,128)S(1)}, u32[]{:S(2)}, u32[]{:S(2)}) %collective-permute-start.16) | collective-permute-done | bytes 32800 | tf_op jit(solution)/shard_map/ppermute | solution.py:260
  72.7 2.7 %collective-permute-start.18 = (f32[64,128]{1,0:T(8,128)S(1)}, f32[64,128]{1,0:T(8,128)S(1)}, u32[]{:S(2)}, u32[]{:S(2)}) collective-permute-start(f32[64,128]{1,0:T(8,128)S(1)} %add.23), channel_id=1, source_target_pairs={{0,4},{1,5},{2,6},{3,7},{4,0},{5,1},{6,2},{7,3},{8,12},{9,13},{10,... | collective-permute-start | bytes 98312 | tf_op jit(solution)/shard_map/ppermute | solution.py:260
  75.4 0.8 collective-permute-start.17
  76.2 1.3 %collective-permute-done.19 = f32[64,128]{1,0:T(8,128)S(1)} collective-permute-done((f32[64,128]{1,0:T(8,128)S(1)}, f32[64,128]{1,0:T(8,128)S(1)}, u32[]{:S(2)}, u32[]{:S(2)}) %collective-permute-start.19) | collective-permute-done | bytes 32800 | tf_op jit(solution)/shard_map/ppermute | solution.py:260
  77.5 0.1 collective-permute-done.18
  77.6 1.7 %collective-permute-done.17 = f32[64,128]{1,0:T(8,128)S(1)} collective-permute-done((f32[64,128]{1,0:T(8,128)S(1)}, f32[64,128]{1,0:T(8,128)S(1)}, u32[]{:S(2)}, u32[]{:S(2)}) %collective-permute-start.17) | collective-permute-done | bytes 32800 | tf_op jit(solution)/shard_map/ppermute | solution.py:260
  79.3 1.3 %collective-permute-start.20 = (f32[64,128]{1,0:T(8,128)S(1)}, f32[64,128]{1,0:T(8,128)S(1)}, u32[]{:S(2)}, u32[]{:S(2)}) collective-permute-start(f32[64,128]{1,0:T(8,128)S(1)} %add_add_fusion), channel_id=1, source_target_pairs={{0,8},{1,9},{2,10},{3,11},{4,12},{5,13},{6,14},{7,15},{8,0},{9,1},... | collective-permute-start | bytes 98312 | tf_op jit(solution)/shard_map/ppermute | solution.py:260
  80.6 3.7 %collective-permute-done.20 = f32[64,128]{1,0:T(8,128)S(1)} collective-permute-done((f32[64,128]{1,0:T(8,128)S(1)}, f32[64,128]{1,0:T(8,128)S(1)}, u32[]{:S(2)}, u32[]{:S(2)}) %collective-permute-start.20) | collective-permute-done | bytes 32800 | tf_op jit(solution)/shard_map/ppermute | solution.py:260
  84.3 0.7 fusion
  (14 shorter events, 0.0 us)
Async XLA Ops:
  1.3 1.0 %copy-start.1 = (f32[64,2048]{1,0:T(8,128)S(1)}, f32[64,2048]{1,0:T(8,128)}, u32[]{:S(2)}) copy-start(f32[64,2048]{1,0:T(8,128)} %vectors_ref.1) | copy-start | bytes 1572868
  2.4 10.5 %collective-permute-start = (f32[64,2048]{1,0:T(8,128)S(1)}, f32[64,2048]{1,0:T(8,128)S(1)}, u32[]{:S(2)}, u32[]{:S(2)}) collective-permute-start(f32[64,2048]{1,0:T(8,128)S(1)} %get-tuple-element.18.field_ref.start_ref), channel_id=1, source_target_pairs={{0,1},{1,0},{2,3},{3,2},{4,5},{5,4},{6,7},{7,6},{8,9},{9,8},{10,11... | collective-permute-start | bytes 1572872 | tf_op jit(solution)/shard_map/ppermute | solution.py:260
  2.9 24.3 %collective-permute-start.1 = (f32[64,2048]{1,0:T(8,128)S(1)}, f32[64,2048]{1,0:T(8,128)S(1)}, u32[]{:S(2)}, u32[]{:S(2)}) collective-permute-start(f32[64,2048]{1,0:T(8,128)S(1)} %get-tuple-element.18.field_ref.start_ref), channel_id=1, source_target_pairs={{0,12},{1,13},{2,14},{3,15},{4,4},{5,5},{6,6},{7,7},{8,8},{9,9},{1... | collective-permute-start | bytes 1572872 | tf_op jit(solution)/shard_map/ppermute | solution.py:243
  9.4 10.1 %collective-permute-start.3 = (f32[32,2048]{1,0:T(8,128)S(1)}, f32[32,2048]{1,0:T(8,128)S(1)}, u32[]{:S(2)}, u32[]{:S(2)}) collective-permute-start(f32[32,2048]{1,0:T(8,128)S(1)} %get-tuple-element.20), channel_id=1, source_target_pairs={{0,2},{1,3},{6,4},{7,5},{8,10},{9,11},{14,12},{15,13},{16,18},{17,... | collective-permute-start | bytes 786440 | tf_op jit(solution)/shard_map/ppermute | solution.py:323
  12.9 15.7 %collective-permute-start.5 = (f32[64,2048]{1,0:T(8,128)S(1)}, f32[64,2048]{1,0:T(8,128)S(1)}, u32[]{:S(2)}, u32[]{:S(2)}) collective-permute-start(f32[64,2048]{1,0:T(8,128)S(1)} %collective-permute-done.flipped_ref), channel_id=1, source_target_pairs={{0,1},{1,3},{2,0},{3,2},{4,5},{5,7},{6,4},{7,6},{8,9},{9,11},{10,8... | collective-permute-start | bytes 1572872 | tf_op jit(solution)/shard_map/ppermute | solution.py:257
  12.9 15.6 %collective-permute-start.2 = (f32[32,2048]{1,0:T(8,128)S(1)}, f32[32,2048]{1,0:T(8,128)S(1)}, u32[]{:S(2)}, u32[]{:S(2)}) collective-permute-start(f32[32,2048]{1,0:T(8,128)S(1)} %get-tuple-element.19), channel_id=1, source_target_pairs={{0,6},{1,7},{2,2},{3,3},{4,4},{5,5},{6,0},{7,1},{8,14},{9,15},{10,... | collective-permute-start | bytes 786440 | tf_op jit(solution)/shard_map/ppermute | solution.py:243
  19.5 9.1 %collective-permute-start.4 = (f32[32,2048]{1,0:T(8,128)S(1)}, f32[32,2048]{1,0:T(8,128)S(1)}, u32[]{:S(2)}, u32[]{:S(2)}) collective-permute-start(f32[32,2048]{1,0:T(8,128)S(1)} %collective-permute-done.3), channel_id=1, source_target_pairs={{2,6},{3,7},{4,0},{5,1},{10,14},{11,15},{12,8},{13,9},{18,22},{19,... | collective-permute-start | bytes 786440 | tf_op jit(solution)/shard_map/ppermute | solution.py:323
  21.6 0.7 copy-start.2
  22.3 22.9 %copy-start = (f32[64,128,128]{2,1,0:T(8,128)S(1)}, f32[64,128,128]{2,1,0:T(8,128)}, u32[]{:S(2)}) copy-start(f32[64,128,128]{2,1,0:T(8,128)} %param.7) | copy-start | bytes 12582916
  29.3 8.0 %collective-permute-start.6 = (f32[64,2048]{1,0:T(8,128)S(1)}, f32[64,2048]{1,0:T(8,128)S(1)}, u32[]{:S(2)}, u32[]{:S(2)}) collective-permute-start(f32[64,2048]{1,0:T(8,128)S(1)} %get-tuple-element.21.field_ref), channel_id=1, source_target_pairs={{0,1},{1,0},{2,3},{3,2},{4,5},{5,4},{6,7},{7,6},{8,9},{9,8},{10,11... | collective-permute-start | bytes 1572872 | tf_op jit(solution)/shard_map/ppermute | solution.py:260
  29.3 19.5 %collective-permute-start.7 = (f32[64,2048]{1,0:T(8,128)S(1)}, f32[64,2048]{1,0:T(8,128)S(1)}, u32[]{:S(2)}, u32[]{:S(2)}) collective-permute-start(f32[64,2048]{1,0:T(8,128)S(1)} %get-tuple-element.21.field_ref), channel_id=1, source_target_pairs={{0,12},{1,13},{2,14},{3,15},{4,4},{5,5},{6,6},{7,7},{8,8},{9,9},{1... | collective-permute-start | bytes 1572872 | tf_op jit(solution)/shard_map/ppermute | solution.py:243
  31.3 12.6 %collective-permute-start.9 = (f32[32,2048]{1,0:T(8,128)S(1)}, f32[32,2048]{1,0:T(8,128)S(1)}, u32[]{:S(2)}, u32[]{:S(2)}) collective-permute-start(f32[32,2048]{1,0:T(8,128)S(1)} %get-tuple-element.23), channel_id=1, source_target_pairs={{0,2},{1,3},{6,4},{7,5},{8,10},{9,11},{14,12},{15,13},{16,18},{17,... | collective-permute-start | bytes 786440 | tf_op jit(solution)/shard_map/ppermute | solution.py:323
  37.3 16.9 %collective-permute-start.11 = (f32[64,2048]{1,0:T(8,128)S(1)}, f32[64,2048]{1,0:T(8,128)S(1)}, u32[]{:S(2)}, u32[]{:S(2)}) collective-permute-start(f32[64,2048]{1,0:T(8,128)S(1)} %collective-permute-done.6.flipped_ref), channel_id=1, source_target_pairs={{0,1},{1,3},{2,0},{3,2},{4,5},{5,7},{6,4},{7,6},{8,9},{9,11},{10,8... | collective-permute-start | bytes 1572872 | tf_op jit(solution)/shard_map/ppermute | solution.py:257
  37.3 16.9 %collective-permute-start.8 = (f32[32,2048]{1,0:T(8,128)S(1)}, f32[32,2048]{1,0:T(8,128)S(1)}, u32[]{:S(2)}, u32[]{:S(2)}) collective-permute-start(f32[32,2048]{1,0:T(8,128)S(1)} %get-tuple-element.22), channel_id=1, source_target_pairs={{0,6},{1,7},{2,2},{3,3},{4,4},{5,5},{6,0},{7,1},{8,14},{9,15},{10,... | collective-permute-start | bytes 786440 | tf_op jit(solution)/shard_map/ppermute | solution.py:243
  43.9 10.3 %collective-permute-start.10 = (f32[32,2048]{1,0:T(8,128)S(1)}, f32[32,2048]{1,0:T(8,128)S(1)}, u32[]{:S(2)}, u32[]{:S(2)}) collective-permute-start(f32[32,2048]{1,0:T(8,128)S(1)} %collective-permute-done.9), channel_id=1, source_target_pairs={{2,6},{3,7},{4,0},{5,1},{10,14},{11,15},{12,8},{13,9},{18,22},{19,... | collective-permute-start | bytes 786440 | tf_op jit(solution)/shard_map/ppermute | solution.py:323
  55.0 2.0 %collective-permute-start.12 = (f32[64,2048]{1,0:T(8,128)S(1)}, f32[64,2048]{1,0:T(8,128)S(1)}, u32[]{:S(2)}, u32[]{:S(2)}) collective-permute-start(f32[64,2048]{1,0:T(8,128)S(1)} %get-tuple-element.24.field_ref), channel_id=1, source_target_pairs={{0,1},{1,0},{2,3},{3,2},{4,5},{5,4},{6,7},{7,6},{8,9},{9,8},{10,11... | collective-permute-start | bytes 1572872 | tf_op jit(solution)/shard_map/ppermute | solution.py:260
  55.0 15.2 %collective-permute-start.13 = (f32[64,1536]{1,0:T(8,128)S(1)}, f32[64,1536]{1,0:T(8,128)S(1)}, u32[]{:S(2)}, u32[]{:S(2)}) collective-permute-start(f32[64,1536]{1,0:T(8,128)S(1)} %get-tuple-element.30), channel_id=1, source_target_pairs={{0,3},{2,14},{3,15},{7,4},{8,11},{12,0},{13,1},{15,12},{16,19},{18... | collective-permute-start | bytes 1179656 | tf_op jit(solution)/shard_map/ppermute | solution.py:253
  57.0 13.3 %collective-permute-start.15 = (f32[64,1024]{1,0:T(8,128)S(1)}, f32[64,1024]{1,0:T(8,128)S(1)}, u32[]{:S(2)}, u32[]{:S(2)}) collective-permute-start(f32[64,1024]{1,0:T(8,128)S(1)} %get-tuple-element.32), channel_id=1, source_target_pairs={{0,6},{1,7},{2,2},{3,3},{4,4},{5,5},{6,0},{7,1},{8,14},{9,15},{10,... | collective-permute-start | bytes 786440 | tf_op jit(solution)/shard_map/ppermute | solution.py:243
  59.3 10.9 %collective-permute-start.14 = (f32[64,512]{1,0:T(8,128)S(1)}, f32[64,512]{1,0:T(8,128)S(1)}, u32[]{:S(2)}, u32[]{:S(2)}) collective-permute-start(f32[64,512]{1,0:T(8,128)S(1)} %get-tuple-element.31), channel_id=1, source_target_pairs={{0,12},{1,13},{3,0},{4,7},{11,8},{12,15},{14,2},{15,3},{16,28},{17... | collective-permute-start | bytes 393224 | tf_op jit(solution)/shard_map/ppermute | solution.py:253
  71.4 1.3 %collective-permute-start.16 = (f32[64,128]{1,0:T(8,128)S(1)}, f32[64,128]{1,0:T(8,128)S(1)}, u32[]{:S(2)}, u32[]{:S(2)}) collective-permute-start(f32[64,128]{1,0:T(8,128)S(1)} %crossed.1), channel_id=1, source_target_pairs={{0,1},{1,0},{2,3},{3,2},{4,5},{5,4},{6,7},{7,6},{8,9},{9,8},{10,11... | collective-permute-start | bytes 98312 | tf_op jit(solution)/shard_map/ppermute | solution.py:260
  72.7 4.8 %collective-permute-start.19 = (f32[64,128]{1,0:T(8,128)S(1)}, f32[64,128]{1,0:T(8,128)S(1)}, u32[]{:S(2)}, u32[]{:S(2)}) collective-permute-start(f32[64,128]{1,0:T(8,128)S(1)} %add.23), channel_id=1, source_target_pairs={{0,6},{1,7},{2,4},{3,5},{4,2},{5,3},{6,0},{7,1},{8,14},{9,15},{10,... | collective-permute-start | bytes 98312 | tf_op jit(solution)/shard_map/ppermute | solution.py:260
  72.7 4.9 %collective-permute-start.18 = (f32[64,128]{1,0:T(8,128)S(1)}, f32[64,128]{1,0:T(8,128)S(1)}, u32[]{:S(2)}, u32[]{:S(2)}) collective-permute-start(f32[64,128]{1,0:T(8,128)S(1)} %add.23), channel_id=1, source_target_pairs={{0,4},{1,5},{2,6},{3,7},{4,0},{5,1},{6,2},{7,3},{8,12},{9,13},{10,... | collective-permute-start | bytes 98312 | tf_op jit(solution)/shard_map/ppermute | solution.py:260
  75.4 3.9 %collective-permute-start.17 = (f32[64,128]{1,0:T(8,128)S(1)}, f32[64,128]{1,0:T(8,128)S(1)}, u32[]{:S(2)}, u32[]{:S(2)}) collective-permute-start(f32[64,128]{1,0:T(8,128)S(1)} %add.23), channel_id=1, source_target_pairs={{0,2},{1,3},{2,0},{3,1},{4,6},{5,7},{6,4},{7,5},{8,10},{9,11},{10,... | collective-permute-start | bytes 98312 | tf_op jit(solution)/shard_map/ppermute | solution.py:260
  79.3 5.0 %collective-permute-start.20 = (f32[64,128]{1,0:T(8,128)S(1)}, f32[64,128]{1,0:T(8,128)S(1)}, u32[]{:S(2)}, u32[]{:S(2)}) collective-permute-start(f32[64,128]{1,0:T(8,128)S(1)} %add_add_fusion), channel_id=1, source_target_pairs={{0,8},{1,9},{2,10},{3,11},{4,12},{5,13},{6,14},{7,15},{8,0},{9,1},... | collective-permute-start | bytes 98312 | tf_op jit(solution)/shard_map/ppermute | solution.py:260

commit v3 on v2

--- a/solution.py
+++ b/solution.py
@@ -102,20 +102,25 @@
 ):
     place_ref, cols_ref, fields_ref = parts_of(table_ref, field_count)
     blocks = tiles_ref.shape[0] // STEPS
-    fetched = []
+
+    def fetch(step):
+        span = pl.ds(step * blocks, blocks)
+        return pltpu.make_async_copy(far_tiles.at[span], tiles_ref.at[span], sems.at[step])
+
     for step in range(STEPS):
-        span = pl.ds(step * blocks, blocks)
-        fetched.append(pltpu.make_async_copy(far_tiles.at[span], tiles_ref.at[span], sems.at[step]))
-    for copy in fetched:
-        copy.start()
+        fetch(step).start()
     split_ref[...] = stacked(field_ref[...])
-    for step in range(STEPS):
-        fetched[step].wait()
+
+    def body(step, carry):
+        fetch(step).wait()
         for row in range(blocks):
             span, total = own_block(
                 step * blocks + row, place_ref[0], cols_ref, fields_ref, field_ref, split_ref, flipped_ref, tiles_ref, map_ref
             )
             out_ref[:, span] = total
+        return carry
+
+    lax.fori_loop(0, STEPS, body, 0)
 
 
 def own_kernel(field_count, table_ref, field_ref, flipped_ref, tiles_ref, map_ref, out_ref, split_ref):

time: 85.5 us -> 85.5 us (level)
  no operation moved by 1% of the time
where the time goes in v3:
time: 85.5 us; the launch traced here: 85 us
  starting transfers between devices  38.1 us (45%)
  waiting for transfers between devices  24 us (28%)
  Pallas kernels  18.2 us (21%)
  local copies, waits for them, and re-layouts  2.43 us (3%)
  between operations  1.53 us (2%)
    ppermute x5, starting transfers between devices, hop(): return lax.ppermute(value, AXES, pairs)  14.6 us
    ppermute x4, starting transfers between devices, apply(): aside = lax.ppermute(lax.ppermute(second_half, AXES, legs), AXES, round_way)  12 us
    ppermute x4, waiting for transfers between devices, apply(): aside = lax.ppermute(lax.ppermute(second_half, AXES, legs), AXES, round_way)  9.33 us
    ppermute x8, waiting for transfers between devices, exchange(): lax.ppermute(value, AXES, [(source, source ^ mask) for source in range(de...  8.03 us
    ppermute x2, starting transfers between devices, one_way(): return lax.ppermute(value, AXES, pairs)  6.02 us
    pallas_call x1, Pallas kernels, own_gram(): pl.pallas_call(functools.partial(own_gram_kernel, bonds + 1), out_shape=[...  5.68 us
    ppermute x8, starting transfers between devices, exchange(): lax.ppermute(value, AXES, [(source, source ^ mask) for source in range(de...  5.47 us
    ppermute x5, waiting for transfers between devices, hop(): return lax.ppermute(value, AXES, pairs)  5.44 us
  transfers between devices with their start and end apart: 21, of which 10 were waited for; matrix products, arithmetic and copies ran while one was open for 1% of the time, Pallas kernels for 18%

profile of v3, /device:TPU:0, one launch (start us, length us, event | category | flops | bytes accessed | tf_op | source)
XLA Modules:
  0.0 85.0 jit_solution(4981230376172543899)
XLA Ops:
  1.3 1.0 %copy-done.1 = f32[64,2048]{1,0:T(8,128)S(1)} copy-done((f32[64,2048]{1,0:T(8,128)S(1)}, f32[64,2048]{1,0:T(8,128)}, u32[]{:S(2)}) %copy-start.1) | copy-done | bytes 524312
  2.3 0.1 start.1
  2.4 0.5 collective-permute-start
  2.9 6.5 %collective-permute-start.1 = (f32[64,2048]{1,0:T(8,128)S(1)}, f32[64,2048]{1,0:T(8,128)S(1)}, u32[]{:S(2)}, u32[]{:S(2)}) collective-permute-start(f32[64,2048]{1,0:T(8,128)S(1)} %get-tuple-element.18.field_ref.start_ref), channel_id=1, source_target_pairs={{0,12},{1,13},{2,14},{3,15},{4,4},{5,5},{6,6},{7,7},{8,8},{9,9},{1... | collective-permute-start | bytes 1572872 | tf_op jit(solution)/shard_map/ppermute | solution.py:248
  9.4 3.4 %collective-permute-start.3 = (f32[32,2048]{1,0:T(8,128)S(1)}, f32[32,2048]{1,0:T(8,128)S(1)}, u32[]{:S(2)}, u32[]{:S(2)}) collective-permute-start(f32[32,2048]{1,0:T(8,128)S(1)} %get-tuple-element.20), channel_id=1, source_target_pairs={{0,2},{1,3},{6,4},{7,5},{8,10},{9,11},{14,12},{15,13},{16,18},{17,... | collective-permute-start | bytes 786440 | tf_op jit(solution)/shard_map/ppermute | solution.py:328
  12.9 0.0 collective-permute-start.5
  12.9 1.9 %collective-permute-start.2 = (f32[32,2048]{1,0:T(8,128)S(1)}, f32[32,2048]{1,0:T(8,128)S(1)}, u32[]{:S(2)}, u32[]{:S(2)}) collective-permute-start(f32[32,2048]{1,0:T(8,128)S(1)} %get-tuple-element.19), channel_id=1, source_target_pairs={{0,6},{1,7},{2,2},{3,3},{4,4},{5,5},{6,0},{7,1},{8,14},{9,15},{10,... | collective-permute-start | bytes 786440 | tf_op jit(solution)/shard_map/ppermute | solution.py:248
  14.9 4.7 %collective-permute-done.3 = f32[32,2048]{1,0:T(8,128)S(1)} collective-permute-done((f32[32,2048]{1,0:T(8,128)S(1)}, f32[32,2048]{1,0:T(8,128)S(1)}, u32[]{:S(2)}, u32[]{:S(2)}) %collective-permute-start.3) | collective-permute-done | bytes 262176 | tf_op jit(solution)/shard_map/ppermute | solution.py:328
  19.5 1.3 %collective-permute-start.4 = (f32[32,2048]{1,0:T(8,128)S(1)}, f32[32,2048]{1,0:T(8,128)S(1)}, u32[]{:S(2)}, u32[]{:S(2)}) collective-permute-start(f32[32,2048]{1,0:T(8,128)S(1)} %collective-permute-done.3), channel_id=1, source_target_pairs={{2,6},{3,7},{4,0},{5,1},{10,14},{11,15},{12,8},{13,9},{18,22},{19,... | collective-permute-start | bytes 786440 | tf_op jit(solution)/shard_map/ppermute | solution.py:328
  20.8 0.8 pad_add_fusion.table_ref.place_ref
  21.6 0.7 copy-done.2
  22.3 5.0 %first_own.1.own_ref = f32[64,2048]{1,0:T(8,128)S(1)} custom-call(s32[70]{0:T(128)S(1)} %pad_add_fusion.table_ref.place_ref, f32[64,2048]{1,0:T(8,128)S(1)} %get-tuple-element.18.field_ref.start_ref, f32[64,2048]{1,0:T(8,128)S(1)} %collective-permute-done.flipped_ref, f32[16,4,128,128]{3,2,1,0:T(8,128)} %bitcast.4, s32[1,2048]{1,0:T(1,128)S(1)} %bitcast.7), custom_call_target="tpu_custom_call" | custom-call | flops 536870912 | bytes 5767168 | tf_op jit(solution)/shard_map/first_own/pallas_call | solution.py:282
  27.2 0.6 far.2.own_ref
  27.9 0.7 collective-permute-done.2.refs_0_
  28.6 0.0 collective-permute-done.4.refs_1_
  28.6 0.0 collective-permute-done.5.refs_2_
  28.6 0.7 combine.1
  29.3 0.1 collective-permute-start.6
  29.3 1.9 %collective-permute-start.7 = (f32[64,2048]{1,0:T(8,128)S(1)}, f32[64,2048]{1,0:T(8,128)S(1)}, u32[]{:S(2)}, u32[]{:S(2)}) collective-permute-start(f32[64,2048]{1,0:T(8,128)S(1)} %get-tuple-element.21.field_ref), channel_id=1, source_target_pairs={{0,12},{1,13},{2,14},{3,15},{4,4},{5,5},{6,6},{7,7},{8,8},{9,9},{1... | collective-permute-start | bytes 1572872 | tf_op jit(solution)/shard_map/ppermute | solution.py:248
  31.3 6.0 %collective-permute-start.9 = (f32[32,2048]{1,0:T(8,128)S(1)}, f32[32,2048]{1,0:T(8,128)S(1)}, u32[]{:S(2)}, u32[]{:S(2)}) collective-permute-start(f32[32,2048]{1,0:T(8,128)S(1)} %get-tuple-element.23), channel_id=1, source_target_pairs={{0,2},{1,3},{6,4},{7,5},{8,10},{9,11},{14,12},{15,13},{16,18},{17,... | collective-permute-start | bytes 786440 | tf_op jit(solution)/shard_map/ppermute | solution.py:328
  37.3 0.0 collective-permute-done.6.flipped_ref
  37.3 0.0 collective-permute-start.11
  37.3 1.9 %collective-permute-start.8 = (f32[32,2048]{1,0:T(8,128)S(1)}, f32[32,2048]{1,0:T(8,128)S(1)}, u32[]{:S(2)}, u32[]{:S(2)}) collective-permute-start(f32[32,2048]{1,0:T(8,128)S(1)} %get-tuple-element.22), channel_id=1, source_target_pairs={{0,6},{1,7},{2,2},{3,3},{4,4},{5,5},{6,0},{7,1},{8,14},{9,15},{10,... | collective-permute-start | bytes 786440 | tf_op jit(solution)/shard_map/ppermute | solution.py:248
  39.2 4.7 %collective-permute-done.9 = f32[32,2048]{1,0:T(8,128)S(1)} collective-permute-done((f32[32,2048]{1,0:T(8,128)S(1)}, f32[32,2048]{1,0:T(8,128)S(1)}, u32[]{:S(2)}, u32[]{:S(2)}) %collective-permute-start.9) | collective-permute-done | bytes 262176 | tf_op jit(solution)/shard_map/ppermute | solution.py:328
  43.9 1.3 %collective-permute-start.10 = (f32[32,2048]{1,0:T(8,128)S(1)}, f32[32,2048]{1,0:T(8,128)S(1)}, u32[]{:S(2)}, u32[]{:S(2)}) collective-permute-start(f32[32,2048]{1,0:T(8,128)S(1)} %collective-permute-done.9), channel_id=1, source_target_pairs={{2,6},{3,7},{4,0},{5,1},{10,14},{11,15},{12,8},{13,9},{18,22},{19,... | collective-permute-start | bytes 786440 | tf_op jit(solution)/shard_map/ppermute | solution.py:328
  45.2 3.7 %own.1.own_ref = f32[64,2048]{1,0:T(8,128)S(1)} custom-call(s32[70]{0:T(128)S(1)} %pad_add_fusion.table_ref.place_ref, f32[64,2048]{1,0:T(8,128)S(1)} %get-tuple-element.21.field_ref, f32[64,2048]{1,0:T(8,128)S(1)} %collective-permute-done.6.flipped_ref, f32[16,4,128,128]{3,2,1,0:T(8,128)S(1)} %bitcast.5, s32[1,2048]{1,0:T(1,128)S(1)} %bitcast.8), custom_call_target="tpu_custom_call" | custom-call | flops 536870912 | bytes 5767168 | tf_op jit(solution)/shard_map/own/pallas_call | solution.py:298
  48.9 0.0 collective-permute-done.7.refs_0_
  48.9 0.6 far.3.own_ref
  49.5 4.7 %collective-permute-done.8.refs_0_ = f32[32,2048]{1,0:T(8,128)S(1)} collective-permute-done((f32[32,2048]{1,0:T(8,128)S(1)}, f32[32,2048]{1,0:T(8,128)S(1)}, u32[]{:S(2)}, u32[]{:S(2)}) %collective-permute-start.8) | collective-permute-done | bytes 262176 | tf_op jit(solution)/shard_map/ppermute | solution.py:248
  54.3 0.0 collective-permute-done.10.refs_1_
  54.3 0.7 filter.1
  55.0 0.1 collective-permute-start.12
  55.1 1.9 %collective-permute-start.13 = (f32[64,1536]{1,0:T(8,128)S(1)}, f32[64,1536]{1,0:T(8,128)S(1)}, u32[]{:S(2)}, u32[]{:S(2)}) collective-permute-start(f32[64,1536]{1,0:T(8,128)S(1)} %get-tuple-element.30), channel_id=1, source_target_pairs={{0,3},{2,14},{3,15},{7,4},{8,11},{12,0},{13,1},{15,12},{16,19},{18... | collective-permute-start | bytes 1179656 | tf_op jit(solution)/shard_map/ppermute | solution.py:258
  57.0 2.3 %collective-permute-start.15 = (f32[64,1024]{1,0:T(8,128)S(1)}, f32[64,1024]{1,0:T(8,128)S(1)}, u32[]{:S(2)}, u32[]{:S(2)}) collective-permute-start(f32[64,1024]{1,0:T(8,128)S(1)} %get-tuple-element.32), channel_id=1, source_target_pairs={{0,6},{1,7},{2,2},{3,3},{4,4},{5,5},{6,0},{7,1},{8,14},{9,15},{10,... | collective-permute-start | bytes 786440 | tf_op jit(solution)/shard_map/ppermute | solution.py:248
  59.3 4.1 %collective-permute-start.14 = (f32[64,512]{1,0:T(8,128)S(1)}, f32[64,512]{1,0:T(8,128)S(1)}, u32[]{:S(2)}, u32[]{:S(2)}) collective-permute-start(f32[64,512]{1,0:T(8,128)S(1)} %get-tuple-element.31), channel_id=1, source_target_pairs={{0,12},{1,13},{3,0},{4,7},{11,8},{12,15},{14,2},{15,3},{16,28},{17... | collective-permute-start | bytes 393224 | tf_op jit(solution)/shard_map/ppermute | solution.py:258
  63.4 5.7 %own_gram.1 = (f32[64,128]{1,0:T(8,128)S(1)}, f32[64,2048]{1,0:T(8,128)}) custom-call(s32[70]{0:T(128)S(1)} %pad_add_fusion.table_ref.place_ref, s32[1]{0:T(128)S(6)} %copy.13.live_ref, f32[64,2048]{1,0:T(8,128)S(1)} %get-tuple-element.24.field_ref, f32[64,2048]{1,0:T(8,128)S(1)} %collective-permute-done.12.flipped_ref, f32[16,4,128,128]{3,2,1,0:T(8,128)S(1)} %bitcast.6, ...), custom_call_target="tpu_custom_call" | custom-call | flops 536870912 | bytes 5767168 | tf_op jit(solution)/shard_map/own_gram/pallas_call | solution.py:310
  69.1 1.2 %collective-permute-done.13.refs_0_ = f32[64,1536]{1,0:T(8,128)S(1)} collective-permute-done((f32[64,1536]{1,0:T(8,128)S(1)}, f32[64,1536]{1,0:T(8,128)S(1)}, u32[]{:S(2)}, u32[]{:S(2)}) %collective-permute-start.13) | collective-permute-done | bytes 393248 | tf_op jit(solution)/shard_map/ppermute | solution.py:258
  70.3 1.1 %crossed.1 = f32[64,128]{1,0:T(8,128)S(1)} custom-call(s32[70]{0:T(128)S(1)} %pad_add_fusion.table_ref.place_ref, f32[64,128]{1,0:T(8,128)S(1)} %get-tuple-element.29.own_ref, f32[64,2048]{1,0:T(8,128)S(1)} %get-tuple-element.24.field_ref, f32[64,1536]{1,0:T(8,128)S(1)} %collective-permute-done.13.refs_0_, f32[64,512]{1,0:T(8,128)S(1)} %collective-permute-done.14.refs_1_, ...), custom_call_target="tpu_custom_call" | custom-call | tf_op jit(solution)/shard_map/crossed/pallas_call | solution.py:376
  71.5 0.1 collective-permute-start.16
  71.5 1.2 %collective-permute-done.16 = f32[64,128]{1,0:T(8,128)S(1)} collective-permute-done((f32[64,128]{1,0:T(8,128)S(1)}, f32[64,128]{1,0:T(8,128)S(1)}, u32[]{:S(2)}, u32[]{:S(2)}) %collective-permute-start.16) | collective-permute-done | bytes 32800 | tf_op jit(solution)/shard_map/ppermute | solution.py:265
  72.7 2.7 %collective-permute-start.18 = (f32[64,128]{1,0:T(8,128)S(1)}, f32[64,128]{1,0:T(8,128)S(1)}, u32[]{:S(2)}, u32[]{:S(2)}) collective-permute-start(f32[64,128]{1,0:T(8,128)S(1)} %add.23), channel_id=1, source_target_pairs={{0,4},{1,5},{2,6},{3,7},{4,0},{5,1},{6,2},{7,3},{8,12},{9,13},{10,... | collective-permute-start | bytes 98312 | tf_op jit(solution)/shard_map/ppermute | solution.py:265
  75.4 0.8 collective-permute-start.17
  76.2 1.3 %collective-permute-done.19 = f32[64,128]{1,0:T(8,128)S(1)} collective-permute-done((f32[64,128]{1,0:T(8,128)S(1)}, f32[64,128]{1,0:T(8,128)S(1)}, u32[]{:S(2)}, u32[]{:S(2)}) %collective-permute-start.19) | collective-permute-done | bytes 32800 | tf_op jit(solution)/shard_map/ppermute | solution.py:265
  77.5 0.1 collective-permute-done.18
  77.7 1.7 %collective-permute-done.17 = f32[64,128]{1,0:T(8,128)S(1)} collective-permute-done((f32[64,128]{1,0:T(8,128)S(1)}, f32[64,128]{1,0:T(8,128)S(1)}, u32[]{:S(2)}, u32[]{:S(2)}) %collective-permute-start.17) | collective-permute-done | bytes 32800 | tf_op jit(solution)/shard_map/ppermute | solution.py:265
  79.4 1.2 %collective-permute-start.20 = (f32[64,128]{1,0:T(8,128)S(1)}, f32[64,128]{1,0:T(8,128)S(1)}, u32[]{:S(2)}, u32[]{:S(2)}) collective-permute-start(f32[64,128]{1,0:T(8,128)S(1)} %add_add_fusion), channel_id=1, source_target_pairs={{0,8},{1,9},{2,10},{3,11},{4,12},{5,13},{6,14},{7,15},{8,0},{9,1},... | collective-permute-start | bytes 98312 | tf_op jit(solution)/shard_map/ppermute | solution.py:265
  80.6 3.7 %collective-permute-done.20 = f32[64,128]{1,0:T(8,128)S(1)} collective-permute-done((f32[64,128]{1,0:T(8,128)S(1)}, f32[64,128]{1,0:T(8,128)S(1)}, u32[]{:S(2)}, u32[]{:S(2)}) %collective-permute-start.20) | collective-permute-done | bytes 32800 | tf_op jit(solution)/shard_map/ppermute | solution.py:265
  84.3 0.7 fusion
  (14 shorter events, 0.0 us)
Async XLA Ops:
  1.3 1.0 %copy-start.1 = (f32[64,2048]{1,0:T(8,128)S(1)}, f32[64,2048]{1,0:T(8,128)}, u32[]{:S(2)}) copy-start(f32[64,2048]{1,0:T(8,128)} %vectors_ref.1) | copy-start | bytes 1572868
  2.4 10.5 %collective-permute-start = (f32[64,2048]{1,0:T(8,128)S(1)}, f32[64,2048]{1,0:T(8,128)S(1)}, u32[]{:S(2)}, u32[]{:S(2)}) collective-permute-start(f32[64,2048]{1,0:T(8,128)S(1)} %get-tuple-element.18.field_ref.start_ref), channel_id=1, source_target_pairs={{0,1},{1,0},{2,3},{3,2},{4,5},{5,4},{6,7},{7,6},{8,9},{9,8},{10,11... | collective-permute-start | bytes 1572872 | tf_op jit(solution)/shard_map/ppermute | solution.py:265
  2.9 24.3 %collective-permute-start.1 = (f32[64,2048]{1,0:T(8,128)S(1)}, f32[64,2048]{1,0:T(8,128)S(1)}, u32[]{:S(2)}, u32[]{:S(2)}) collective-permute-start(f32[64,2048]{1,0:T(8,128)S(1)} %get-tuple-element.18.field_ref.start_ref), channel_id=1, source_target_pairs={{0,12},{1,13},{2,14},{3,15},{4,4},{5,5},{6,6},{7,7},{8,8},{9,9},{1... | collective-permute-start | bytes 1572872 | tf_op jit(solution)/shard_map/ppermute | solution.py:248
  9.4 10.1 %collective-permute-start.3 = (f32[32,2048]{1,0:T(8,128)S(1)}, f32[32,2048]{1,0:T(8,128)S(1)}, u32[]{:S(2)}, u32[]{:S(2)}) collective-permute-start(f32[32,2048]{1,0:T(8,128)S(1)} %get-tuple-element.20), channel_id=1, source_target_pairs={{0,2},{1,3},{6,4},{7,5},{8,10},{9,11},{14,12},{15,13},{16,18},{17,... | collective-permute-start | bytes 786440 | tf_op jit(solution)/shard_map/ppermute | solution.py:328
  12.9 15.7 %collective-permute-start.5 = (f32[64,2048]{1,0:T(8,128)S(1)}, f32[64,2048]{1,0:T(8,128)S(1)}, u32[]{:S(2)}, u32[]{:S(2)}) collective-permute-start(f32[64,2048]{1,0:T(8,128)S(1)} %collective-permute-done.flipped_ref), channel_id=1, source_target_pairs={{0,1},{1,3},{2,0},{3,2},{4,5},{5,7},{6,4},{7,6},{8,9},{9,11},{10,8... | collective-permute-start | bytes 1572872 | tf_op jit(solution)/shard_map/ppermute | solution.py:262
  12.9 15.6 %collective-permute-start.2 = (f32[32,2048]{1,0:T(8,128)S(1)}, f32[32,2048]{1,0:T(8,128)S(1)}, u32[]{:S(2)}, u32[]{:S(2)}) collective-permute-start(f32[32,2048]{1,0:T(8,128)S(1)} %get-tuple-element.19), channel_id=1, source_target_pairs={{0,6},{1,7},{2,2},{3,3},{4,4},{5,5},{6,0},{7,1},{8,14},{9,15},{10,... | collective-permute-start | bytes 786440 | tf_op jit(solution)/shard_map/ppermute | solution.py:248
  19.5 9.1 %collective-permute-start.4 = (f32[32,2048]{1,0:T(8,128)S(1)}, f32[32,2048]{1,0:T(8,128)S(1)}, u32[]{:S(2)}, u32[]{:S(2)}) collective-permute-start(f32[32,2048]{1,0:T(8,128)S(1)} %collective-permute-done.3), channel_id=1, source_target_pairs={{2,6},{3,7},{4,0},{5,1},{10,14},{11,15},{12,8},{13,9},{18,22},{19,... | collective-permute-start | bytes 786440 | tf_op jit(solution)/shard_map/ppermute | solution.py:328
  21.6 0.7 copy-start.2
  22.3 22.9 %copy-start = (f32[64,128,128]{2,1,0:T(8,128)S(1)}, f32[64,128,128]{2,1,0:T(8,128)}, u32[]{:S(2)}) copy-start(f32[64,128,128]{2,1,0:T(8,128)} %param.7) | copy-start | bytes 12582916
  29.3 8.0 %collective-permute-start.6 = (f32[64,2048]{1,0:T(8,128)S(1)}, f32[64,2048]{1,0:T(8,128)S(1)}, u32[]{:S(2)}, u32[]{:S(2)}) collective-permute-start(f32[64,2048]{1,0:T(8,128)S(1)} %get-tuple-element.21.field_ref), channel_id=1, source_target_pairs={{0,1},{1,0},{2,3},{3,2},{4,5},{5,4},{6,7},{7,6},{8,9},{9,8},{10,11... | collective-permute-start | bytes 1572872 | tf_op jit(solution)/shard_map/ppermute | solution.py:265
  29.3 19.5 %collective-permute-start.7 = (f32[64,2048]{1,0:T(8,128)S(1)}, f32[64,2048]{1,0:T(8,128)S(1)}, u32[]{:S(2)}, u32[]{:S(2)}) collective-permute-start(f32[64,2048]{1,0:T(8,128)S(1)} %get-tuple-element.21.field_ref), channel_id=1, source_target_pairs={{0,12},{1,13},{2,14},{3,15},{4,4},{5,5},{6,6},{7,7},{8,8},{9,9},{1... | collective-permute-start | bytes 1572872 | tf_op jit(solution)/shard_map/ppermute | solution.py:248
  31.3 12.6 %collective-permute-start.9 = (f32[32,2048]{1,0:T(8,128)S(1)}, f32[32,2048]{1,0:T(8,128)S(1)}, u32[]{:S(2)}, u32[]{:S(2)}) collective-permute-start(f32[32,2048]{1,0:T(8,128)S(1)} %get-tuple-element.23), channel_id=1, source_target_pairs={{0,2},{1,3},{6,4},{7,5},{8,10},{9,11},{14,12},{15,13},{16,18},{17,... | collective-permute-start | bytes 786440 | tf_op jit(solution)/shard_map/ppermute | solution.py:328
  37.3 17.0 %collective-permute-start.11 = (f32[64,2048]{1,0:T(8,128)S(1)}, f32[64,2048]{1,0:T(8,128)S(1)}, u32[]{:S(2)}, u32[]{:S(2)}) collective-permute-start(f32[64,2048]{1,0:T(8,128)S(1)} %collective-permute-done.6.flipped_ref), channel_id=1, source_target_pairs={{0,1},{1,3},{2,0},{3,2},{4,5},{5,7},{6,4},{7,6},{8,9},{9,11},{10,8... | collective-permute-start | bytes 1572872 | tf_op jit(solution)/shard_map/ppermute | solution.py:262
  37.3 16.9 %collective-permute-start.8 = (f32[32,2048]{1,0:T(8,128)S(1)}, f32[32,2048]{1,0:T(8,128)S(1)}, u32[]{:S(2)}, u32[]{:S(2)}) collective-permute-start(f32[32,2048]{1,0:T(8,128)S(1)} %get-tuple-element.22), channel_id=1, source_target_pairs={{0,6},{1,7},{2,2},{3,3},{4,4},{5,5},{6,0},{7,1},{8,14},{9,15},{10,... | collective-permute-start | bytes 786440 | tf_op jit(solution)/shard_map/ppermute | solution.py:248
  43.9 10.4 %collective-permute-start.10 = (f32[32,2048]{1,0:T(8,128)S(1)}, f32[32,2048]{1,0:T(8,128)S(1)}, u32[]{:S(2)}, u32[]{:S(2)}) collective-permute-start(f32[32,2048]{1,0:T(8,128)S(1)} %collective-permute-done.9), channel_id=1, source_target_pairs={{2,6},{3,7},{4,0},{5,1},{10,14},{11,15},{12,8},{13,9},{18,22},{19,... | collective-permute-start | bytes 786440 | tf_op jit(solution)/shard_map/ppermute | solution.py:328
  55.0 2.0 %collective-permute-start.12 = (f32[64,2048]{1,0:T(8,128)S(1)}, f32[64,2048]{1,0:T(8,128)S(1)}, u32[]{:S(2)}, u32[]{:S(2)}) collective-permute-start(f32[64,2048]{1,0:T(8,128)S(1)} %get-tuple-element.24.field_ref), channel_id=1, source_target_pairs={{0,1},{1,0},{2,3},{3,2},{4,5},{5,4},{6,7},{7,6},{8,9},{9,8},{10,11... | collective-permute-start | bytes 1572872 | tf_op jit(solution)/shard_map/ppermute | solution.py:265
  55.1 15.2 %collective-permute-start.13 = (f32[64,1536]{1,0:T(8,128)S(1)}, f32[64,1536]{1,0:T(8,128)S(1)}, u32[]{:S(2)}, u32[]{:S(2)}) collective-permute-start(f32[64,1536]{1,0:T(8,128)S(1)} %get-tuple-element.30), channel_id=1, source_target_pairs={{0,3},{2,14},{3,15},{7,4},{8,11},{12,0},{13,1},{15,12},{16,19},{18... | collective-permute-start | bytes 1179656 | tf_op jit(solution)/shard_map/ppermute | solution.py:258
  57.0 13.3 %collective-permute-start.15 = (f32[64,1024]{1,0:T(8,128)S(1)}, f32[64,1024]{1,0:T(8,128)S(1)}, u32[]{:S(2)}, u32[]{:S(2)}) collective-permute-start(f32[64,1024]{1,0:T(8,128)S(1)} %get-tuple-element.32), channel_id=1, source_target_pairs={{0,6},{1,7},{2,2},{3,3},{4,4},{5,5},{6,0},{7,1},{8,14},{9,15},{10,... | collective-permute-start | bytes 786440 | tf_op jit(solution)/shard_map/ppermute | solution.py:248
  59.3 11.0 %collective-permute-start.14 = (f32[64,512]{1,0:T(8,128)S(1)}, f32[64,512]{1,0:T(8,128)S(1)}, u32[]{:S(2)}, u32[]{:S(2)}) collective-permute-start(f32[64,512]{1,0:T(8,128)S(1)} %get-tuple-element.31), channel_id=1, source_target_pairs={{0,12},{1,13},{3,0},{4,7},{11,8},{12,15},{14,2},{15,3},{16,28},{17... | collective-permute-start | bytes 393224 | tf_op jit(solution)/shard_map/ppermute | solution.py:258
  71.5 1.3 %collective-permute-start.16 = (f32[64,128]{1,0:T(8,128)S(1)}, f32[64,128]{1,0:T(8,128)S(1)}, u32[]{:S(2)}, u32[]{:S(2)}) collective-permute-start(f32[64,128]{1,0:T(8,128)S(1)} %crossed.1), channel_id=1, source_target_pairs={{0,1},{1,0},{2,3},{3,2},{4,5},{5,4},{6,7},{7,6},{8,9},{9,8},{10,11... | collective-permute-start | bytes 98312 | tf_op jit(solution)/shard_map/ppermute | solution.py:265
  72.7 4.8 %collective-permute-start.19 = (f32[64,128]{1,0:T(8,128)S(1)}, f32[64,128]{1,0:T(8,128)S(1)}, u32[]{:S(2)}, u32[]{:S(2)}) collective-permute-start(f32[64,128]{1,0:T(8,128)S(1)} %add.23), channel_id=1, source_target_pairs={{0,6},{1,7},{2,4},{3,5},{4,2},{5,3},{6,0},{7,1},{8,14},{9,15},{10,... | collective-permute-start | bytes 98312 | tf_op jit(solution)/shard_map/ppermute | solution.py:265
  72.7 4.9 %collective-permute-start.18 = (f32[64,128]{1,0:T(8,128)S(1)}, f32[64,128]{1,0:T(8,128)S(1)}, u32[]{:S(2)}, u32[]{:S(2)}) collective-permute-start(f32[64,128]{1,0:T(8,128)S(1)} %add.23), channel_id=1, source_target_pairs={{0,4},{1,5},{2,6},{3,7},{4,0},{5,1},{6,2},{7,3},{8,12},{9,13},{10,... | collective-permute-start | bytes 98312 | tf_op jit(solution)/shard_map/ppermute | solution.py:265
  75.4 3.9 %collective-permute-start.17 = (f32[64,128]{1,0:T(8,128)S(1)}, f32[64,128]{1,0:T(8,128)S(1)}, u32[]{:S(2)}, u32[]{:S(2)}) collective-permute-start(f32[64,128]{1,0:T(8,128)S(1)} %add.23), channel_id=1, source_target_pairs={{0,2},{1,3},{2,0},{3,1},{4,6},{5,7},{6,4},{7,5},{8,10},{9,11},{10,... | collective-permute-start | bytes 98312 | tf_op jit(solution)/shard_map/ppermute | solution.py:265
  79.4 4.9 %collective-permute-start.20 = (f32[64,128]{1,0:T(8,128)S(1)}, f32[64,128]{1,0:T(8,128)S(1)}, u32[]{:S(2)}, u32[]{:S(2)}) collective-permute-start(f32[64,128]{1,0:T(8,128)S(1)} %add_add_fusion), channel_id=1, source_target_pairs={{0,8},{1,9},{2,10},{3,11},{4,12},{5,13},{6,14},{7,15},{8,0},{9,1},... | collective-permute-start | bytes 98312 | tf_op jit(solution)/shard_map/ppermute | solution.py:265

commit v4 on v3

--- a/solution.py
+++ b/solution.py
@@ -16,7 +16,7 @@
 F32, BF16 = jnp.float32, jnp.bfloat16
 SMEM = pl.BlockSpec(memory_space=pltpu.SMEM)
 LIMIT = 32 * 1024 * 1024
-FIRST_LIMIT = 50 * 1024 * 1024
+FIRST_LIMIT = 47 * 1024 * 1024
 
 
 class Part:
@@ -98,7 +98,7 @@
 
 
 def first_own_kernel(
-    field_count, table_ref, field_ref, flipped_ref, far_tiles, map_ref, out_ref, split_ref, tiles_ref, sems
+    field_count, table_ref, field_ref, flipped_ref, far_tiles, map_ref, out_ref, tiles_ref, split_ref, sems
 ):
     place_ref, cols_ref, fields_ref = parts_of(table_ref, field_count)
     blocks = tiles_ref.shape[0] // STEPS
@@ -281,12 +281,11 @@
     def first_own_part(field, flipped):
         return pl.pallas_call(
             functools.partial(first_own_kernel, bonds + 1),
-            out_shape=full,
+            out_shape=[full, jax.ShapeDtypeStruct(tiles.shape, F32)],
             in_specs=[SMEM] + [inside] * 2 + [pl.BlockSpec(memory_space=pl.ANY), inside],
-            out_specs=inside,
+            out_specs=[inside, inside],
             scratch_shapes=[
                 split,
-                pltpu.VMEM(tiles.shape, F32),
                 pltpu.SemaphoreType.DMA((STEPS,)),
             ],
             compiler_params=pltpu.CompilerParams(vmem_limit_bytes=FIRST_LIMIT),
@@ -294,7 +293,7 @@
             name="first_own",
         )(table, field, flipped, tiles, targets)
 
-    def own_part(field, flipped):
+    def own_part(field, flipped, tiles):
         return pl.pallas_call(
             functools.partial(own_kernel, bonds + 1),
             out_shape=full,
@@ -306,7 +305,7 @@
             name="own",
         )(table, field, flipped, tiles, targets)
 
-    def own_gram(field, flipped):
+    def own_gram(field, flipped, tiles):
         return pl.pallas_call(
             functools.partial(own_gram_kernel, bonds + 1),
             out_shape=[gram_shape, full],
@@ -320,7 +319,7 @@
 
     three = [full, rows_by(vec_count // 2, row_count), rows_by(vec_count // 2, row_count)]
 
-    def apply(own, field, first_half, second_half):
+    def apply(own_of, field, first_half, second_half):
         legs = [(here, here ^ 2) for here in range(dev_count) if coupled(here, 1)]
         round_way = [(here, here ^ 4) for here in range(dev_count) if not coupled(here, 1)]
         flipped = exchange(field, 1)
@@ -328,6 +327,7 @@
         aside = lax.ppermute(lax.ppermute(second_half, AXES, legs), AXES, round_way)
         direct = hop(first_half, 1)
         closest = near(flipped)
+        own, *kept_tiles = own_of(field, flipped)
         total = pl.pallas_call(
             functools.partial(far_kernel, bonds),
             out_shape=full,
@@ -337,8 +337,8 @@
             compiler_params=params,
             cost_estimate=pl.CostEstimate(flops=vec_count * row_count, bytes_accessed=12 * vec_count * row_count, transcendentals=0),
             name="far",
-        )(table, own(field, flipped), *far)
-        return total, [direct, aside, closest]
+        )(table, own, *far)
+        return total, [direct, aside, closest], kept_tiles
 
     start, *halves_of = pl.pallas_call(
         start_kernel,
@@ -348,7 +348,7 @@
         compiler_params=params,
         name="start",
     )(live_rows, vectors)
-    own, hops = apply(first_own_part, start, *halves_of)
+    own, hops, (close_tiles,) = apply(first_own_part, start, *halves_of)
     first, *halves_of = pl.pallas_call(
         combine_kernel,
         out_shape=three,
@@ -357,7 +357,7 @@
         compiler_params=params,
         name="combine",
     )(table, live_rows, own, *hops)
-    own, hops = apply(own_part, first, *halves_of)
+    own, hops, _ = apply(lambda *arrays: (own_part(*arrays, close_tiles),), first, *halves_of)
     cut = row_count * 3 // 4
     kept, sent, lead, rest = pl.pallas_call(
         filter_kernel,
@@ -372,7 +372,7 @@
     flipped, sent, rest = lax.optimization_barrier((flipped, sent, rest))
     hops += [one_way(rest, bond, 0) for bond in reversed(range(2, bonds))]
     hops += [hop(sent, 1)]
-    grams, second = own_gram(kept, flipped)
+    grams, second = own_gram(kept, flipped, close_tiles)
     sums = pl.pallas_call(
         functools.partial(crossed_kernel, bonds, dev_count * row_count),
         out_shape=gram_shape,

time: 85.5 us -> 85.5 us (level)
    unnamed x6 -> x4, local copies, waits for them, and re-layouts: 1.74 us -> 1.73 us
where the time goes in v4:
time: 85.5 us; the launch traced here: 85 us
  starting transfers between devices  38.1 us (45%)
  waiting for transfers between devices  24.1 us (28%)
  Pallas kernels  18 us (21%)
  local copies, waits for them, and re-layouts  2.43 us (3%)
  between operations  1.52 us (2%)
    ppermute x5, starting transfers between devices, hop(): return lax.ppermute(value, AXES, pairs)  14.8 us
    ppermute x4, starting transfers between devices, apply(): aside = lax.ppermute(lax.ppermute(second_half, AXES, legs), AXES, round_way)  12 us
    ppermute x4, waiting for transfers between devices, apply(): aside = lax.ppermute(lax.ppermute(second_half, AXES, legs), AXES, round_way)  9.33 us
    ppermute x8, waiting for transfers between devices, exchange(): lax.ppermute(value, AXES, [(source, source ^ mask) for source in range(de...  8.19 us
    ppermute x2, starting transfers between devices, one_way(): return lax.ppermute(value, AXES, pairs)  5.82 us
    pallas_call x1, Pallas kernels, own_gram(): pl.pallas_call(functools.partial(own_gram_kernel, bonds + 1), out_shape=[...  5.68 us
    ppermute x8, starting transfers between devices, exchange(): lax.ppermute(value, AXES, [(source, source ^ mask) for source in range(de...  5.51 us
    ppermute x5, waiting for transfers between devices, hop(): return lax.ppermute(value, AXES, pairs)  5.44 us
  transfers between devices with their start and end apart: 21, of which 10 were waited for; matrix products, arithmetic and copies ran while one was open for 1% of the time, Pallas kernels for 18%

profile of v4, /device:TPU:0, one launch (start us, length us, event | category | flops | bytes accessed | tf_op | source)
XLA Modules:
  0.0 85.0 jit_solution(16409904014361166838)
XLA Ops:
  1.3 1.0 %copy-done = f32[64,2048]{1,0:T(8,128)S(1)} copy-done((f32[64,2048]{1,0:T(8,128)S(1)}, f32[64,2048]{1,0:T(8,128)}, u32[]{:S(2)}) %copy-start) | copy-done | bytes 524312
  2.3 0.1 start.1
  2.4 0.5 collective-permute-start
  2.9 6.5 %collective-permute-start.1 = (f32[64,2048]{1,0:T(8,128)S(1)}, f32[64,2048]{1,0:T(8,128)S(1)}, u32[]{:S(2)}, u32[]{:S(2)}) collective-permute-start(f32[64,2048]{1,0:T(8,128)S(1)} %get-tuple-element.20.field_ref.start_ref), channel_id=1, source_target_pairs={{0,12},{1,13},{2,14},{3,15},{4,4},{5,5},{6,6},{7,7},{8,8},{9,9},{1... | collective-permute-start | bytes 1572872 | tf_op jit(solution)/shard_map/ppermute | solution.py:248
  9.4 3.4 %collective-permute-start.3 = (f32[32,2048]{1,0:T(8,128)S(1)}, f32[32,2048]{1,0:T(8,128)S(1)}, u32[]{:S(2)}, u32[]{:S(2)}) collective-permute-start(f32[32,2048]{1,0:T(8,128)S(1)} %get-tuple-element.23), channel_id=1, source_target_pairs={{0,2},{1,3},{6,4},{7,5},{8,10},{9,11},{14,12},{15,13},{16,18},{17,... | collective-permute-start | bytes 786440 | tf_op jit(solution)/shard_map/ppermute | solution.py:327
  12.9 0.0 collective-permute-start.5
  12.9 1.9 %collective-permute-start.2 = (f32[32,2048]{1,0:T(8,128)S(1)}, f32[32,2048]{1,0:T(8,128)S(1)}, u32[]{:S(2)}, u32[]{:S(2)}) collective-permute-start(f32[32,2048]{1,0:T(8,128)S(1)} %get-tuple-element.22), channel_id=1, source_target_pairs={{0,6},{1,7},{2,2},{3,3},{4,4},{5,5},{6,0},{7,1},{8,14},{9,15},{10,... | collective-permute-start | bytes 786440 | tf_op jit(solution)/shard_map/ppermute | solution.py:248
  14.9 4.7 %collective-permute-done.3 = f32[32,2048]{1,0:T(8,128)S(1)} collective-permute-done((f32[32,2048]{1,0:T(8,128)S(1)}, f32[32,2048]{1,0:T(8,128)S(1)}, u32[]{:S(2)}, u32[]{:S(2)}) %collective-permute-start.3) | collective-permute-done | bytes 262176 | tf_op jit(solution)/shard_map/ppermute | solution.py:327
  19.5 1.3 %collective-permute-start.4 = (f32[32,2048]{1,0:T(8,128)S(1)}, f32[32,2048]{1,0:T(8,128)S(1)}, u32[]{:S(2)}, u32[]{:S(2)}) collective-permute-start(f32[32,2048]{1,0:T(8,128)S(1)} %collective-permute-done.3), channel_id=1, source_target_pairs={{2,6},{3,7},{4,0},{5,1},{10,14},{11,15},{12,8},{13,9},{18,22},{19,... | collective-permute-start | bytes 786440 | tf_op jit(solution)/shard_map/ppermute | solution.py:327
  20.8 0.8 pad_add_fusion.table_ref.place_ref
  21.6 0.7 copy-done.1
  22.3 4.8 %first_own.1 = (f32[64,2048]{1,0:T(8,128)S(1)}, f32[16,4,128,128]{3,2,1,0:T(8,128)S(1)}) custom-call(s32[70]{0:T(128)S(1)} %pad_add_fusion.table_ref.place_ref, f32[64,2048]{1,0:T(8,128)S(1)} %get-tuple-element.20.field_ref.start_ref, f32[64,2048]{1,0:T(8,128)S(1)} %collective-permute-done.flipped_ref, f32[16,4,128,128]{3,2,1,0:T(8,128)} %bitcast.7, ...), custom_call_target="tpu_custom_call" | custom-call | flops 536870912 | bytes 5767168 | tf_op jit(solution)/shard_map/first_own/pallas_call | solution.py:282
  27.1 0.6 far.2.own_ref
  27.7 0.9 %collective-permute-done.2.refs_0_ = f32[32,2048]{1,0:T(8,128)S(1)} collective-permute-done((f32[32,2048]{1,0:T(8,128)S(1)}, f32[32,2048]{1,0:T(8,128)S(1)}, u32[]{:S(2)}, u32[]{:S(2)}) %collective-permute-start.2) | collective-permute-done | bytes 262176 | tf_op jit(solution)/shard_map/ppermute | solution.py:248
  28.6 0.0 collective-permute-done.4.refs_1_
  28.6 0.0 collective-permute-done.5.refs_2_
  28.6 0.7 combine.1
  29.3 0.1 collective-permute-start.6
  29.3 1.9 %collective-permute-start.7 = (f32[64,2048]{1,0:T(8,128)S(1)}, f32[64,2048]{1,0:T(8,128)S(1)}, u32[]{:S(2)}, u32[]{:S(2)}) collective-permute-start(f32[64,2048]{1,0:T(8,128)S(1)} %get-tuple-element.24.field_ref), channel_id=1, source_target_pairs={{0,12},{1,13},{2,14},{3,15},{4,4},{5,5},{6,6},{7,7},{8,8},{9,9},{1... | collective-permute-start | bytes 1572872 | tf_op jit(solution)/shard_map/ppermute | solution.py:248
  31.3 6.0 %collective-permute-start.9 = (f32[32,2048]{1,0:T(8,128)S(1)}, f32[32,2048]{1,0:T(8,128)S(1)}, u32[]{:S(2)}, u32[]{:S(2)}) collective-permute-start(f32[32,2048]{1,0:T(8,128)S(1)} %get-tuple-element.27), channel_id=1, source_target_pairs={{0,2},{1,3},{6,4},{7,5},{8,10},{9,11},{14,12},{15,13},{16,18},{17,... | collective-permute-start | bytes 786440 | tf_op jit(solution)/shard_map/ppermute | solution.py:327
  37.3 0.0 collective-permute-done.6.flipped_ref
  37.3 0.0 collective-permute-start.11
  37.3 1.9 %collective-permute-start.8 = (f32[32,2048]{1,0:T(8,128)S(1)}, f32[32,2048]{1,0:T(8,128)S(1)}, u32[]{:S(2)}, u32[]{:S(2)}) collective-permute-start(f32[32,2048]{1,0:T(8,128)S(1)} %get-tuple-element.26), channel_id=1, source_target_pairs={{0,6},{1,7},{2,2},{3,3},{4,4},{5,5},{6,0},{7,1},{8,14},{9,15},{10,... | collective-permute-start | bytes 786440 | tf_op jit(solution)/shard_map/ppermute | solution.py:248
  39.2 4.7 %collective-permute-done.9 = f32[32,2048]{1,0:T(8,128)S(1)} collective-permute-done((f32[32,2048]{1,0:T(8,128)S(1)}, f32[32,2048]{1,0:T(8,128)S(1)}, u32[]{:S(2)}, u32[]{:S(2)}) %collective-permute-start.9) | collective-permute-done | bytes 262176 | tf_op jit(solution)/shard_map/ppermute | solution.py:327
  43.9 1.3 %collective-permute-start.10 = (f32[32,2048]{1,0:T(8,128)S(1)}, f32[32,2048]{1,0:T(8,128)S(1)}, u32[]{:S(2)}, u32[]{:S(2)}) collective-permute-start(f32[32,2048]{1,0:T(8,128)S(1)} %collective-permute-done.9), channel_id=1, source_target_pairs={{2,6},{3,7},{4,0},{5,1},{10,14},{11,15},{12,8},{13,9},{18,22},{19,... | collective-permute-start | bytes 786440 | tf_op jit(solution)/shard_map/ppermute | solution.py:327
  45.2 3.6 %own.1.own_ref = f32[64,2048]{1,0:T(8,128)S(1)} custom-call(s32[70]{0:T(128)S(1)} %pad_add_fusion.table_ref.place_ref, f32[64,2048]{1,0:T(8,128)S(1)} %get-tuple-element.24.field_ref, f32[64,2048]{1,0:T(8,128)S(1)} %collective-permute-done.6.flipped_ref, f32[16,4,128,128]{3,2,1,0:T(8,128)S(1)} %get-tuple-element.25.tiles_ref, s32[1,2048]{1,0:T(1,128)S(1)} %bitcast.5), custom_call_target="tpu_custom_call" | custom-call | flops 536870912 | bytes 5767168 | tf_op jit(solution)/shard_map/own/pallas_call | solution.py:297
  48.9 0.6 far.3.own_ref
  49.5 4.5 %collective-permute-done.8.refs_0_ = f32[32,2048]{1,0:T(8,128)S(1)} collective-permute-done((f32[32,2048]{1,0:T(8,128)S(1)}, f32[32,2048]{1,0:T(8,128)S(1)}, u32[]{:S(2)}, u32[]{:S(2)}) %collective-permute-start.8) | collective-permute-done | bytes 262176 | tf_op jit(solution)/shard_map/ppermute | solution.py:248
  54.1 0.0 collective-permute-done.10.refs_1_
  54.1 0.8 filter.1
  54.8 0.1 collective-permute-start.12
  54.9 1.9 %collective-permute-start.13 = (f32[64,1536]{1,0:T(8,128)S(1)}, f32[64,1536]{1,0:T(8,128)S(1)}, u32[]{:S(2)}, u32[]{:S(2)}) collective-permute-start(f32[64,1536]{1,0:T(8,128)S(1)} %get-tuple-element.34), channel_id=1, source_target_pairs={{0,3},{2,14},{3,15},{7,4},{8,11},{12,0},{13,1},{15,12},{16,19},{18... | collective-permute-start | bytes 1179656 | tf_op jit(solution)/shard_map/ppermute | solution.py:258
  56.8 0.0 collective-permute-done.12.flipped_ref
  56.8 2.5 %collective-permute-start.15 = (f32[64,1024]{1,0:T(8,128)S(1)}, f32[64,1024]{1,0:T(8,128)S(1)}, u32[]{:S(2)}, u32[]{:S(2)}) collective-permute-start(f32[64,1024]{1,0:T(8,128)S(1)} %get-tuple-element.36), channel_id=1, source_target_pairs={{0,6},{1,7},{2,2},{3,3},{4,4},{5,5},{6,0},{7,1},{8,14},{9,15},{10,... | collective-permute-start | bytes 786440 | tf_op jit(solution)/shard_map/ppermute | solution.py:248
  59.3 3.9 %collective-permute-start.14 = (f32[64,512]{1,0:T(8,128)S(1)}, f32[64,512]{1,0:T(8,128)S(1)}, u32[]{:S(2)}, u32[]{:S(2)}) collective-permute-start(f32[64,512]{1,0:T(8,128)S(1)} %get-tuple-element.35), channel_id=1, source_target_pairs={{0,12},{1,13},{3,0},{4,7},{11,8},{12,15},{14,2},{15,3},{16,28},{17... | collective-permute-start | bytes 393224 | tf_op jit(solution)/shard_map/ppermute | solution.py:258
  63.3 5.7 %own_gram.1 = (f32[64,128]{1,0:T(8,128)S(1)}, f32[64,2048]{1,0:T(8,128)}) custom-call(s32[70]{0:T(128)S(1)} %pad_add_fusion.table_ref.place_ref, s32[1]{0:T(128)S(6)} %copy.13.live_ref, f32[64,2048]{1,0:T(8,128)S(1)} %get-tuple-element.28.field_ref, f32[64,2048]{1,0:T(8,128)S(1)} %collective-permute-done.12.flipped_ref, ...), custom_call_target="tpu_custom_call" | custom-call | flops 536870912 | bytes 5767168 | tf_op jit(solution)/shard_map/own_gram/pallas_call | solution.py:309
  68.9 1.2 %collective-permute-done.13.refs_0_ = f32[64,1536]{1,0:T(8,128)S(1)} collective-permute-done((f32[64,1536]{1,0:T(8,128)S(1)}, f32[64,1536]{1,0:T(8,128)S(1)}, u32[]{:S(2)}, u32[]{:S(2)}) %collective-permute-start.13) | collective-permute-done | bytes 393248 | tf_op jit(solution)/shard_map/ppermute | solution.py:258
  70.1 1.1 %crossed.1 = f32[64,128]{1,0:T(8,128)S(1)} custom-call(s32[70]{0:T(128)S(1)} %pad_add_fusion.table_ref.place_ref, f32[64,128]{1,0:T(8,128)S(1)} %get-tuple-element.33.own_ref, f32[64,2048]{1,0:T(8,128)S(1)} %get-tuple-element.28.field_ref, f32[64,1536]{1,0:T(8,128)S(1)} %collective-permute-done.13.refs_0_, f32[64,512]{1,0:T(8,128)S(1)} %collective-permute-done.14.refs_1_, ...), custom_call_target="tpu_custom_call" | custom-call | tf_op jit(solution)/shard_map/crossed/pallas_call | solution.py:376
  71.3 0.1 collective-permute-start.16
  71.3 1.2 %collective-permute-done.16 = f32[64,128]{1,0:T(8,128)S(1)} collective-permute-done((f32[64,128]{1,0:T(8,128)S(1)}, f32[64,128]{1,0:T(8,128)S(1)}, u32[]{:S(2)}, u32[]{:S(2)}) %collective-permute-start.16) | collective-permute-done | bytes 32800 | tf_op jit(solution)/shard_map/ppermute | solution.py:265
  72.5 2.9 %collective-permute-start.18 = (f32[64,128]{1,0:T(8,128)S(1)}, f32[64,128]{1,0:T(8,128)S(1)}, u32[]{:S(2)}, u32[]{:S(2)}) collective-permute-start(f32[64,128]{1,0:T(8,128)S(1)} %add.23), channel_id=1, source_target_pairs={{0,4},{1,5},{2,6},{3,7},{4,0},{5,1},{6,2},{7,3},{8,12},{9,13},{10,... | collective-permute-start | bytes 98312 | tf_op jit(solution)/shard_map/ppermute | solution.py:265
  75.4 0.6 collective-permute-start.17
  76.0 1.3 %collective-permute-done.19 = f32[64,128]{1,0:T(8,128)S(1)} collective-permute-done((f32[64,128]{1,0:T(8,128)S(1)}, f32[64,128]{1,0:T(8,128)S(1)}, u32[]{:S(2)}, u32[]{:S(2)}) %collective-permute-start.19) | collective-permute-done | bytes 32800 | tf_op jit(solution)/shard_map/ppermute | solution.py:265
  77.4 0.3 collective-permute-done.18
  77.6 1.7 %collective-permute-done.17 = f32[64,128]{1,0:T(8,128)S(1)} collective-permute-done((f32[64,128]{1,0:T(8,128)S(1)}, f32[64,128]{1,0:T(8,128)S(1)}, u32[]{:S(2)}, u32[]{:S(2)}) %collective-permute-start.17) | collective-permute-done | bytes 32800 | tf_op jit(solution)/shard_map/ppermute | solution.py:265
  79.3 1.3 %collective-permute-start.20 = (f32[64,128]{1,0:T(8,128)S(1)}, f32[64,128]{1,0:T(8,128)S(1)}, u32[]{:S(2)}, u32[]{:S(2)}) collective-permute-start(f32[64,128]{1,0:T(8,128)S(1)} %add_add_fusion), channel_id=1, source_target_pairs={{0,8},{1,9},{2,10},{3,11},{4,12},{5,13},{6,14},{7,15},{8,0},{9,1},... | collective-permute-start | bytes 98312 | tf_op jit(solution)/shard_map/ppermute | solution.py:265
  80.6 3.7 %collective-permute-done.20 = f32[64,128]{1,0:T(8,128)S(1)} collective-permute-done((f32[64,128]{1,0:T(8,128)S(1)}, f32[64,128]{1,0:T(8,128)S(1)}, u32[]{:S(2)}, u32[]{:S(2)}) %collective-permute-start.20) | collective-permute-done | bytes 32800 | tf_op jit(solution)/shard_map/ppermute | solution.py:265
  84.3 0.7 fusion
  (12 shorter events, 0.0 us)
Async XLA Ops:
  1.3 1.0 %copy-start = (f32[64,2048]{1,0:T(8,128)S(1)}, f32[64,2048]{1,0:T(8,128)}, u32[]{:S(2)}) copy-start(f32[64,2048]{1,0:T(8,128)} %vectors_ref.1) | copy-start | bytes 1572868
  2.4 10.5 %collective-permute-start = (f32[64,2048]{1,0:T(8,128)S(1)}, f32[64,2048]{1,0:T(8,128)S(1)}, u32[]{:S(2)}, u32[]{:S(2)}) collective-permute-start(f32[64,2048]{1,0:T(8,128)S(1)} %get-tuple-element.20.field_ref.start_ref), channel_id=1, source_target_pairs={{0,1},{1,0},{2,3},{3,2},{4,5},{5,4},{6,7},{7,6},{8,9},{9,8},{10,11... | collective-permute-start | bytes 1572872 | tf_op jit(solution)/shard_map/ppermute | solution.py:265
  2.9 24.1 %collective-permute-start.1 = (f32[64,2048]{1,0:T(8,128)S(1)}, f32[64,2048]{1,0:T(8,128)S(1)}, u32[]{:S(2)}, u32[]{:S(2)}) collective-permute-start(f32[64,2048]{1,0:T(8,128)S(1)} %get-tuple-element.20.field_ref.start_ref), channel_id=1, source_target_pairs={{0,12},{1,13},{2,14},{3,15},{4,4},{5,5},{6,6},{7,7},{8,8},{9,9},{1... | collective-permute-start | bytes 1572872 | tf_op jit(solution)/shard_map/ppermute | solution.py:248
  9.4 10.1 %collective-permute-start.3 = (f32[32,2048]{1,0:T(8,128)S(1)}, f32[32,2048]{1,0:T(8,128)S(1)}, u32[]{:S(2)}, u32[]{:S(2)}) collective-permute-start(f32[32,2048]{1,0:T(8,128)S(1)} %get-tuple-element.23), channel_id=1, source_target_pairs={{0,2},{1,3},{6,4},{7,5},{8,10},{9,11},{14,12},{15,13},{16,18},{17,... | collective-permute-start | bytes 786440 | tf_op jit(solution)/shard_map/ppermute | solution.py:327
  12.9 15.7 %collective-permute-start.5 = (f32[64,2048]{1,0:T(8,128)S(1)}, f32[64,2048]{1,0:T(8,128)S(1)}, u32[]{:S(2)}, u32[]{:S(2)}) collective-permute-start(f32[64,2048]{1,0:T(8,128)S(1)} %collective-permute-done.flipped_ref), channel_id=1, source_target_pairs={{0,1},{1,3},{2,0},{3,2},{4,5},{5,7},{6,4},{7,6},{8,9},{9,11},{10,8... | collective-permute-start | bytes 1572872 | tf_op jit(solution)/shard_map/ppermute | solution.py:262
  12.9 15.6 %collective-permute-start.2 = (f32[32,2048]{1,0:T(8,128)S(1)}, f32[32,2048]{1,0:T(8,128)S(1)}, u32[]{:S(2)}, u32[]{:S(2)}) collective-permute-start(f32[32,2048]{1,0:T(8,128)S(1)} %get-tuple-element.22), channel_id=1, source_target_pairs={{0,6},{1,7},{2,2},{3,3},{4,4},{5,5},{6,0},{7,1},{8,14},{9,15},{10,... | collective-permute-start | bytes 786440 | tf_op jit(solution)/shard_map/ppermute | solution.py:248
  19.5 9.1 %collective-permute-start.4 = (f32[32,2048]{1,0:T(8,128)S(1)}, f32[32,2048]{1,0:T(8,128)S(1)}, u32[]{:S(2)}, u32[]{:S(2)}) collective-permute-start(f32[32,2048]{1,0:T(8,128)S(1)} %collective-permute-done.3), channel_id=1, source_target_pairs={{2,6},{3,7},{4,0},{5,1},{10,14},{11,15},{12,8},{13,9},{18,22},{19,... | collective-permute-start | bytes 786440 | tf_op jit(solution)/shard_map/ppermute | solution.py:327
  21.6 0.7 copy-start.1
  29.3 8.0 %collective-permute-start.6 = (f32[64,2048]{1,0:T(8,128)S(1)}, f32[64,2048]{1,0:T(8,128)S(1)}, u32[]{:S(2)}, u32[]{:S(2)}) collective-permute-start(f32[64,2048]{1,0:T(8,128)S(1)} %get-tuple-element.24.field_ref), channel_id=1, source_target_pairs={{0,1},{1,0},{2,3},{3,2},{4,5},{5,4},{6,7},{7,6},{8,9},{9,8},{10,11... | collective-permute-start | bytes 1572872 | tf_op jit(solution)/shard_map/ppermute | solution.py:265
  29.3 19.5 %collective-permute-start.7 = (f32[64,2048]{1,0:T(8,128)S(1)}, f32[64,2048]{1,0:T(8,128)S(1)}, u32[]{:S(2)}, u32[]{:S(2)}) collective-permute-start(f32[64,2048]{1,0:T(8,128)S(1)} %get-tuple-element.24.field_ref), channel_id=1, source_target_pairs={{0,12},{1,13},{2,14},{3,15},{4,4},{5,5},{6,6},{7,7},{8,8},{9,9},{1... | collective-permute-start | bytes 1572872 | tf_op jit(solution)/shard_map/ppermute | solution.py:248
  31.3 12.6 %collective-permute-start.9 = (f32[32,2048]{1,0:T(8,128)S(1)}, f32[32,2048]{1,0:T(8,128)S(1)}, u32[]{:S(2)}, u32[]{:S(2)}) collective-permute-start(f32[32,2048]{1,0:T(8,128)S(1)} %get-tuple-element.27), channel_id=1, source_target_pairs={{0,2},{1,3},{6,4},{7,5},{8,10},{9,11},{14,12},{15,13},{16,18},{17,... | collective-permute-start | bytes 786440 | tf_op jit(solution)/shard_map/ppermute | solution.py:327
  37.3 16.8 %collective-permute-start.11 = (f32[64,2048]{1,0:T(8,128)S(1)}, f32[64,2048]{1,0:T(8,128)S(1)}, u32[]{:S(2)}, u32[]{:S(2)}) collective-permute-start(f32[64,2048]{1,0:T(8,128)S(1)} %collective-permute-done.6.flipped_ref), channel_id=1, source_target_pairs={{0,1},{1,3},{2,0},{3,2},{4,5},{5,7},{6,4},{7,6},{8,9},{9,11},{10,8... | collective-permute-start | bytes 1572872 | tf_op jit(solution)/shard_map/ppermute | solution.py:262
  37.3 16.7 %collective-permute-start.8 = (f32[32,2048]{1,0:T(8,128)S(1)}, f32[32,2048]{1,0:T(8,128)S(1)}, u32[]{:S(2)}, u32[]{:S(2)}) collective-permute-start(f32[32,2048]{1,0:T(8,128)S(1)} %get-tuple-element.26), channel_id=1, source_target_pairs={{0,6},{1,7},{2,2},{3,3},{4,4},{5,5},{6,0},{7,1},{8,14},{9,15},{10,... | collective-permute-start | bytes 786440 | tf_op jit(solution)/shard_map/ppermute | solution.py:248
  43.9 10.1 %collective-permute-start.10 = (f32[32,2048]{1,0:T(8,128)S(1)}, f32[32,2048]{1,0:T(8,128)S(1)}, u32[]{:S(2)}, u32[]{:S(2)}) collective-permute-start(f32[32,2048]{1,0:T(8,128)S(1)} %collective-permute-done.9), channel_id=1, source_target_pairs={{2,6},{3,7},{4,0},{5,1},{10,14},{11,15},{12,8},{13,9},{18,22},{19,... | collective-permute-start | bytes 786440 | tf_op jit(solution)/shard_map/ppermute | solution.py:327
  54.8 2.0 %collective-permute-start.12 = (f32[64,2048]{1,0:T(8,128)S(1)}, f32[64,2048]{1,0:T(8,128)S(1)}, u32[]{:S(2)}, u32[]{:S(2)}) collective-permute-start(f32[64,2048]{1,0:T(8,128)S(1)} %get-tuple-element.28.field_ref), channel_id=1, source_target_pairs={{0,1},{1,0},{2,3},{3,2},{4,5},{5,4},{6,7},{7,6},{8,9},{9,8},{10,11... | collective-permute-start | bytes 1572872 | tf_op jit(solution)/shard_map/ppermute | solution.py:265
  54.9 15.2 %collective-permute-start.13 = (f32[64,1536]{1,0:T(8,128)S(1)}, f32[64,1536]{1,0:T(8,128)S(1)}, u32[]{:S(2)}, u32[]{:S(2)}) collective-permute-start(f32[64,1536]{1,0:T(8,128)S(1)} %get-tuple-element.34), channel_id=1, source_target_pairs={{0,3},{2,14},{3,15},{7,4},{8,11},{12,0},{13,1},{15,12},{16,19},{18... | collective-permute-start | bytes 1179656 | tf_op jit(solution)/shard_map/ppermute | solution.py:258
  56.8 13.3 %collective-permute-start.15 = (f32[64,1024]{1,0:T(8,128)S(1)}, f32[64,1024]{1,0:T(8,128)S(1)}, u32[]{:S(2)}, u32[]{:S(2)}) collective-permute-start(f32[64,1024]{1,0:T(8,128)S(1)} %get-tuple-element.36), channel_id=1, source_target_pairs={{0,6},{1,7},{2,2},{3,3},{4,4},{5,5},{6,0},{7,1},{8,14},{9,15},{10,... | collective-permute-start | bytes 786440 | tf_op jit(solution)/shard_map/ppermute | solution.py:248
  59.3 10.8 %collective-permute-start.14 = (f32[64,512]{1,0:T(8,128)S(1)}, f32[64,512]{1,0:T(8,128)S(1)}, u32[]{:S(2)}, u32[]{:S(2)}) collective-permute-start(f32[64,512]{1,0:T(8,128)S(1)} %get-tuple-element.35), channel_id=1, source_target_pairs={{0,12},{1,13},{3,0},{4,7},{11,8},{12,15},{14,2},{15,3},{16,28},{17... | collective-permute-start | bytes 393224 | tf_op jit(solution)/shard_map/ppermute | solution.py:258
  71.3 1.3 %collective-permute-start.16 = (f32[64,128]{1,0:T(8,128)S(1)}, f32[64,128]{1,0:T(8,128)S(1)}, u32[]{:S(2)}, u32[]{:S(2)}) collective-permute-start(f32[64,128]{1,0:T(8,128)S(1)} %crossed.1), channel_id=1, source_target_pairs={{0,1},{1,0},{2,3},{3,2},{4,5},{5,4},{6,7},{7,6},{8,9},{9,8},{10,11... | collective-permute-start | bytes 98312 | tf_op jit(solution)/shard_map/ppermute | solution.py:265
  72.5 4.8 %collective-permute-start.19 = (f32[64,128]{1,0:T(8,128)S(1)}, f32[64,128]{1,0:T(8,128)S(1)}, u32[]{:S(2)}, u32[]{:S(2)}) collective-permute-start(f32[64,128]{1,0:T(8,128)S(1)} %add.23), channel_id=1, source_target_pairs={{0,6},{1,7},{2,4},{3,5},{4,2},{5,3},{6,0},{7,1},{8,14},{9,15},{10,... | collective-permute-start | bytes 98312 | tf_op jit(solution)/shard_map/ppermute | solution.py:265
  72.5 5.1 %collective-permute-start.18 = (f32[64,128]{1,0:T(8,128)S(1)}, f32[64,128]{1,0:T(8,128)S(1)}, u32[]{:S(2)}, u32[]{:S(2)}) collective-permute-start(f32[64,128]{1,0:T(8,128)S(1)} %add.23), channel_id=1, source_target_pairs={{0,4},{1,5},{2,6},{3,7},{4,0},{5,1},{6,2},{7,3},{8,12},{9,13},{10,... | collective-permute-start | bytes 98312 | tf_op jit(solution)/shard_map/ppermute | solution.py:265
  75.4 3.9 %collective-permute-start.17 = (f32[64,128]{1,0:T(8,128)S(1)}, f32[64,128]{1,0:T(8,128)S(1)}, u32[]{:S(2)}, u32[]{:S(2)}) collective-permute-start(f32[64,128]{1,0:T(8,128)S(1)} %add.23), channel_id=1, source_target_pairs={{0,2},{1,3},{2,0},{3,1},{4,6},{5,7},{6,4},{7,5},{8,10},{9,11},{10,... | collective-permute-start | bytes 98312 | tf_op jit(solution)/shard_map/ppermute | solution.py:265
  79.3 5.0 %collective-permute-start.20 = (f32[64,128]{1,0:T(8,128)S(1)}, f32[64,128]{1,0:T(8,128)S(1)}, u32[]{:S(2)}, u32[]{:S(2)}) collective-permute-start(f32[64,128]{1,0:T(8,128)S(1)} %add_add_fusion), channel_id=1, source_target_pairs={{0,8},{1,9},{2,10},{3,11},{4,12},{5,13},{6,14},{7,15},{8,0},{9,1},... | collective-permute-start | bytes 98312 | tf_op jit(solution)/shard_map/ppermute | solution.py:265

commit v5 on v4

--- a/solution.py
+++ b/solution.py
@@ -107,11 +107,14 @@
         span = pl.ds(step * blocks, blocks)
         return pltpu.make_async_copy(far_tiles.at[span], tiles_ref.at[span], sems.at[step])
 
-    for step in range(STEPS):
-        fetch(step).start()
+    fetch(0).start()
     split_ref[...] = stacked(field_ref[...])
 
     def body(step, carry):
+        @pl.when(step + 1 < STEPS)
+        def _():
+            fetch(step + 1).start()
+
         fetch(step).wait()
         for row in range(blocks):
             span, total = own_block(

time: 85.5 us -> 85.9 us (level)
  transfers between devices with their start and end apart: 21 -> 21, of which waited for: 10 -> 10; matrix products, arithmetic and copies ran while one was open for 1% -> 1% of each run, Pallas kernels for 18% -> 19%
where the time goes in v5:
time: 85.9 us; the launch traced here: 85.3 us
  starting transfers between devices  37.7 us (44%)
  waiting for transfers between devices  24.3 us (28%)
  Pallas kernels  18.6 us (22%)
  local copies, waits for them, and re-layouts  2.43 us (3%)
  between operations  1.52 us (2%)
    ppermute x5, starting transfers between devices, hop(): return lax.ppermute(value, AXES, pairs)  14.5 us
    ppermute x4, starting transfers between devices, apply(): aside = lax.ppermute(lax.ppermute(second_half, AXES, legs), AXES, round_way)  11.7 us
    ppermute x4, waiting for transfers between devices, apply(): aside = lax.ppermute(lax.ppermute(second_half, AXES, legs), AXES, round_way)  9.33 us
    ppermute x8, waiting for transfers between devices, exchange(): lax.ppermute(value, AXES, [(source, source ^ mask) for source in range(de...  8.33 us
    ppermute x2, starting transfers between devices, one_way(): return lax.ppermute(value, AXES, pairs)  6.38 us
    pallas_call x1, Pallas kernels, own_gram(): pl.pallas_call(functools.partial(own_gram_kernel, bonds + 1), out_shape=[...  5.68 us
    ppermute x5, waiting for transfers between devices, hop(): return lax.ppermute(value, AXES, pairs)  5.45 us
    pallas_call x1, Pallas kernels, first_own_part(): pl.pallas_call(functools.partial(first_own_kernel, bonds + 1), out_shape=...  5.32 us
  transfers between devices with their start and end apart: 21, of which 10 were waited for; matrix products, arithmetic and copies ran while one was open for 1% of the time, Pallas kernels for 19%

profile of v5, /device:TPU:0, one launch (start us, length us, event | category | flops | bytes accessed | tf_op | source)
XLA Modules:
  0.0 85.3 jit_solution(14591987096735939509)
XLA Ops:
  1.3 1.0 %copy-done = f32[64,2048]{1,0:T(8,128)S(1)} copy-done((f32[64,2048]{1,0:T(8,128)S(1)}, f32[64,2048]{1,0:T(8,128)}, u32[]{:S(2)}) %copy-start) | copy-done | bytes 524312
  2.3 0.1 start.1
  2.4 0.5 collective-permute-start
  2.9 6.5 %collective-permute-start.1 = (f32[64,2048]{1,0:T(8,128)S(1)}, f32[64,2048]{1,0:T(8,128)S(1)}, u32[]{:S(2)}, u32[]{:S(2)}) collective-permute-start(f32[64,2048]{1,0:T(8,128)S(1)} %get-tuple-element.20.field_ref.start_ref), channel_id=1, source_target_pairs={{0,12},{1,13},{2,14},{3,15},{4,4},{5,5},{6,6},{7,7},{8,8},{9,9},{1... | collective-permute-start | bytes 1572872 | tf_op jit(solution)/shard_map/ppermute | solution.py:251
  9.4 3.4 %collective-permute-start.3 = (f32[32,2048]{1,0:T(8,128)S(1)}, f32[32,2048]{1,0:T(8,128)S(1)}, u32[]{:S(2)}, u32[]{:S(2)}) collective-permute-start(f32[32,2048]{1,0:T(8,128)S(1)} %get-tuple-element.23), channel_id=1, source_target_pairs={{0,2},{1,3},{6,4},{7,5},{8,10},{9,11},{14,12},{15,13},{16,18},{17,... | collective-permute-start | bytes 786440 | tf_op jit(solution)/shard_map/ppermute | solution.py:330
  12.9 0.0 collective-permute-done.flipped_ref
  12.9 0.0 collective-permute-start.5
  12.9 1.9 %collective-permute-start.2 = (f32[32,2048]{1,0:T(8,128)S(1)}, f32[32,2048]{1,0:T(8,128)S(1)}, u32[]{:S(2)}, u32[]{:S(2)}) collective-permute-start(f32[32,2048]{1,0:T(8,128)S(1)} %get-tuple-element.22), channel_id=1, source_target_pairs={{0,6},{1,7},{2,2},{3,3},{4,4},{5,5},{6,0},{7,1},{8,14},{9,15},{10,... | collective-permute-start | bytes 786440 | tf_op jit(solution)/shard_map/ppermute | solution.py:251
  14.9 4.7 %collective-permute-done.3 = f32[32,2048]{1,0:T(8,128)S(1)} collective-permute-done((f32[32,2048]{1,0:T(8,128)S(1)}, f32[32,2048]{1,0:T(8,128)S(1)}, u32[]{:S(2)}, u32[]{:S(2)}) %collective-permute-start.3) | collective-permute-done | bytes 262176 | tf_op jit(solution)/shard_map/ppermute | solution.py:330
  19.5 1.3 %collective-permute-start.4 = (f32[32,2048]{1,0:T(8,128)S(1)}, f32[32,2048]{1,0:T(8,128)S(1)}, u32[]{:S(2)}, u32[]{:S(2)}) collective-permute-start(f32[32,2048]{1,0:T(8,128)S(1)} %collective-permute-done.3), channel_id=1, source_target_pairs={{2,6},{3,7},{4,0},{5,1},{10,14},{11,15},{12,8},{13,9},{18,22},{19,... | collective-permute-start | bytes 786440 | tf_op jit(solution)/shard_map/ppermute | solution.py:330
  20.8 0.8 pad_add_fusion.table_ref.place_ref
  21.6 0.7 copy-done.1
  22.3 5.3 %first_own.1 = (f32[64,2048]{1,0:T(8,128)S(1)}, f32[16,4,128,128]{3,2,1,0:T(8,128)S(1)}) custom-call(s32[70]{0:T(128)S(1)} %pad_add_fusion.table_ref.place_ref, f32[64,2048]{1,0:T(8,128)S(1)} %get-tuple-element.20.field_ref.start_ref, f32[64,2048]{1,0:T(8,128)S(1)} %collective-permute-done.flipped_ref, f32[16,4,128,128]{3,2,1,0:T(8,128)} %bitcast.7, ...), custom_call_target="tpu_custom_call" | custom-call | flops 536870912 | bytes 5767168 | tf_op jit(solution)/shard_map/first_own/pallas_call | solution.py:285
  27.6 0.0 collective-permute-done.1.refs_0_
  27.6 0.6 far.2.own_ref
  28.2 0.3 collective-permute-done.2.refs_0_
  28.6 0.0 collective-permute-done.4.refs_1_
  28.6 0.0 collective-permute-done.5.refs_2_
  28.6 0.7 combine.1
  29.3 0.1 collective-permute-start.6
  29.3 2.2 %collective-permute-start.7 = (f32[64,2048]{1,0:T(8,128)S(1)}, f32[64,2048]{1,0:T(8,128)S(1)}, u32[]{:S(2)}, u32[]{:S(2)}) collective-permute-start(f32[64,2048]{1,0:T(8,128)S(1)} %get-tuple-element.24.field_ref), channel_id=1, source_target_pairs={{0,12},{1,13},{2,14},{3,15},{4,4},{5,5},{6,6},{7,7},{8,8},{9,9},{1... | collective-permute-start | bytes 1572872 | tf_op jit(solution)/shard_map/ppermute | solution.py:251
  31.5 5.7 %collective-permute-start.9 = (f32[32,2048]{1,0:T(8,128)S(1)}, f32[32,2048]{1,0:T(8,128)S(1)}, u32[]{:S(2)}, u32[]{:S(2)}) collective-permute-start(f32[32,2048]{1,0:T(8,128)S(1)} %get-tuple-element.27), channel_id=1, source_target_pairs={{0,2},{1,3},{6,4},{7,5},{8,10},{9,11},{14,12},{15,13},{16,18},{17,... | collective-permute-start | bytes 786440 | tf_op jit(solution)/shard_map/ppermute | solution.py:330
  37.3 0.0 collective-permute-done.6.flipped_ref
  37.3 0.0 collective-permute-start.11
  37.3 1.9 %collective-permute-start.8 = (f32[32,2048]{1,0:T(8,128)S(1)}, f32[32,2048]{1,0:T(8,128)S(1)}, u32[]{:S(2)}, u32[]{:S(2)}) collective-permute-start(f32[32,2048]{1,0:T(8,128)S(1)} %get-tuple-element.26), channel_id=1, source_target_pairs={{0,6},{1,7},{2,2},{3,3},{4,4},{5,5},{6,0},{7,1},{8,14},{9,15},{10,... | collective-permute-start | bytes 786440 | tf_op jit(solution)/shard_map/ppermute | solution.py:251
  39.2 4.7 %collective-permute-done.9 = f32[32,2048]{1,0:T(8,128)S(1)} collective-permute-done((f32[32,2048]{1,0:T(8,128)S(1)}, f32[32,2048]{1,0:T(8,128)S(1)}, u32[]{:S(2)}, u32[]{:S(2)}) %collective-permute-start.9) | collective-permute-done | bytes 262176 | tf_op jit(solution)/shard_map/ppermute | solution.py:330
  43.9 1.3 %collective-permute-start.10 = (f32[32,2048]{1,0:T(8,128)S(1)}, f32[32,2048]{1,0:T(8,128)S(1)}, u32[]{:S(2)}, u32[]{:S(2)}) collective-permute-start(f32[32,2048]{1,0:T(8,128)S(1)} %collective-permute-done.9), channel_id=1, source_target_pairs={{2,6},{3,7},{4,0},{5,1},{10,14},{11,15},{12,8},{13,9},{18,22},{19,... | collective-permute-start | bytes 786440 | tf_op jit(solution)/shard_map/ppermute | solution.py:330
  45.2 3.6 %own.1.own_ref = f32[64,2048]{1,0:T(8,128)S(1)} custom-call(s32[70]{0:T(128)S(1)} %pad_add_fusion.table_ref.place_ref, f32[64,2048]{1,0:T(8,128)S(1)} %get-tuple-element.24.field_ref, f32[64,2048]{1,0:T(8,128)S(1)} %collective-permute-done.6.flipped_ref, f32[16,4,128,128]{3,2,1,0:T(8,128)S(1)} %get-tuple-element.25.tiles_ref, s32[1,2048]{1,0:T(1,128)S(1)} %bitcast.5), custom_call_target="tpu_custom_call" | custom-call | flops 536870912 | bytes 5767168 | tf_op jit(solution)/shard_map/own/pallas_call | solution.py:300
  48.9 0.6 far.3.own_ref
  49.5 5.1 %collective-permute-done.8.refs_0_ = f32[32,2048]{1,0:T(8,128)S(1)} collective-permute-done((f32[32,2048]{1,0:T(8,128)S(1)}, f32[32,2048]{1,0:T(8,128)S(1)}, u32[]{:S(2)}, u32[]{:S(2)}) %collective-permute-start.8) | collective-permute-done | bytes 262176 | tf_op jit(solution)/shard_map/ppermute | solution.py:251
  54.6 0.8 filter.1
  55.4 0.1 collective-permute-start.12
  55.5 1.9 %collective-permute-start.13 = (f32[64,1536]{1,0:T(8,128)S(1)}, f32[64,1536]{1,0:T(8,128)S(1)}, u32[]{:S(2)}, u32[]{:S(2)}) collective-permute-start(f32[64,1536]{1,0:T(8,128)S(1)} %get-tuple-element.34), channel_id=1, source_target_pairs={{0,3},{2,14},{3,15},{7,4},{8,11},{12,0},{13,1},{15,12},{16,19},{18... | collective-permute-start | bytes 1179656 | tf_op jit(solution)/shard_map/ppermute | solution.py:261
  57.4 1.9 %collective-permute-start.15 = (f32[64,1024]{1,0:T(8,128)S(1)}, f32[64,1024]{1,0:T(8,128)S(1)}, u32[]{:S(2)}, u32[]{:S(2)}) collective-permute-start(f32[64,1024]{1,0:T(8,128)S(1)} %get-tuple-element.36), channel_id=1, source_target_pairs={{0,6},{1,7},{2,2},{3,3},{4,4},{5,5},{6,0},{7,1},{8,14},{9,15},{10,... | collective-permute-start | bytes 786440 | tf_op jit(solution)/shard_map/ppermute | solution.py:251
  59.3 4.5 %collective-permute-start.14 = (f32[64,512]{1,0:T(8,128)S(1)}, f32[64,512]{1,0:T(8,128)S(1)}, u32[]{:S(2)}, u32[]{:S(2)}) collective-permute-start(f32[64,512]{1,0:T(8,128)S(1)} %get-tuple-element.35), channel_id=1, source_target_pairs={{0,12},{1,13},{3,0},{4,7},{11,8},{12,15},{14,2},{15,3},{16,28},{17... | collective-permute-start | bytes 393224 | tf_op jit(solution)/shard_map/ppermute | solution.py:261
  63.8 5.7 %own_gram.1 = (f32[64,128]{1,0:T(8,128)S(1)}, f32[64,2048]{1,0:T(8,128)}) custom-call(s32[70]{0:T(128)S(1)} %pad_add_fusion.table_ref.place_ref, s32[1]{0:T(128)S(6)} %copy.13.live_ref, f32[64,2048]{1,0:T(8,128)S(1)} %get-tuple-element.28.field_ref, f32[64,2048]{1,0:T(8,128)S(1)} %collective-permute-done.12.flipped_ref, ...), custom_call_target="tpu_custom_call" | custom-call | flops 536870912 | bytes 5767168 | tf_op jit(solution)/shard_map/own_gram/pallas_call | solution.py:312
  69.5 1.2 %collective-permute-done.13.refs_0_ = f32[64,1536]{1,0:T(8,128)S(1)} collective-permute-done((f32[64,1536]{1,0:T(8,128)S(1)}, f32[64,1536]{1,0:T(8,128)S(1)}, u32[]{:S(2)}, u32[]{:S(2)}) %collective-permute-start.13) | collective-permute-done | bytes 393248 | tf_op jit(solution)/shard_map/ppermute | solution.py:261
  70.7 1.1 %crossed.1 = f32[64,128]{1,0:T(8,128)S(1)} custom-call(s32[70]{0:T(128)S(1)} %pad_add_fusion.table_ref.place_ref, f32[64,128]{1,0:T(8,128)S(1)} %get-tuple-element.33.own_ref, f32[64,2048]{1,0:T(8,128)S(1)} %get-tuple-element.28.field_ref, f32[64,1536]{1,0:T(8,128)S(1)} %collective-permute-done.13.refs_0_, f32[64,512]{1,0:T(8,128)S(1)} %collective-permute-done.14.refs_1_, ...), custom_call_target="tpu_custom_call" | custom-call | tf_op jit(solution)/shard_map/crossed/pallas_call | solution.py:379
  71.8 0.1 collective-permute-start.16
  71.9 1.2 %collective-permute-done.16 = f32[64,128]{1,0:T(8,128)S(1)} collective-permute-done((f32[64,128]{1,0:T(8,128)S(1)}, f32[64,128]{1,0:T(8,128)S(1)}, u32[]{:S(2)}, u32[]{:S(2)}) %collective-permute-start.16) | collective-permute-done | bytes 32800 | tf_op jit(solution)/shard_map/ppermute | solution.py:268
  73.1 2.7 %collective-permute-start.18 = (f32[64,128]{1,0:T(8,128)S(1)}, f32[64,128]{1,0:T(8,128)S(1)}, u32[]{:S(2)}, u32[]{:S(2)}) collective-permute-start(f32[64,128]{1,0:T(8,128)S(1)} %add.23), channel_id=1, source_target_pairs={{0,4},{1,5},{2,6},{3,7},{4,0},{5,1},{6,2},{7,3},{8,12},{9,13},{10,... | collective-permute-start | bytes 98312 | tf_op jit(solution)/shard_map/ppermute | solution.py:268
  75.8 0.8 collective-permute-start.17
  76.6 1.3 %collective-permute-done.19 = f32[64,128]{1,0:T(8,128)S(1)} collective-permute-done((f32[64,128]{1,0:T(8,128)S(1)}, f32[64,128]{1,0:T(8,128)S(1)}, u32[]{:S(2)}, u32[]{:S(2)}) %collective-permute-start.19) | collective-permute-done | bytes 32800 | tf_op jit(solution)/shard_map/ppermute | solution.py:268
  77.9 0.1 collective-permute-done.18
  78.0 1.7 %collective-permute-done.17 = f32[64,128]{1,0:T(8,128)S(1)} collective-permute-done((f32[64,128]{1,0:T(8,128)S(1)}, f32[64,128]{1,0:T(8,128)S(1)}, u32[]{:S(2)}, u32[]{:S(2)}) %collective-permute-start.17) | collective-permute-done | bytes 32800 | tf_op jit(solution)/shard_map/ppermute | solution.py:268
  79.7 0.9 %collective-permute-start.20 = (f32[64,128]{1,0:T(8,128)S(1)}, f32[64,128]{1,0:T(8,128)S(1)}, u32[]{:S(2)}, u32[]{:S(2)}) collective-permute-start(f32[64,128]{1,0:T(8,128)S(1)} %add_add_fusion), channel_id=1, source_target_pairs={{0,8},{1,9},{2,10},{3,11},{4,12},{5,13},{6,14},{7,15},{8,0},{9,1},... | collective-permute-start | bytes 98312 | tf_op jit(solution)/shard_map/ppermute | solution.py:268
  80.6 4.0 %collective-permute-done.20 = f32[64,128]{1,0:T(8,128)S(1)} collective-permute-done((f32[64,128]{1,0:T(8,128)S(1)}, f32[64,128]{1,0:T(8,128)S(1)}, u32[]{:S(2)}, u32[]{:S(2)}) %collective-permute-start.20) | collective-permute-done | bytes 32800 | tf_op jit(solution)/shard_map/ppermute | solution.py:268
  84.6 0.7 fusion
  (12 shorter events, 0.0 us)
Async XLA Ops:
  1.3 1.0 %copy-start = (f32[64,2048]{1,0:T(8,128)S(1)}, f32[64,2048]{1,0:T(8,128)}, u32[]{:S(2)}) copy-start(f32[64,2048]{1,0:T(8,128)} %vectors_ref.1) | copy-start | bytes 1572868
  2.4 10.5 %collective-permute-start = (f32[64,2048]{1,0:T(8,128)S(1)}, f32[64,2048]{1,0:T(8,128)S(1)}, u32[]{:S(2)}, u32[]{:S(2)}) collective-permute-start(f32[64,2048]{1,0:T(8,128)S(1)} %get-tuple-element.20.field_ref.start_ref), channel_id=1, source_target_pairs={{0,1},{1,0},{2,3},{3,2},{4,5},{5,4},{6,7},{7,6},{8,9},{9,8},{10,11... | collective-permute-start | bytes 1572872 | tf_op jit(solution)/shard_map/ppermute | solution.py:268
  2.9 24.7 %collective-permute-start.1 = (f32[64,2048]{1,0:T(8,128)S(1)}, f32[64,2048]{1,0:T(8,128)S(1)}, u32[]{:S(2)}, u32[]{:S(2)}) collective-permute-start(f32[64,2048]{1,0:T(8,128)S(1)} %get-tuple-element.20.field_ref.start_ref), channel_id=1, source_target_pairs={{0,12},{1,13},{2,14},{3,15},{4,4},{5,5},{6,6},{7,7},{8,8},{9,9},{1... | collective-permute-start | bytes 1572872 | tf_op jit(solution)/shard_map/ppermute | solution.py:251
  9.4 10.1 %collective-permute-start.3 = (f32[32,2048]{1,0:T(8,128)S(1)}, f32[32,2048]{1,0:T(8,128)S(1)}, u32[]{:S(2)}, u32[]{:S(2)}) collective-permute-start(f32[32,2048]{1,0:T(8,128)S(1)} %get-tuple-element.23), channel_id=1, source_target_pairs={{0,2},{1,3},{6,4},{7,5},{8,10},{9,11},{14,12},{15,13},{16,18},{17,... | collective-permute-start | bytes 786440 | tf_op jit(solution)/shard_map/ppermute | solution.py:330
  12.9 15.7 %collective-permute-start.5 = (f32[64,2048]{1,0:T(8,128)S(1)}, f32[64,2048]{1,0:T(8,128)S(1)}, u32[]{:S(2)}, u32[]{:S(2)}) collective-permute-start(f32[64,2048]{1,0:T(8,128)S(1)} %collective-permute-done.flipped_ref), channel_id=1, source_target_pairs={{0,1},{1,3},{2,0},{3,2},{4,5},{5,7},{6,4},{7,6},{8,9},{9,11},{10,8... | collective-permute-start | bytes 1572872 | tf_op jit(solution)/shard_map/ppermute | solution.py:265
  12.9 15.6 %collective-permute-start.2 = (f32[32,2048]{1,0:T(8,128)S(1)}, f32[32,2048]{1,0:T(8,128)S(1)}, u32[]{:S(2)}, u32[]{:S(2)}) collective-permute-start(f32[32,2048]{1,0:T(8,128)S(1)} %get-tuple-element.22), channel_id=1, source_target_pairs={{0,6},{1,7},{2,2},{3,3},{4,4},{5,5},{6,0},{7,1},{8,14},{9,15},{10,... | collective-permute-start | bytes 786440 | tf_op jit(solution)/shard_map/ppermute | solution.py:251
  19.5 9.1 %collective-permute-start.4 = (f32[32,2048]{1,0:T(8,128)S(1)}, f32[32,2048]{1,0:T(8,128)S(1)}, u32[]{:S(2)}, u32[]{:S(2)}) collective-permute-start(f32[32,2048]{1,0:T(8,128)S(1)} %collective-permute-done.3), channel_id=1, source_target_pairs={{2,6},{3,7},{4,0},{5,1},{10,14},{11,15},{12,8},{13,9},{18,22},{19,... | collective-permute-start | bytes 786440 | tf_op jit(solution)/shard_map/ppermute | solution.py:330
  21.6 0.7 copy-start.1
  29.3 8.0 %collective-permute-start.6 = (f32[64,2048]{1,0:T(8,128)S(1)}, f32[64,2048]{1,0:T(8,128)S(1)}, u32[]{:S(2)}, u32[]{:S(2)}) collective-permute-start(f32[64,2048]{1,0:T(8,128)S(1)} %get-tuple-element.24.field_ref), channel_id=1, source_target_pairs={{0,1},{1,0},{2,3},{3,2},{4,5},{5,4},{6,7},{7,6},{8,9},{9,8},{10,11... | collective-permute-start | bytes 1572872 | tf_op jit(solution)/shard_map/ppermute | solution.py:268
  29.3 19.5 %collective-permute-start.7 = (f32[64,2048]{1,0:T(8,128)S(1)}, f32[64,2048]{1,0:T(8,128)S(1)}, u32[]{:S(2)}, u32[]{:S(2)}) collective-permute-start(f32[64,2048]{1,0:T(8,128)S(1)} %get-tuple-element.24.field_ref), channel_id=1, source_target_pairs={{0,12},{1,13},{2,14},{3,15},{4,4},{5,5},{6,6},{7,7},{8,8},{9,9},{1... | collective-permute-start | bytes 1572872 | tf_op jit(solution)/shard_map/ppermute | solution.py:251
  31.5 12.4 %collective-permute-start.9 = (f32[32,2048]{1,0:T(8,128)S(1)}, f32[32,2048]{1,0:T(8,128)S(1)}, u32[]{:S(2)}, u32[]{:S(2)}) collective-permute-start(f32[32,2048]{1,0:T(8,128)S(1)} %get-tuple-element.27), channel_id=1, source_target_pairs={{0,2},{1,3},{6,4},{7,5},{8,10},{9,11},{14,12},{15,13},{16,18},{17,... | collective-permute-start | bytes 786440 | tf_op jit(solution)/shard_map/ppermute | solution.py:330
  37.3 17.3 %collective-permute-start.11 = (f32[64,2048]{1,0:T(8,128)S(1)}, f32[64,2048]{1,0:T(8,128)S(1)}, u32[]{:S(2)}, u32[]{:S(2)}) collective-permute-start(f32[64,2048]{1,0:T(8,128)S(1)} %collective-permute-done.6.flipped_ref), channel_id=1, source_target_pairs={{0,1},{1,3},{2,0},{3,2},{4,5},{5,7},{6,4},{7,6},{8,9},{9,11},{10,8... | collective-permute-start | bytes 1572872 | tf_op jit(solution)/shard_map/ppermute | solution.py:265
  37.3 17.3 %collective-permute-start.8 = (f32[32,2048]{1,0:T(8,128)S(1)}, f32[32,2048]{1,0:T(8,128)S(1)}, u32[]{:S(2)}, u32[]{:S(2)}) collective-permute-start(f32[32,2048]{1,0:T(8,128)S(1)} %get-tuple-element.26), channel_id=1, source_target_pairs={{0,6},{1,7},{2,2},{3,3},{4,4},{5,5},{6,0},{7,1},{8,14},{9,15},{10,... | collective-permute-start | bytes 786440 | tf_op jit(solution)/shard_map/ppermute | solution.py:251
  43.9 10.7 %collective-permute-start.10 = (f32[32,2048]{1,0:T(8,128)S(1)}, f32[32,2048]{1,0:T(8,128)S(1)}, u32[]{:S(2)}, u32[]{:S(2)}) collective-permute-start(f32[32,2048]{1,0:T(8,128)S(1)} %collective-permute-done.9), channel_id=1, source_target_pairs={{2,6},{3,7},{4,0},{5,1},{10,14},{11,15},{12,8},{13,9},{18,22},{19,... | collective-permute-start | bytes 786440 | tf_op jit(solution)/shard_map/ppermute | solution.py:330
  55.4 2.0 %collective-permute-start.12 = (f32[64,2048]{1,0:T(8,128)S(1)}, f32[64,2048]{1,0:T(8,128)S(1)}, u32[]{:S(2)}, u32[]{:S(2)}) collective-permute-start(f32[64,2048]{1,0:T(8,128)S(1)} %get-tuple-element.28.field_ref), channel_id=1, source_target_pairs={{0,1},{1,0},{2,3},{3,2},{4,5},{5,4},{6,7},{7,6},{8,9},{9,8},{10,11... | collective-permute-start | bytes 1572872 | tf_op jit(solution)/shard_map/ppermute | solution.py:268
  55.5 15.2 %collective-permute-start.13 = (f32[64,1536]{1,0:T(8,128)S(1)}, f32[64,1536]{1,0:T(8,128)S(1)}, u32[]{:S(2)}, u32[]{:S(2)}) collective-permute-start(f32[64,1536]{1,0:T(8,128)S(1)} %get-tuple-element.34), channel_id=1, source_target_pairs={{0,3},{2,14},{3,15},{7,4},{8,11},{12,0},{13,1},{15,12},{16,19},{18... | collective-permute-start | bytes 1179656 | tf_op jit(solution)/shard_map/ppermute | solution.py:261
  57.4 13.3 %collective-permute-start.15 = (f32[64,1024]{1,0:T(8,128)S(1)}, f32[64,1024]{1,0:T(8,128)S(1)}, u32[]{:S(2)}, u32[]{:S(2)}) collective-permute-start(f32[64,1024]{1,0:T(8,128)S(1)} %get-tuple-element.36), channel_id=1, source_target_pairs={{0,6},{1,7},{2,2},{3,3},{4,4},{5,5},{6,0},{7,1},{8,14},{9,15},{10,... | collective-permute-start | bytes 786440 | tf_op jit(solution)/shard_map/ppermute | solution.py:251
  59.3 11.3 %collective-permute-start.14 = (f32[64,512]{1,0:T(8,128)S(1)}, f32[64,512]{1,0:T(8,128)S(1)}, u32[]{:S(2)}, u32[]{:S(2)}) collective-permute-start(f32[64,512]{1,0:T(8,128)S(1)} %get-tuple-element.35), channel_id=1, source_target_pairs={{0,12},{1,13},{3,0},{4,7},{11,8},{12,15},{14,2},{15,3},{16,28},{17... | collective-permute-start | bytes 393224 | tf_op jit(solution)/shard_map/ppermute | solution.py:261
  71.8 1.3 %collective-permute-start.16 = (f32[64,128]{1,0:T(8,128)S(1)}, f32[64,128]{1,0:T(8,128)S(1)}, u32[]{:S(2)}, u32[]{:S(2)}) collective-permute-start(f32[64,128]{1,0:T(8,128)S(1)} %crossed.1), channel_id=1, source_target_pairs={{0,1},{1,0},{2,3},{3,2},{4,5},{5,4},{6,7},{7,6},{8,9},{9,8},{10,11... | collective-permute-start | bytes 98312 | tf_op jit(solution)/shard_map/ppermute | solution.py:268
  73.1 4.8 %collective-permute-start.19 = (f32[64,128]{1,0:T(8,128)S(1)}, f32[64,128]{1,0:T(8,128)S(1)}, u32[]{:S(2)}, u32[]{:S(2)}) collective-permute-start(f32[64,128]{1,0:T(8,128)S(1)} %add.23), channel_id=1, source_target_pairs={{0,6},{1,7},{2,4},{3,5},{4,2},{5,3},{6,0},{7,1},{8,14},{9,15},{10,... | collective-permute-start | bytes 98312 | tf_op jit(solution)/shard_map/ppermute | solution.py:268
  73.1 4.9 %collective-permute-start.18 = (f32[64,128]{1,0:T(8,128)S(1)}, f32[64,128]{1,0:T(8,128)S(1)}, u32[]{:S(2)}, u32[]{:S(2)}) collective-permute-start(f32[64,128]{1,0:T(8,128)S(1)} %add.23), channel_id=1, source_target_pairs={{0,4},{1,5},{2,6},{3,7},{4,0},{5,1},{6,2},{7,3},{8,12},{9,13},{10,... | collective-permute-start | bytes 98312 | tf_op jit(solution)/shard_map/ppermute | solution.py:268
  75.8 3.9 %collective-permute-start.17 = (f32[64,128]{1,0:T(8,128)S(1)}, f32[64,128]{1,0:T(8,128)S(1)}, u32[]{:S(2)}, u32[]{:S(2)}) collective-permute-start(f32[64,128]{1,0:T(8,128)S(1)} %add.23), channel_id=1, source_target_pairs={{0,2},{1,3},{2,0},{3,1},{4,6},{5,7},{6,4},{7,5},{8,10},{9,11},{10,... | collective-permute-start | bytes 98312 | tf_op jit(solution)/shard_map/ppermute | solution.py:268
  79.7 4.9 %collective-permute-start.20 = (f32[64,128]{1,0:T(8,128)S(1)}, f32[64,128]{1,0:T(8,128)S(1)}, u32[]{:S(2)}, u32[]{:S(2)}) collective-permute-start(f32[64,128]{1,0:T(8,128)S(1)} %add_add_fusion), channel_id=1, source_target_pairs={{0,8},{1,9},{2,10},{3,11},{4,12},{5,13},{6,14},{7,15},{8,0},{9,1},... | collective-permute-start | bytes 98312 | tf_op jit(solution)/shard_map/ppermute | solution.py:268

commit v6 on v2

--- a/solution.py
+++ b/solution.py
@@ -315,13 +315,16 @@
 
     three = [full, rows_by(vec_count // 2, row_count), rows_by(vec_count // 2, row_count)]
 
-    def apply(own, field, first_half, second_half):
+    def apply(own_of, late, field, first_half, second_half):
         legs = [(here, here ^ 2) for here in range(dev_count) if coupled(here, 1)]
         round_way = [(here, here ^ 4) for here in range(dev_count) if not coupled(here, 1)]
         flipped = exchange(field, 1)
         far = [hop(field, bond) for bond in reversed(range(2, bonds))]
         aside = lax.ppermute(lax.ppermute(second_half, AXES, legs), AXES, round_way)
         direct = hop(first_half, 1)
+        own = own_of(field, flipped)
+        if late:
+            own, flipped = lax.optimization_barrier((own, flipped))
         closest = near(flipped)
         total = pl.pallas_call(
             functools.partial(far_kernel, bonds),
@@ -332,7 +335,7 @@
             compiler_params=params,
             cost_estimate=pl.CostEstimate(flops=vec_count * row_count, bytes_accessed=12 * vec_count * row_count, transcendentals=0),
             name="far",
-        )(table, own(field, flipped), *far)
+        )(table, own, *far)
         return total, [direct, aside, closest]
 
     start, *halves_of = pl.pallas_call(
@@ -343,7 +346,7 @@
         compiler_params=params,
         name="start",
     )(live_rows, vectors)
-    own, hops = apply(first_own_part, start, *halves_of)
+    own, hops = apply(first_own_part, False, start, *halves_of)
     first, *halves_of = pl.pallas_call(
         combine_kernel,
         out_shape=three,
@@ -352,7 +355,7 @@
         compiler_params=params,
         name="combine",
     )(table, live_rows, own, *hops)
-    own, hops = apply(own_part, first, *halves_of)
+    own, hops = apply(own_part, True, first, *halves_of)
     cut = row_count * 3 // 4
     kept, sent, lead, rest = pl.pallas_call(
         filter_kernel,

time: 85.5 us -> 86.7 us (1.014)
  waiting for transfers between devices: 23.9 us -> 26 us
    ppermute x5, waiting for transfers between devices: 5.4 us -> 9.86 us  [hop(): return lax.ppermute(value, AXES, pairs)]
    ppermute x4, waiting for transfers between devices: 9.33 us -> 5.66 us  [apply(): aside = lax.ppermute(lax.ppermute(second_half, AXES, legs), AXES, round_way)]
    ppermute x2, waiting for transfers between devices: 0.01 us -> 1.43 us  [near(): return lax.ppermute(flipped, AXES, pairs)]
    ppermute x8, starting transfers between devices: 5.51 us -> 4.64 us  [exchange(): lax.ppermute(value, AXES, [(source, source ^ mask) for source in range(de...]
  transfers between devices with their start and end apart: 21 -> 21, of which waited for: 10 -> 12; matrix products, arithmetic and copies ran while one was open for 1% -> 1% of each run, Pallas kernels for 18% -> 18%
where the time goes in v6:
time: 86.7 us; the launch traced here: 86.2 us
  starting transfers between devices  37.3 us (43%)
  waiting for transfers between devices  26 us (30%)
  Pallas kernels  18.2 us (21%)
  local copies, waits for them, and re-layouts  2.43 us (3%)
  between operations  1.53 us (2%)
    ppermute x5, starting transfers between devices, hop(): return lax.ppermute(value, AXES, pairs)  14.2 us
    ppermute x4, starting transfers between devices, apply(): aside = lax.ppermute(lax.ppermute(second_half, AXES, legs), AXES, round_way)  12 us
    ppermute x5, waiting for transfers between devices, hop(): return lax.ppermute(value, AXES, pairs)  9.86 us
    ppermute x8, waiting for transfers between devices, exchange(): lax.ppermute(value, AXES, [(source, source ^ mask) for source in range(de...  7.91 us
    ppermute x2, starting transfers between devices, one_way(): return lax.ppermute(value, AXES, pairs)  6.4 us
    pallas_call x1, Pallas kernels, own_gram(): pl.pallas_call(functools.partial(own_gram_kernel, bonds + 1), out_shape=[...  5.69 us
    ppermute x4, waiting for transfers between devices, apply(): aside = lax.ppermute(lax.ppermute(second_half, AXES, legs), AXES, round_way)  5.66 us
    pallas_call x1, Pallas kernels, first_own_part(): pl.pallas_call(functools.partial(first_own_kernel, bonds + 1), out_shape=...  4.94 us
  transfers between devices with their start and end apart: 21, of which 12 were waited for; matrix products, arithmetic and copies ran while one was open for 1% of the time, Pallas kernels for 18%

profile of v6, /device:TPU:0, one launch (start us, length us, event | category | flops | bytes accessed | tf_op | source)
XLA Modules:
  0.0 86.2 jit_solution(5098862012851604866)
XLA Ops:
  1.3 1.0 %copy-done.1 = f32[64,2048]{1,0:T(8,128)S(1)} copy-done((f32[64,2048]{1,0:T(8,128)S(1)}, f32[64,2048]{1,0:T(8,128)}, u32[]{:S(2)}) %copy-start.1) | copy-done | bytes 524312
  2.3 0.1 start.1
  2.4 0.5 collective-permute-start
  2.9 6.5 %collective-permute-start.1 = (f32[64,2048]{1,0:T(8,128)S(1)}, f32[64,2048]{1,0:T(8,128)S(1)}, u32[]{:S(2)}, u32[]{:S(2)}) collective-permute-start(f32[64,2048]{1,0:T(8,128)S(1)} %get-tuple-element.20.field_ref.start_ref), channel_id=1, source_target_pairs={{0,12},{1,13},{2,14},{3,15},{4,4},{5,5},{6,6},{7,7},{8,8},{9,9},{1... | collective-permute-start | bytes 1572872 | tf_op jit(solution)/shard_map/ppermute | solution.py:243
  9.4 3.4 %collective-permute-start.3 = (f32[32,2048]{1,0:T(8,128)S(1)}, f32[32,2048]{1,0:T(8,128)S(1)}, u32[]{:S(2)}, u32[]{:S(2)}) collective-permute-start(f32[32,2048]{1,0:T(8,128)S(1)} %get-tuple-element.22), channel_id=1, source_target_pairs={{0,2},{1,3},{6,4},{7,5},{8,10},{9,11},{14,12},{15,13},{16,18},{17,... | collective-permute-start | bytes 786440 | tf_op jit(solution)/shard_map/ppermute | solution.py:323
  12.9 0.0 collective-permute-start.5
  12.9 1.9 %collective-permute-start.2 = (f32[32,2048]{1,0:T(8,128)S(1)}, f32[32,2048]{1,0:T(8,128)S(1)}, u32[]{:S(2)}, u32[]{:S(2)}) collective-permute-start(f32[32,2048]{1,0:T(8,128)S(1)} %get-tuple-element.21), channel_id=1, source_target_pairs={{0,6},{1,7},{2,2},{3,3},{4,4},{5,5},{6,0},{7,1},{8,14},{9,15},{10,... | collective-permute-start | bytes 786440 | tf_op jit(solution)/shard_map/ppermute | solution.py:243
  14.9 4.7 %collective-permute-done.3 = f32[32,2048]{1,0:T(8,128)S(1)} collective-permute-done((f32[32,2048]{1,0:T(8,128)S(1)}, f32[32,2048]{1,0:T(8,128)S(1)}, u32[]{:S(2)}, u32[]{:S(2)}) %collective-permute-start.3) | collective-permute-done | bytes 262176 | tf_op jit(solution)/shard_map/ppermute | solution.py:323
  19.5 1.3 %collective-permute-start.4 = (f32[32,2048]{1,0:T(8,128)S(1)}, f32[32,2048]{1,0:T(8,128)S(1)}, u32[]{:S(2)}, u32[]{:S(2)}) collective-permute-start(f32[32,2048]{1,0:T(8,128)S(1)} %collective-permute-done.3), channel_id=1, source_target_pairs={{2,6},{3,7},{4,0},{5,1},{10,14},{11,15},{12,8},{13,9},{18,22},{19,... | collective-permute-start | bytes 786440 | tf_op jit(solution)/shard_map/ppermute | solution.py:323
  20.8 0.8 pad_add_fusion.table_ref.place_ref
  21.6 0.7 copy-done.2
  22.3 4.9 %first_own.1.own_ref = f32[64,2048]{1,0:T(8,128)S(1)} custom-call(s32[70]{0:T(128)S(1)} %pad_add_fusion.table_ref.place_ref, f32[64,2048]{1,0:T(8,128)S(1)} %get-tuple-element.20.field_ref.start_ref, f32[64,2048]{1,0:T(8,128)S(1)} %collective-permute-done.flipped_ref, f32[16,4,128,128]{3,2,1,0:T(8,128)} %bitcast.4, s32[1,2048]{1,0:T(1,128)S(1)} %bitcast.7), custom_call_target="tpu_custom_call" | custom-call | flops 536870912 | bytes 5767168 | tf_op jit(solution)/shard_map/first_own/pallas_call | solution.py:277
  27.2 0.0 collective-permute-done.1.refs_0_
  27.2 0.6 far.2.own_ref
  27.9 0.7 collective-permute-done.2.refs_0_
  28.6 0.0 collective-permute-done.4.refs_1_
  28.6 0.7 combine.1
  29.3 0.1 collective-permute-start.6
  29.3 1.9 %collective-permute-start.7 = (f32[64,2048]{1,0:T(8,128)S(1)}, f32[64,2048]{1,0:T(8,128)S(1)}, u32[]{:S(2)}, u32[]{:S(2)}) collective-permute-start(f32[64,2048]{1,0:T(8,128)S(1)} %get-tuple-element.23.field_ref), channel_id=1, source_target_pairs={{0,12},{1,13},{2,14},{3,15},{4,4},{5,5},{6,6},{7,7},{8,8},{9,9},{1... | collective-permute-start | bytes 1572872 | tf_op jit(solution)/shard_map/ppermute | solution.py:243
  31.3 6.0 %collective-permute-start.9 = (f32[32,2048]{1,0:T(8,128)S(1)}, f32[32,2048]{1,0:T(8,128)S(1)}, u32[]{:S(2)}, u32[]{:S(2)}) collective-permute-start(f32[32,2048]{1,0:T(8,128)S(1)} %get-tuple-element.26), channel_id=1, source_target_pairs={{0,2},{1,3},{6,4},{7,5},{8,10},{9,11},{14,12},{15,13},{16,18},{17,... | collective-permute-start | bytes 786440 | tf_op jit(solution)/shard_map/ppermute | solution.py:323
  37.3 0.0 collective-permute-done.6.flipped_ref
  37.3 3.6 %own.1.own_ref = f32[64,2048]{1,0:T(8,128)S(1)} custom-call(s32[70]{0:T(128)S(1)} %pad_add_fusion.table_ref.place_ref, f32[64,2048]{1,0:T(8,128)S(1)} %get-tuple-element.23.field_ref, f32[64,2048]{1,0:T(8,128)S(1)} %collective-permute-done.6.flipped_ref, f32[16,4,128,128]{3,2,1,0:T(8,128)S(1)} %bitcast.5, s32[1,2048]{1,0:T(1,128)S(1)} %bitcast.8), custom_call_target="tpu_custom_call" | custom-call | flops 536870912 | bytes 5767168 | tf_op jit(solution)/shard_map/own/pallas_call | solution.py:293
  41.0 0.0 collective-permute-start.11
  41.0 1.9 %collective-permute-start.8 = (f32[32,2048]{1,0:T(8,128)S(1)}, f32[32,2048]{1,0:T(8,128)S(1)}, u32[]{:S(2)}, u32[]{:S(2)}) collective-permute-start(f32[32,2048]{1,0:T(8,128)S(1)} %get-tuple-element.25), channel_id=1, source_target_pairs={{0,6},{1,7},{2,2},{3,3},{4,4},{5,5},{6,0},{7,1},{8,14},{9,15},{10,... | collective-permute-start | bytes 786440 | tf_op jit(solution)/shard_map/ppermute | solution.py:243
  42.9 1.0 %collective-permute-done.9 = f32[32,2048]{1,0:T(8,128)S(1)} collective-permute-done((f32[32,2048]{1,0:T(8,128)S(1)}, f32[32,2048]{1,0:T(8,128)S(1)}, u32[]{:S(2)}, u32[]{:S(2)}) %collective-permute-start.9) | collective-permute-done | bytes 262176 | tf_op jit(solution)/shard_map/ppermute | solution.py:323
  43.9 1.3 %collective-permute-start.10 = (f32[32,2048]{1,0:T(8,128)S(1)}, f32[32,2048]{1,0:T(8,128)S(1)}, u32[]{:S(2)}, u32[]{:S(2)}) collective-permute-start(f32[32,2048]{1,0:T(8,128)S(1)} %collective-permute-done.9), channel_id=1, source_target_pairs={{2,6},{3,7},{4,0},{5,1},{10,14},{11,15},{12,8},{13,9},{18,22},{19,... | collective-permute-start | bytes 786440 | tf_op jit(solution)/shard_map/ppermute | solution.py:323
  45.2 2.2 %collective-permute-done.7.refs_0_ = f32[64,2048]{1,0:T(8,128)S(1)} collective-permute-done((f32[64,2048]{1,0:T(8,128)S(1)}, f32[64,2048]{1,0:T(8,128)S(1)}, u32[]{:S(2)}, u32[]{:S(2)}) %collective-permute-start.7) | collective-permute-done | bytes 524320 | tf_op jit(solution)/shard_map/ppermute | solution.py:243
  47.4 0.6 far.3.own_ref
  48.0 6.3 %collective-permute-done.8.refs_0_ = f32[32,2048]{1,0:T(8,128)S(1)} collective-permute-done((f32[32,2048]{1,0:T(8,128)S(1)}, f32[32,2048]{1,0:T(8,128)S(1)}, u32[]{:S(2)}, u32[]{:S(2)}) %collective-permute-start.8) | collective-permute-done | bytes 262176 | tf_op jit(solution)/shard_map/ppermute | solution.py:243
  54.3 1.4 %collective-permute-done.11.refs_2_ = f32[64,2048]{1,0:T(8,128)S(1)} collective-permute-done((f32[64,2048]{1,0:T(8,128)S(1)}, f32[64,2048]{1,0:T(8,128)S(1)}, u32[]{:S(2)}, u32[]{:S(2)}) %collective-permute-start.11) | collective-permute-done | bytes 524320 | tf_op jit(solution)/shard_map/ppermute | solution.py:257
  55.8 0.8 filter.1
  56.5 0.1 collective-permute-start.12
  56.6 1.9 %collective-permute-start.13 = (f32[64,1536]{1,0:T(8,128)S(1)}, f32[64,1536]{1,0:T(8,128)S(1)}, u32[]{:S(2)}, u32[]{:S(2)}) collective-permute-start(f32[64,1536]{1,0:T(8,128)S(1)} %get-tuple-element.34), channel_id=1, source_target_pairs={{0,3},{2,14},{3,15},{7,4},{8,11},{12,0},{13,1},{15,12},{16,19},{18... | collective-permute-start | bytes 1179656 | tf_op jit(solution)/shard_map/ppermute | solution.py:253
  58.5 1.9 %collective-permute-start.15 = (f32[64,1024]{1,0:T(8,128)S(1)}, f32[64,1024]{1,0:T(8,128)S(1)}, u32[]{:S(2)}, u32[]{:S(2)}) collective-permute-start(f32[64,1024]{1,0:T(8,128)S(1)} %get-tuple-element.36), channel_id=1, source_target_pairs={{0,6},{1,7},{2,2},{3,3},{4,4},{5,5},{6,0},{7,1},{8,14},{9,15},{10,... | collective-permute-start | bytes 786440 | tf_op jit(solution)/shard_map/ppermute | solution.py:243
  60.5 4.5 %collective-permute-start.14 = (f32[64,512]{1,0:T(8,128)S(1)}, f32[64,512]{1,0:T(8,128)S(1)}, u32[]{:S(2)}, u32[]{:S(2)}) collective-permute-start(f32[64,512]{1,0:T(8,128)S(1)} %get-tuple-element.35), channel_id=1, source_target_pairs={{0,12},{1,13},{3,0},{4,7},{11,8},{12,15},{14,2},{15,3},{16,28},{17... | collective-permute-start | bytes 393224 | tf_op jit(solution)/shard_map/ppermute | solution.py:253
  65.0 5.7 %own_gram.1 = (f32[64,128]{1,0:T(8,128)S(1)}, f32[64,2048]{1,0:T(8,128)}) custom-call(s32[70]{0:T(128)S(1)} %pad_add_fusion.table_ref.place_ref, s32[1]{0:T(128)S(6)} %copy.13.live_ref, f32[64,2048]{1,0:T(8,128)S(1)} %get-tuple-element.28.field_ref, f32[64,2048]{1,0:T(8,128)S(1)} %collective-permute-done.12.flipped_ref, f32[16,4,128,128]{3,2,1,0:T(8,128)S(1)} %bitcast.6, ...), custom_call_target="tpu_custom_call" | custom-call | flops 536870912 | bytes 5767168 | tf_op jit(solution)/shard_map/own_gram/pallas_call | solution.py:305
  70.7 1.2 %collective-permute-done.13.refs_0_ = f32[64,1536]{1,0:T(8,128)S(1)} collective-permute-done((f32[64,1536]{1,0:T(8,128)S(1)}, f32[64,1536]{1,0:T(8,128)S(1)}, u32[]{:S(2)}, u32[]{:S(2)}) %collective-permute-start.13) | collective-permute-done | bytes 393248 | tf_op jit(solution)/shard_map/ppermute | solution.py:253
  71.8 0.7 collective-permute-done.15.refs_2_
  72.5 1.1 %crossed.1 = f32[64,128]{1,0:T(8,128)S(1)} custom-call(s32[70]{0:T(128)S(1)} %pad_add_fusion.table_ref.place_ref, f32[64,128]{1,0:T(8,128)S(1)} %get-tuple-element.33.own_ref, f32[64,2048]{1,0:T(8,128)S(1)} %get-tuple-element.28.field_ref, f32[64,1536]{1,0:T(8,128)S(1)} %collective-permute-done.13.refs_0_, f32[64,512]{1,0:T(8,128)S(1)} %collective-permute-done.14.refs_1_, ...), custom_call_target="tpu_custom_call" | custom-call | tf_op jit(solution)/shard_map/crossed/pallas_call | solution.py:374
  73.6 0.1 collective-permute-start.16
  73.7 1.2 %collective-permute-done.16 = f32[64,128]{1,0:T(8,128)S(1)} collective-permute-done((f32[64,128]{1,0:T(8,128)S(1)}, f32[64,128]{1,0:T(8,128)S(1)}, u32[]{:S(2)}, u32[]{:S(2)}) %collective-permute-start.16) | collective-permute-done | bytes 32800 | tf_op jit(solution)/shard_map/ppermute | solution.py:260
  74.9 0.7 collective-permute-start.18
  75.7 2.7 %collective-permute-start.17 = (f32[64,128]{1,0:T(8,128)S(1)}, f32[64,128]{1,0:T(8,128)S(1)}, u32[]{:S(2)}, u32[]{:S(2)}) collective-permute-start(f32[64,128]{1,0:T(8,128)S(1)} %add.23), channel_id=1, source_target_pairs={{0,2},{1,3},{2,0},{3,1},{4,6},{5,7},{6,4},{7,5},{8,10},{9,11},{10,... | collective-permute-start | bytes 98312 | tf_op jit(solution)/shard_map/ppermute | solution.py:260
  78.4 1.3 %collective-permute-done.19 = f32[64,128]{1,0:T(8,128)S(1)} collective-permute-done((f32[64,128]{1,0:T(8,128)S(1)}, f32[64,128]{1,0:T(8,128)S(1)}, u32[]{:S(2)}, u32[]{:S(2)}) %collective-permute-start.19) | collective-permute-done | bytes 32800 | tf_op jit(solution)/shard_map/ppermute | solution.py:260
  79.7 0.6 collective-permute-done.17
  80.3 0.4 collective-permute-start.20
  80.7 4.8 %collective-permute-done.20 = f32[64,128]{1,0:T(8,128)S(1)} collective-permute-done((f32[64,128]{1,0:T(8,128)S(1)}, f32[64,128]{1,0:T(8,128)S(1)}, u32[]{:S(2)}, u32[]{:S(2)}) %collective-permute-start.20) | collective-permute-done | bytes 32800 | tf_op jit(solution)/shard_map/ppermute | solution.py:260
  85.5 0.7 fusion
  (14 shorter events, 0.0 us)
Async XLA Ops:
  1.3 1.0 %copy-start.1 = (f32[64,2048]{1,0:T(8,128)S(1)}, f32[64,2048]{1,0:T(8,128)}, u32[]{:S(2)}) copy-start(f32[64,2048]{1,0:T(8,128)} %vectors_ref.1) | copy-start | bytes 1572868
  2.4 10.5 %collective-permute-start = (f32[64,2048]{1,0:T(8,128)S(1)}, f32[64,2048]{1,0:T(8,128)S(1)}, u32[]{:S(2)}, u32[]{:S(2)}) collective-permute-start(f32[64,2048]{1,0:T(8,128)S(1)} %get-tuple-element.20.field_ref.start_ref), channel_id=1, source_target_pairs={{0,1},{1,0},{2,3},{3,2},{4,5},{5,4},{6,7},{7,6},{8,9},{9,8},{10,11... | collective-permute-start | bytes 1572872 | tf_op jit(solution)/shard_map/ppermute | solution.py:260
  2.9 24.3 %collective-permute-start.1 = (f32[64,2048]{1,0:T(8,128)S(1)}, f32[64,2048]{1,0:T(8,128)S(1)}, u32[]{:S(2)}, u32[]{:S(2)}) collective-permute-start(f32[64,2048]{1,0:T(8,128)S(1)} %get-tuple-element.20.field_ref.start_ref), channel_id=1, source_target_pairs={{0,12},{1,13},{2,14},{3,15},{4,4},{5,5},{6,6},{7,7},{8,8},{9,9},{1... | collective-permute-start | bytes 1572872 | tf_op jit(solution)/shard_map/ppermute | solution.py:243
  9.4 10.1 %collective-permute-start.3 = (f32[32,2048]{1,0:T(8,128)S(1)}, f32[32,2048]{1,0:T(8,128)S(1)}, u32[]{:S(2)}, u32[]{:S(2)}) collective-permute-start(f32[32,2048]{1,0:T(8,128)S(1)} %get-tuple-element.22), channel_id=1, source_target_pairs={{0,2},{1,3},{6,4},{7,5},{8,10},{9,11},{14,12},{15,13},{16,18},{17,... | collective-permute-start | bytes 786440 | tf_op jit(solution)/shard_map/ppermute | solution.py:323
  12.9 15.7 %collective-permute-start.5 = (f32[64,2048]{1,0:T(8,128)S(1)}, f32[64,2048]{1,0:T(8,128)S(1)}, u32[]{:S(2)}, u32[]{:S(2)}) collective-permute-start(f32[64,2048]{1,0:T(8,128)S(1)} %collective-permute-done.flipped_ref), channel_id=1, source_target_pairs={{0,1},{1,3},{2,0},{3,2},{4,5},{5,7},{6,4},{7,6},{8,9},{9,11},{10,8... | collective-permute-start | bytes 1572872 | tf_op jit(solution)/shard_map/ppermute | solution.py:257
  12.9 15.6 %collective-permute-start.2 = (f32[32,2048]{1,0:T(8,128)S(1)}, f32[32,2048]{1,0:T(8,128)S(1)}, u32[]{:S(2)}, u32[]{:S(2)}) collective-permute-start(f32[32,2048]{1,0:T(8,128)S(1)} %get-tuple-element.21), channel_id=1, source_target_pairs={{0,6},{1,7},{2,2},{3,3},{4,4},{5,5},{6,0},{7,1},{8,14},{9,15},{10,... | collective-permute-start | bytes 786440 | tf_op jit(solution)/shard_map/ppermute | solution.py:243
  19.5 9.1 %collective-permute-start.4 = (f32[32,2048]{1,0:T(8,128)S(1)}, f32[32,2048]{1,0:T(8,128)S(1)}, u32[]{:S(2)}, u32[]{:S(2)}) collective-permute-start(f32[32,2048]{1,0:T(8,128)S(1)} %collective-permute-done.3), channel_id=1, source_target_pairs={{2,6},{3,7},{4,0},{5,1},{10,14},{11,15},{12,8},{13,9},{18,22},{19,... | collective-permute-start | bytes 786440 | tf_op jit(solution)/shard_map/ppermute | solution.py:323
  21.6 0.7 copy-start.2
  22.3 15.0 %copy-start = (f32[64,128,128]{2,1,0:T(8,128)S(1)}, f32[64,128,128]{2,1,0:T(8,128)}, u32[]{:S(2)}) copy-start(f32[64,128,128]{2,1,0:T(8,128)} %param.7) | copy-start | bytes 12582916
  29.3 8.0 %collective-permute-start.6 = (f32[64,2048]{1,0:T(8,128)S(1)}, f32[64,2048]{1,0:T(8,128)S(1)}, u32[]{:S(2)}, u32[]{:S(2)}) collective-permute-start(f32[64,2048]{1,0:T(8,128)S(1)} %get-tuple-element.23.field_ref), channel_id=1, source_target_pairs={{0,1},{1,0},{2,3},{3,2},{4,5},{5,4},{6,7},{7,6},{8,9},{9,8},{10,11... | collective-permute-start | bytes 1572872 | tf_op jit(solution)/shard_map/ppermute | solution.py:260
  29.3 18.0 %collective-permute-start.7 = (f32[64,2048]{1,0:T(8,128)S(1)}, f32[64,2048]{1,0:T(8,128)S(1)}, u32[]{:S(2)}, u32[]{:S(2)}) collective-permute-start(f32[64,2048]{1,0:T(8,128)S(1)} %get-tuple-element.23.field_ref), channel_id=1, source_target_pairs={{0,12},{1,13},{2,14},{3,15},{4,4},{5,5},{6,6},{7,7},{8,8},{9,9},{1... | collective-permute-start | bytes 1572872 | tf_op jit(solution)/shard_map/ppermute | solution.py:243
  31.3 12.6 %collective-permute-start.9 = (f32[32,2048]{1,0:T(8,128)S(1)}, f32[32,2048]{1,0:T(8,128)S(1)}, u32[]{:S(2)}, u32[]{:S(2)}) collective-permute-start(f32[32,2048]{1,0:T(8,128)S(1)} %get-tuple-element.26), channel_id=1, source_target_pairs={{0,2},{1,3},{6,4},{7,5},{8,10},{9,11},{14,12},{15,13},{16,18},{17,... | collective-permute-start | bytes 786440 | tf_op jit(solution)/shard_map/ppermute | solution.py:323
  41.0 14.8 %collective-permute-start.11 = (f32[64,2048]{1,0:T(8,128)S(1)}, f32[64,2048]{1,0:T(8,128)S(1)}, u32[]{:S(2)}, u32[]{:S(2)}) collective-permute-start(f32[64,2048]{1,0:T(8,128)S(1)} %collective-permute-done.6.flipped_ref), channel_id=1, source_target_pairs={{0,1},{1,3},{2,0},{3,2},{4,5},{5,7},{6,4},{7,6},{8,9},{9,11},{10,8... | collective-permute-start | bytes 1572872 | tf_op jit(solution)/shard_map/ppermute | solution.py:257
  41.0 13.4 %collective-permute-start.8 = (f32[32,2048]{1,0:T(8,128)S(1)}, f32[32,2048]{1,0:T(8,128)S(1)}, u32[]{:S(2)}, u32[]{:S(2)}) collective-permute-start(f32[32,2048]{1,0:T(8,128)S(1)} %get-tuple-element.25), channel_id=1, source_target_pairs={{0,6},{1,7},{2,2},{3,3},{4,4},{5,5},{6,0},{7,1},{8,14},{9,15},{10,... | collective-permute-start | bytes 786440 | tf_op jit(solution)/shard_map/ppermute | solution.py:243
  43.9 10.4 %collective-permute-start.10 = (f32[32,2048]{1,0:T(8,128)S(1)}, f32[32,2048]{1,0:T(8,128)S(1)}, u32[]{:S(2)}, u32[]{:S(2)}) collective-permute-start(f32[32,2048]{1,0:T(8,128)S(1)} %collective-permute-done.9), channel_id=1, source_target_pairs={{2,6},{3,7},{4,0},{5,1},{10,14},{11,15},{12,8},{13,9},{18,22},{19,... | collective-permute-start | bytes 786440 | tf_op jit(solution)/shard_map/ppermute | solution.py:323
  56.5 2.0 %collective-permute-start.12 = (f32[64,2048]{1,0:T(8,128)S(1)}, f32[64,2048]{1,0:T(8,128)S(1)}, u32[]{:S(2)}, u32[]{:S(2)}) collective-permute-start(f32[64,2048]{1,0:T(8,128)S(1)} %get-tuple-element.28.field_ref), channel_id=1, source_target_pairs={{0,1},{1,0},{2,3},{3,2},{4,5},{5,4},{6,7},{7,6},{8,9},{9,8},{10,11... | collective-permute-start | bytes 1572872 | tf_op jit(solution)/shard_map/ppermute | solution.py:260
  56.6 15.2 %collective-permute-start.13 = (f32[64,1536]{1,0:T(8,128)S(1)}, f32[64,1536]{1,0:T(8,128)S(1)}, u32[]{:S(2)}, u32[]{:S(2)}) collective-permute-start(f32[64,1536]{1,0:T(8,128)S(1)} %get-tuple-element.34), channel_id=1, source_target_pairs={{0,3},{2,14},{3,15},{7,4},{8,11},{12,0},{13,1},{15,12},{16,19},{18... | collective-permute-start | bytes 1179656 | tf_op jit(solution)/shard_map/ppermute | solution.py:253
  58.5 13.9 %collective-permute-start.15 = (f32[64,1024]{1,0:T(8,128)S(1)}, f32[64,1024]{1,0:T(8,128)S(1)}, u32[]{:S(2)}, u32[]{:S(2)}) collective-permute-start(f32[64,1024]{1,0:T(8,128)S(1)} %get-tuple-element.36), channel_id=1, source_target_pairs={{0,6},{1,7},{2,2},{3,3},{4,4},{5,5},{6,0},{7,1},{8,14},{9,15},{10,... | collective-permute-start | bytes 786440 | tf_op jit(solution)/shard_map/ppermute | solution.py:243
  60.5 11.3 %collective-permute-start.14 = (f32[64,512]{1,0:T(8,128)S(1)}, f32[64,512]{1,0:T(8,128)S(1)}, u32[]{:S(2)}, u32[]{:S(2)}) collective-permute-start(f32[64,512]{1,0:T(8,128)S(1)} %get-tuple-element.35), channel_id=1, source_target_pairs={{0,12},{1,13},{3,0},{4,7},{11,8},{12,15},{14,2},{15,3},{16,28},{17... | collective-permute-start | bytes 393224 | tf_op jit(solution)/shard_map/ppermute | solution.py:253
  73.6 1.3 %collective-permute-start.16 = (f32[64,128]{1,0:T(8,128)S(1)}, f32[64,128]{1,0:T(8,128)S(1)}, u32[]{:S(2)}, u32[]{:S(2)}) collective-permute-start(f32[64,128]{1,0:T(8,128)S(1)} %crossed.1), channel_id=1, source_target_pairs={{0,1},{1,0},{2,3},{3,2},{4,5},{5,4},{6,7},{7,6},{8,9},{9,8},{10,11... | collective-permute-start | bytes 98312 | tf_op jit(solution)/shard_map/ppermute | solution.py:260
  74.9 4.8 %collective-permute-start.19 = (f32[64,128]{1,0:T(8,128)S(1)}, f32[64,128]{1,0:T(8,128)S(1)}, u32[]{:S(2)}, u32[]{:S(2)}) collective-permute-start(f32[64,128]{1,0:T(8,128)S(1)} %add.23), channel_id=1, source_target_pairs={{0,6},{1,7},{2,4},{3,5},{4,2},{5,3},{6,0},{7,1},{8,14},{9,15},{10,... | collective-permute-start | bytes 98312 | tf_op jit(solution)/shard_map/ppermute | solution.py:260
  74.9 4.8 %collective-permute-start.18 = (f32[64,128]{1,0:T(8,128)S(1)}, f32[64,128]{1,0:T(8,128)S(1)}, u32[]{:S(2)}, u32[]{:S(2)}) collective-permute-start(f32[64,128]{1,0:T(8,128)S(1)} %add.23), channel_id=1, source_target_pairs={{0,4},{1,5},{2,6},{3,7},{4,0},{5,1},{6,2},{7,3},{8,12},{9,13},{10,... | collective-permute-start | bytes 98312 | tf_op jit(solution)/shard_map/ppermute | solution.py:260
  75.7 4.6 %collective-permute-start.17 = (f32[64,128]{1,0:T(8,128)S(1)}, f32[64,128]{1,0:T(8,128)S(1)}, u32[]{:S(2)}, u32[]{:S(2)}) collective-permute-start(f32[64,128]{1,0:T(8,128)S(1)} %add.23), channel_id=1, source_target_pairs={{0,2},{1,3},{2,0},{3,1},{4,6},{5,7},{6,4},{7,5},{8,10},{9,11},{10,... | collective-permute-start | bytes 98312 | tf_op jit(solution)/shard_map/ppermute | solution.py:260
  80.3 5.2 %collective-permute-start.20 = (f32[64,128]{1,0:T(8,128)S(1)}, f32[64,128]{1,0:T(8,128)S(1)}, u32[]{:S(2)}, u32[]{:S(2)}) collective-permute-start(f32[64,128]{1,0:T(8,128)S(1)} %add_add_fusion), channel_id=1, source_target_pairs={{0,8},{1,9},{2,10},{3,11},{4,12},{5,13},{6,14},{7,15},{8,0},{9,1},... | collective-permute-start | bytes 98312 | tf_op jit(solution)/shard_map/ppermute | solution.py:260

commit v7 on v2

--- a/solution.py
+++ b/solution.py
@@ -376,8 +376,7 @@
         compiler_params=params,
         name="crossed",
     )(table, grams, kept, *hops)
-    sums = sums + exchange(sums, 1)
-    for digit in range(1, bonds + 1, 2):
+    for digit in range(0, bonds + 1, 2):
         near_mask, far_mask = 1 << digit, 2 << digit
         pair = sums + exchange(sums, near_mask)
         if far_mask < dev_count:

time: 85.5 us -> 83.8 us (0.980)
  waiting for transfers between devices: 23.9 us -> 20.7 us
  starting transfers between devices: 38.1 us -> 39.7 us
    ppermute x8 -> x9, waiting for transfers between devices: 8.04 us -> 4.77 us  [exchange(): lax.ppermute(value, AXES, [(source, source ^ mask) for source in range(de...]
    ppermute x8 -> x9, starting transfers between devices: 5.51 us -> 7.05 us  [exchange(): lax.ppermute(value, AXES, [(source, source ^ mask) for source in range(de...]
  transfers between devices with their start and end apart: 21 -> 22, of which waited for: 10 -> 9; matrix products, arithmetic and copies ran while one was open for 1% -> 1% of each run, Pallas kernels for 18% -> 19%
where the time goes in v7:
time: 83.8 us; the launch traced here: 83.3 us
  starting transfers between devices  39.7 us (47%)
  waiting for transfers between devices  20.7 us (25%)
  Pallas kernels  18.2 us (22%)
  local copies, waits for them, and re-layouts  2.43 us (3%)
  between operations  1.53 us (2%)
    ppermute x5, starting transfers between devices, hop(): return lax.ppermute(value, AXES, pairs)  14.6 us
    ppermute x4, starting transfers between devices, apply(): aside = lax.ppermute(lax.ppermute(second_half, AXES, legs), AXES, round_way)  12 us
    ppermute x4, waiting for transfers between devices, apply(): aside = lax.ppermute(lax.ppermute(second_half, AXES, legs), AXES, round_way)  9.33 us
    ppermute x9, starting transfers between devices, exchange(): lax.ppermute(value, AXES, [(source, source ^ mask) for source in range(de...  7.05 us
    ppermute x2, starting transfers between devices, one_way(): return lax.ppermute(value, AXES, pairs)  5.99 us
    pallas_call x1, Pallas kernels, own_gram(): pl.pallas_call(functools.partial(own_gram_kernel, bonds + 1), out_shape=[...  5.68 us
    ppermute x5, waiting for transfers between devices, hop(): return lax.ppermute(value, AXES, pairs)  5.43 us
    pallas_call x1, Pallas kernels, first_own_part(): pl.pallas_call(functools.partial(first_own_kernel, bonds + 1), out_shape=...  4.92 us
  transfers between devices with their start and end apart: 22, of which 9 were waited for; matrix products, arithmetic and copies ran while one was open for 1% of the time, Pallas kernels for 19%

profile of v7, /device:TPU:0, one launch (start us, length us, event | category | flops | bytes accessed | tf_op | source)
XLA Modules:
  0.0 83.3 jit_solution(8228553149957720281)
XLA Ops:
  1.3 1.0 %copy-done.1 = f32[64,2048]{1,0:T(8,128)S(1)} copy-done((f32[64,2048]{1,0:T(8,128)S(1)}, f32[64,2048]{1,0:T(8,128)}, u32[]{:S(2)}) %copy-start.1) | copy-done | bytes 524312
  2.3 0.1 start.1
  2.4 0.5 collective-permute-start
  2.9 6.5 %collective-permute-start.1 = (f32[64,2048]{1,0:T(8,128)S(1)}, f32[64,2048]{1,0:T(8,128)S(1)}, u32[]{:S(2)}, u32[]{:S(2)}) collective-permute-start(f32[64,2048]{1,0:T(8,128)S(1)} %get-tuple-element.18.field_ref.start_ref), channel_id=1, source_target_pairs={{0,12},{1,13},{2,14},{3,15},{4,4},{5,5},{6,6},{7,7},{8,8},{9,9},{1... | collective-permute-start | bytes 1572872 | tf_op jit(solution)/shard_map/ppermute | solution.py:243
  9.4 3.4 %collective-permute-start.3 = (f32[32,2048]{1,0:T(8,128)S(1)}, f32[32,2048]{1,0:T(8,128)S(1)}, u32[]{:S(2)}, u32[]{:S(2)}) collective-permute-start(f32[32,2048]{1,0:T(8,128)S(1)} %get-tuple-element.20), channel_id=1, source_target_pairs={{0,2},{1,3},{6,4},{7,5},{8,10},{9,11},{14,12},{15,13},{16,18},{17,... | collective-permute-start | bytes 786440 | tf_op jit(solution)/shard_map/ppermute | solution.py:323
  12.9 0.0 collective-permute-done.flipped_ref
  12.9 0.0 collective-permute-start.5
  12.9 1.9 %collective-permute-start.2 = (f32[32,2048]{1,0:T(8,128)S(1)}, f32[32,2048]{1,0:T(8,128)S(1)}, u32[]{:S(2)}, u32[]{:S(2)}) collective-permute-start(f32[32,2048]{1,0:T(8,128)S(1)} %get-tuple-element.19), channel_id=1, source_target_pairs={{0,6},{1,7},{2,2},{3,3},{4,4},{5,5},{6,0},{7,1},{8,14},{9,15},{10,... | collective-permute-start | bytes 786440 | tf_op jit(solution)/shard_map/ppermute | solution.py:243
  14.9 4.7 %collective-permute-done.3 = f32[32,2048]{1,0:T(8,128)S(1)} collective-permute-done((f32[32,2048]{1,0:T(8,128)S(1)}, f32[32,2048]{1,0:T(8,128)S(1)}, u32[]{:S(2)}, u32[]{:S(2)}) %collective-permute-start.3) | collective-permute-done | bytes 262176 | tf_op jit(solution)/shard_map/ppermute | solution.py:323
  19.5 1.3 %collective-permute-start.4 = (f32[32,2048]{1,0:T(8,128)S(1)}, f32[32,2048]{1,0:T(8,128)S(1)}, u32[]{:S(2)}, u32[]{:S(2)}) collective-permute-start(f32[32,2048]{1,0:T(8,128)S(1)} %collective-permute-done.3), channel_id=1, source_target_pairs={{2,6},{3,7},{4,0},{5,1},{10,14},{11,15},{12,8},{13,9},{18,22},{19,... | collective-permute-start | bytes 786440 | tf_op jit(solution)/shard_map/ppermute | solution.py:323
  20.8 0.8 pad_add_fusion.table_ref.place_ref
  21.6 0.7 copy-done.2
  22.3 4.9 %first_own.1.own_ref = f32[64,2048]{1,0:T(8,128)S(1)} custom-call(s32[70]{0:T(128)S(1)} %pad_add_fusion.table_ref.place_ref, f32[64,2048]{1,0:T(8,128)S(1)} %get-tuple-element.18.field_ref.start_ref, f32[64,2048]{1,0:T(8,128)S(1)} %collective-permute-done.flipped_ref, f32[16,4,128,128]{3,2,1,0:T(8,128)} %bitcast.4, s32[1,2048]{1,0:T(1,128)S(1)} %bitcast.7), custom_call_target="tpu_custom_call" | custom-call | flops 536870912 | bytes 5767168 | tf_op jit(solution)/shard_map/first_own/pallas_call | solution.py:277
  27.2 0.6 far.2.own_ref
  27.8 0.7 collective-permute-done.2.refs_0_
  28.6 0.0 collective-permute-done.4.refs_1_
  28.6 0.0 collective-permute-done.5.refs_2_
  28.6 0.7 combine.1
  29.3 0.1 collective-permute-start.6
  29.3 1.9 %collective-permute-start.7 = (f32[64,2048]{1,0:T(8,128)S(1)}, f32[64,2048]{1,0:T(8,128)S(1)}, u32[]{:S(2)}, u32[]{:S(2)}) collective-permute-start(f32[64,2048]{1,0:T(8,128)S(1)} %get-tuple-element.21.field_ref), channel_id=1, source_target_pairs={{0,12},{1,13},{2,14},{3,15},{4,4},{5,5},{6,6},{7,7},{8,8},{9,9},{1... | collective-permute-start | bytes 1572872 | tf_op jit(solution)/shard_map/ppermute | solution.py:243
  31.3 6.0 %collective-permute-start.9 = (f32[32,2048]{1,0:T(8,128)S(1)}, f32[32,2048]{1,0:T(8,128)S(1)}, u32[]{:S(2)}, u32[]{:S(2)}) collective-permute-start(f32[32,2048]{1,0:T(8,128)S(1)} %get-tuple-element.23), channel_id=1, source_target_pairs={{0,2},{1,3},{6,4},{7,5},{8,10},{9,11},{14,12},{15,13},{16,18},{17,... | collective-permute-start | bytes 786440 | tf_op jit(solution)/shard_map/ppermute | solution.py:323
  37.3 0.0 collective-permute-done.6.flipped_ref
  37.3 0.0 collective-permute-start.11
  37.3 1.9 %collective-permute-start.8 = (f32[32,2048]{1,0:T(8,128)S(1)}, f32[32,2048]{1,0:T(8,128)S(1)}, u32[]{:S(2)}, u32[]{:S(2)}) collective-permute-start(f32[32,2048]{1,0:T(8,128)S(1)} %get-tuple-element.22), channel_id=1, source_target_pairs={{0,6},{1,7},{2,2},{3,3},{4,4},{5,5},{6,0},{7,1},{8,14},{9,15},{10,... | collective-permute-start | bytes 786440 | tf_op jit(solution)/shard_map/ppermute | solution.py:243
  39.2 4.7 %collective-permute-done.9 = f32[32,2048]{1,0:T(8,128)S(1)} collective-permute-done((f32[32,2048]{1,0:T(8,128)S(1)}, f32[32,2048]{1,0:T(8,128)S(1)}, u32[]{:S(2)}, u32[]{:S(2)}) %collective-permute-start.9) | collective-permute-done | bytes 262176 | tf_op jit(solution)/shard_map/ppermute | solution.py:323
  43.9 1.3 %collective-permute-start.10 = (f32[32,2048]{1,0:T(8,128)S(1)}, f32[32,2048]{1,0:T(8,128)S(1)}, u32[]{:S(2)}, u32[]{:S(2)}) collective-permute-start(f32[32,2048]{1,0:T(8,128)S(1)} %collective-permute-done.9), channel_id=1, source_target_pairs={{2,6},{3,7},{4,0},{5,1},{10,14},{11,15},{12,8},{13,9},{18,22},{19,... | collective-permute-start | bytes 786440 | tf_op jit(solution)/shard_map/ppermute | solution.py:323
  45.2 3.7 %own.1.own_ref = f32[64,2048]{1,0:T(8,128)S(1)} custom-call(s32[70]{0:T(128)S(1)} %pad_add_fusion.table_ref.place_ref, f32[64,2048]{1,0:T(8,128)S(1)} %get-tuple-element.21.field_ref, f32[64,2048]{1,0:T(8,128)S(1)} %collective-permute-done.6.flipped_ref, f32[16,4,128,128]{3,2,1,0:T(8,128)S(1)} %bitcast.5, s32[1,2048]{1,0:T(1,128)S(1)} %bitcast.8), custom_call_target="tpu_custom_call" | custom-call | flops 536870912 | bytes 5767168 | tf_op jit(solution)/shard_map/own/pallas_call | solution.py:293
  48.9 0.0 collective-permute-done.7.refs_0_
  48.9 0.6 far.3.own_ref
  49.5 4.7 %collective-permute-done.8.refs_0_ = f32[32,2048]{1,0:T(8,128)S(1)} collective-permute-done((f32[32,2048]{1,0:T(8,128)S(1)}, f32[32,2048]{1,0:T(8,128)S(1)}, u32[]{:S(2)}, u32[]{:S(2)}) %collective-permute-start.8) | collective-permute-done | bytes 262176 | tf_op jit(solution)/shard_map/ppermute | solution.py:243
  54.2 0.7 filter.1
  55.0 0.1 collective-permute-start.12
  55.1 1.9 %collective-permute-start.13 = (f32[64,1536]{1,0:T(8,128)S(1)}, f32[64,1536]{1,0:T(8,128)S(1)}, u32[]{:S(2)}, u32[]{:S(2)}) collective-permute-start(f32[64,1536]{1,0:T(8,128)S(1)} %get-tuple-element.30), channel_id=1, source_target_pairs={{0,3},{2,14},{3,15},{7,4},{8,11},{12,0},{13,1},{15,12},{16,19},{18... | collective-permute-start | bytes 1179656 | tf_op jit(solution)/shard_map/ppermute | solution.py:253
  57.0 2.3 %collective-permute-start.15 = (f32[64,1024]{1,0:T(8,128)S(1)}, f32[64,1024]{1,0:T(8,128)S(1)}, u32[]{:S(2)}, u32[]{:S(2)}) collective-permute-start(f32[64,1024]{1,0:T(8,128)S(1)} %get-tuple-element.32), channel_id=1, source_target_pairs={{0,6},{1,7},{2,2},{3,3},{4,4},{5,5},{6,0},{7,1},{8,14},{9,15},{10,... | collective-permute-start | bytes 786440 | tf_op jit(solution)/shard_map/ppermute | solution.py:243
  59.3 4.1 %collective-permute-start.14 = (f32[64,512]{1,0:T(8,128)S(1)}, f32[64,512]{1,0:T(8,128)S(1)}, u32[]{:S(2)}, u32[]{:S(2)}) collective-permute-start(f32[64,512]{1,0:T(8,128)S(1)} %get-tuple-element.31), channel_id=1, source_target_pairs={{0,12},{1,13},{3,0},{4,7},{11,8},{12,15},{14,2},{15,3},{16,28},{17... | collective-permute-start | bytes 393224 | tf_op jit(solution)/shard_map/ppermute | solution.py:253
  63.4 5.7 %own_gram.1 = (f32[64,128]{1,0:T(8,128)S(1)}, f32[64,2048]{1,0:T(8,128)}) custom-call(s32[70]{0:T(128)S(1)} %pad_add_fusion.table_ref.place_ref, s32[1]{0:T(128)S(6)} %copy.13.live_ref, f32[64,2048]{1,0:T(8,128)S(1)} %get-tuple-element.24.field_ref, f32[64,2048]{1,0:T(8,128)S(1)} %collective-permute-done.12.flipped_ref, f32[16,4,128,128]{3,2,1,0:T(8,128)S(1)} %bitcast.6, ...), custom_call_target="tpu_custom_call" | custom-call | flops 536870912 | bytes 5767168 | tf_op jit(solution)/shard_map/own_gram/pallas_call | solution.py:305
  69.1 1.2 %collective-permute-done.13.refs_0_ = f32[64,1536]{1,0:T(8,128)S(1)} collective-permute-done((f32[64,1536]{1,0:T(8,128)S(1)}, f32[64,1536]{1,0:T(8,128)S(1)}, u32[]{:S(2)}, u32[]{:S(2)}) %collective-permute-start.13) | collective-permute-done | bytes 393248 | tf_op jit(solution)/shard_map/ppermute | solution.py:253
  70.3 1.1 %crossed.1 = f32[64,128]{1,0:T(8,128)S(1)} custom-call(s32[70]{0:T(128)S(1)} %pad_add_fusion.table_ref.place_ref, f32[64,128]{1,0:T(8,128)S(1)} %get-tuple-element.29.own_ref, f32[64,2048]{1,0:T(8,128)S(1)} %get-tuple-element.24.field_ref, f32[64,1536]{1,0:T(8,128)S(1)} %collective-permute-done.13.refs_0_, f32[64,512]{1,0:T(8,128)S(1)} %collective-permute-done.14.refs_1_, ...), custom_call_target="tpu_custom_call" | custom-call | tf_op jit(solution)/shard_map/crossed/pallas_call | solution.py:371
  71.4 0.1 collective-permute-start.18
  71.5 1.3 %collective-permute-start.17 = (f32[64,128]{1,0:T(8,128)S(1)}, f32[64,128]{1,0:T(8,128)S(1)}, u32[]{:S(2)}, u32[]{:S(2)}) collective-permute-start(f32[64,128]{1,0:T(8,128)S(1)} %crossed.1), channel_id=1, source_target_pairs={{0,2},{1,3},{2,0},{3,1},{4,6},{5,7},{6,4},{7,5},{8,10},{9,11},{10,... | collective-permute-start | bytes 98312 | tf_op jit(solution)/shard_map/ppermute | solution.py:260
  72.8 0.5 collective-permute-start.16
  73.3 1.7 %collective-permute-done.18 = f32[64,128]{1,0:T(8,128)S(1)} collective-permute-done((f32[64,128]{1,0:T(8,128)S(1)}, f32[64,128]{1,0:T(8,128)S(1)}, u32[]{:S(2)}, u32[]{:S(2)}) %collective-permute-start.18) | collective-permute-done | bytes 32800 | tf_op jit(solution)/shard_map/ppermute | solution.py:260
  75.1 0.5 collective-permute-done.17
  75.5 2.2 %collective-permute-start.21 = (f32[64,128]{1,0:T(8,128)S(1)}, f32[64,128]{1,0:T(8,128)S(1)}, u32[]{:S(2)}, u32[]{:S(2)}) collective-permute-start(f32[64,128]{1,0:T(8,128)S(1)} %add_add_fusion.1), channel_id=1, source_target_pairs={{0,12},{1,13},{2,14},{3,15},{4,8},{5,9},{6,10},{7,11},{8,4},{9,5},... | collective-permute-start | bytes 98312 | tf_op jit(solution)/shard_map/ppermute | solution.py:260
  77.7 2.3 %collective-permute-start.19 = (f32[64,128]{1,0:T(8,128)S(1)}, f32[64,128]{1,0:T(8,128)S(1)}, u32[]{:S(2)}, u32[]{:S(2)}) collective-permute-start(f32[64,128]{1,0:T(8,128)S(1)} %add_add_fusion.1), channel_id=1, source_target_pairs={{0,4},{1,5},{2,6},{3,7},{4,0},{5,1},{6,2},{7,3},{8,12},{9,13},{10,... | collective-permute-start | bytes 98312 | tf_op jit(solution)/shard_map/ppermute | solution.py:260
  80.0 1.4 %collective-permute-done.21 = f32[64,128]{1,0:T(8,128)S(1)} collective-permute-done((f32[64,128]{1,0:T(8,128)S(1)}, f32[64,128]{1,0:T(8,128)S(1)}, u32[]{:S(2)}, u32[]{:S(2)}) %collective-permute-start.21) | collective-permute-done | bytes 32800 | tf_op jit(solution)/shard_map/ppermute | solution.py:260
  81.4 1.2 %collective-permute-done.20 = f32[64,128]{1,0:T(8,128)S(1)} collective-permute-done((f32[64,128]{1,0:T(8,128)S(1)}, f32[64,128]{1,0:T(8,128)S(1)}, u32[]{:S(2)}, u32[]{:S(2)}) %collective-permute-start.20) | collective-permute-done | bytes 32800 | tf_op jit(solution)/shard_map/ppermute | solution.py:260
  82.6 0.7 fusion
  (15 shorter events, 0.1 us)
Async XLA Ops:
  1.3 1.0 %copy-start.1 = (f32[64,2048]{1,0:T(8,128)S(1)}, f32[64,2048]{1,0:T(8,128)}, u32[]{:S(2)}) copy-start(f32[64,2048]{1,0:T(8,128)} %vectors_ref.1) | copy-start | bytes 1572868
  2.4 10.5 %collective-permute-start = (f32[64,2048]{1,0:T(8,128)S(1)}, f32[64,2048]{1,0:T(8,128)S(1)}, u32[]{:S(2)}, u32[]{:S(2)}) collective-permute-start(f32[64,2048]{1,0:T(8,128)S(1)} %get-tuple-element.18.field_ref.start_ref), channel_id=1, source_target_pairs={{0,1},{1,0},{2,3},{3,2},{4,5},{5,4},{6,7},{7,6},{8,9},{9,8},{10,11... | collective-permute-start | bytes 1572872 | tf_op jit(solution)/shard_map/ppermute | solution.py:260
  2.9 24.3 %collective-permute-start.1 = (f32[64,2048]{1,0:T(8,128)S(1)}, f32[64,2048]{1,0:T(8,128)S(1)}, u32[]{:S(2)}, u32[]{:S(2)}) collective-permute-start(f32[64,2048]{1,0:T(8,128)S(1)} %get-tuple-element.18.field_ref.start_ref), channel_id=1, source_target_pairs={{0,12},{1,13},{2,14},{3,15},{4,4},{5,5},{6,6},{7,7},{8,8},{9,9},{1... | collective-permute-start | bytes 1572872 | tf_op jit(solution)/shard_map/ppermute | solution.py:243
  9.4 10.1 %collective-permute-start.3 = (f32[32,2048]{1,0:T(8,128)S(1)}, f32[32,2048]{1,0:T(8,128)S(1)}, u32[]{:S(2)}, u32[]{:S(2)}) collective-permute-start(f32[32,2048]{1,0:T(8,128)S(1)} %get-tuple-element.20), channel_id=1, source_target_pairs={{0,2},{1,3},{6,4},{7,5},{8,10},{9,11},{14,12},{15,13},{16,18},{17,... | collective-permute-start | bytes 786440 | tf_op jit(solution)/shard_map/ppermute | solution.py:323
  12.9 15.7 %collective-permute-start.5 = (f32[64,2048]{1,0:T(8,128)S(1)}, f32[64,2048]{1,0:T(8,128)S(1)}, u32[]{:S(2)}, u32[]{:S(2)}) collective-permute-start(f32[64,2048]{1,0:T(8,128)S(1)} %collective-permute-done.flipped_ref), channel_id=1, source_target_pairs={{0,1},{1,3},{2,0},{3,2},{4,5},{5,7},{6,4},{7,6},{8,9},{9,11},{10,8... | collective-permute-start | bytes 1572872 | tf_op jit(solution)/shard_map/ppermute | solution.py:257
  12.9 15.6 %collective-permute-start.2 = (f32[32,2048]{1,0:T(8,128)S(1)}, f32[32,2048]{1,0:T(8,128)S(1)}, u32[]{:S(2)}, u32[]{:S(2)}) collective-permute-start(f32[32,2048]{1,0:T(8,128)S(1)} %get-tuple-element.19), channel_id=1, source_target_pairs={{0,6},{1,7},{2,2},{3,3},{4,4},{5,5},{6,0},{7,1},{8,14},{9,15},{10,... | collective-permute-start | bytes 786440 | tf_op jit(solution)/shard_map/ppermute | solution.py:243
  19.5 9.1 %collective-permute-start.4 = (f32[32,2048]{1,0:T(8,128)S(1)}, f32[32,2048]{1,0:T(8,128)S(1)}, u32[]{:S(2)}, u32[]{:S(2)}) collective-permute-start(f32[32,2048]{1,0:T(8,128)S(1)} %collective-permute-done.3), channel_id=1, source_target_pairs={{2,6},{3,7},{4,0},{5,1},{10,14},{11,15},{12,8},{13,9},{18,22},{19,... | collective-permute-start | bytes 786440 | tf_op jit(solution)/shard_map/ppermute | solution.py:323
  21.6 0.7 copy-start.2
  22.3 22.9 %copy-start = (f32[64,128,128]{2,1,0:T(8,128)S(1)}, f32[64,128,128]{2,1,0:T(8,128)}, u32[]{:S(2)}) copy-start(f32[64,128,128]{2,1,0:T(8,128)} %param.7) | copy-start | bytes 12582916
  29.3 8.0 %collective-permute-start.6 = (f32[64,2048]{1,0:T(8,128)S(1)}, f32[64,2048]{1,0:T(8,128)S(1)}, u32[]{:S(2)}, u32[]{:S(2)}) collective-permute-start(f32[64,2048]{1,0:T(8,128)S(1)} %get-tuple-element.21.field_ref), channel_id=1, source_target_pairs={{0,1},{1,0},{2,3},{3,2},{4,5},{5,4},{6,7},{7,6},{8,9},{9,8},{10,11... | collective-permute-start | bytes 1572872 | tf_op jit(solution)/shard_map/ppermute | solution.py:260
  29.3 19.5 %collective-permute-start.7 = (f32[64,2048]{1,0:T(8,128)S(1)}, f32[64,2048]{1,0:T(8,128)S(1)}, u32[]{:S(2)}, u32[]{:S(2)}) collective-permute-start(f32[64,2048]{1,0:T(8,128)S(1)} %get-tuple-element.21.field_ref), channel_id=1, source_target_pairs={{0,12},{1,13},{2,14},{3,15},{4,4},{5,5},{6,6},{7,7},{8,8},{9,9},{1... | collective-permute-start | bytes 1572872 | tf_op jit(solution)/shard_map/ppermute | solution.py:243
  31.3 12.6 %collective-permute-start.9 = (f32[32,2048]{1,0:T(8,128)S(1)}, f32[32,2048]{1,0:T(8,128)S(1)}, u32[]{:S(2)}, u32[]{:S(2)}) collective-permute-start(f32[32,2048]{1,0:T(8,128)S(1)} %get-tuple-element.23), channel_id=1, source_target_pairs={{0,2},{1,3},{6,4},{7,5},{8,10},{9,11},{14,12},{15,13},{16,18},{17,... | collective-permute-start | bytes 786440 | tf_op jit(solution)/shard_map/ppermute | solution.py:323
  37.3 16.9 %collective-permute-start.11 = (f32[64,2048]{1,0:T(8,128)S(1)}, f32[64,2048]{1,0:T(8,128)S(1)}, u32[]{:S(2)}, u32[]{:S(2)}) collective-permute-start(f32[64,2048]{1,0:T(8,128)S(1)} %collective-permute-done.6.flipped_ref), channel_id=1, source_target_pairs={{0,1},{1,3},{2,0},{3,2},{4,5},{5,7},{6,4},{7,6},{8,9},{9,11},{10,8... | collective-permute-start | bytes 1572872 | tf_op jit(solution)/shard_map/ppermute | solution.py:257
  37.3 16.9 %collective-permute-start.8 = (f32[32,2048]{1,0:T(8,128)S(1)}, f32[32,2048]{1,0:T(8,128)S(1)}, u32[]{:S(2)}, u32[]{:S(2)}) collective-permute-start(f32[32,2048]{1,0:T(8,128)S(1)} %get-tuple-element.22), channel_id=1, source_target_pairs={{0,6},{1,7},{2,2},{3,3},{4,4},{5,5},{6,0},{7,1},{8,14},{9,15},{10,... | collective-permute-start | bytes 786440 | tf_op jit(solution)/shard_map/ppermute | solution.py:243
  43.9 10.3 %collective-permute-start.10 = (f32[32,2048]{1,0:T(8,128)S(1)}, f32[32,2048]{1,0:T(8,128)S(1)}, u32[]{:S(2)}, u32[]{:S(2)}) collective-permute-start(f32[32,2048]{1,0:T(8,128)S(1)} %collective-permute-done.9), channel_id=1, source_target_pairs={{2,6},{3,7},{4,0},{5,1},{10,14},{11,15},{12,8},{13,9},{18,22},{19,... | collective-permute-start | bytes 786440 | tf_op jit(solution)/shard_map/ppermute | solution.py:323
  55.0 2.0 %collective-permute-start.12 = (f32[64,2048]{1,0:T(8,128)S(1)}, f32[64,2048]{1,0:T(8,128)S(1)}, u32[]{:S(2)}, u32[]{:S(2)}) collective-permute-start(f32[64,2048]{1,0:T(8,128)S(1)} %get-tuple-element.24.field_ref), channel_id=1, source_target_pairs={{0,1},{1,0},{2,3},{3,2},{4,5},{5,4},{6,7},{7,6},{8,9},{9,8},{10,11... | collective-permute-start | bytes 1572872 | tf_op jit(solution)/shard_map/ppermute | solution.py:260
  55.1 15.2 %collective-permute-start.13 = (f32[64,1536]{1,0:T(8,128)S(1)}, f32[64,1536]{1,0:T(8,128)S(1)}, u32[]{:S(2)}, u32[]{:S(2)}) collective-permute-start(f32[64,1536]{1,0:T(8,128)S(1)} %get-tuple-element.30), channel_id=1, source_target_pairs={{0,3},{2,14},{3,15},{7,4},{8,11},{12,0},{13,1},{15,12},{16,19},{18... | collective-permute-start | bytes 1179656 | tf_op jit(solution)/shard_map/ppermute | solution.py:253
  57.0 13.3 %collective-permute-start.15 = (f32[64,1024]{1,0:T(8,128)S(1)}, f32[64,1024]{1,0:T(8,128)S(1)}, u32[]{:S(2)}, u32[]{:S(2)}) collective-permute-start(f32[64,1024]{1,0:T(8,128)S(1)} %get-tuple-element.32), channel_id=1, source_target_pairs={{0,6},{1,7},{2,2},{3,3},{4,4},{5,5},{6,0},{7,1},{8,14},{9,15},{10,... | collective-permute-start | bytes 786440 | tf_op jit(solution)/shard_map/ppermute | solution.py:243
  59.3 10.9 %collective-permute-start.14 = (f32[64,512]{1,0:T(8,128)S(1)}, f32[64,512]{1,0:T(8,128)S(1)}, u32[]{:S(2)}, u32[]{:S(2)}) collective-permute-start(f32[64,512]{1,0:T(8,128)S(1)} %get-tuple-element.31), channel_id=1, source_target_pairs={{0,12},{1,13},{3,0},{4,7},{11,8},{12,15},{14,2},{15,3},{16,28},{17... | collective-permute-start | bytes 393224 | tf_op jit(solution)/shard_map/ppermute | solution.py:253
  71.4 3.6 %collective-permute-start.18 = (f32[64,128]{1,0:T(8,128)S(1)}, f32[64,128]{1,0:T(8,128)S(1)}, u32[]{:S(2)}, u32[]{:S(2)}) collective-permute-start(f32[64,128]{1,0:T(8,128)S(1)} %crossed.1), channel_id=1, source_target_pairs={{0,3},{1,2},{2,1},{3,0},{4,7},{5,6},{6,5},{7,4},{8,11},{9,10},{10,... | collective-permute-start | bytes 98312 | tf_op jit(solution)/shard_map/ppermute | solution.py:260
  71.5 4.0 %collective-permute-start.17 = (f32[64,128]{1,0:T(8,128)S(1)}, f32[64,128]{1,0:T(8,128)S(1)}, u32[]{:S(2)}, u32[]{:S(2)}) collective-permute-start(f32[64,128]{1,0:T(8,128)S(1)} %crossed.1), channel_id=1, source_target_pairs={{0,2},{1,3},{2,0},{3,1},{4,6},{5,7},{6,4},{7,5},{8,10},{9,11},{10,... | collective-permute-start | bytes 98312 | tf_op jit(solution)/shard_map/ppermute | solution.py:260
  72.8 2.7 %collective-permute-start.16 = (f32[64,128]{1,0:T(8,128)S(1)}, f32[64,128]{1,0:T(8,128)S(1)}, u32[]{:S(2)}, u32[]{:S(2)}) collective-permute-start(f32[64,128]{1,0:T(8,128)S(1)} %crossed.1), channel_id=1, source_target_pairs={{0,1},{1,0},{2,3},{3,2},{4,5},{5,4},{6,7},{7,6},{8,9},{9,8},{10,11... | collective-permute-start | bytes 98312 | tf_op jit(solution)/shard_map/ppermute | solution.py:260
  75.5 5.8 %collective-permute-start.21 = (f32[64,128]{1,0:T(8,128)S(1)}, f32[64,128]{1,0:T(8,128)S(1)}, u32[]{:S(2)}, u32[]{:S(2)}) collective-permute-start(f32[64,128]{1,0:T(8,128)S(1)} %add_add_fusion.1), channel_id=1, source_target_pairs={{0,12},{1,13},{2,14},{3,15},{4,8},{5,9},{6,10},{7,11},{8,4},{9,5},... | collective-permute-start | bytes 98312 | tf_op jit(solution)/shard_map/ppermute | solution.py:260
  77.7 4.9 %collective-permute-start.20 = (f32[64,128]{1,0:T(8,128)S(1)}, f32[64,128]{1,0:T(8,128)S(1)}, u32[]{:S(2)}, u32[]{:S(2)}) collective-permute-start(f32[64,128]{1,0:T(8,128)S(1)} %add_add_fusion.1), channel_id=1, source_target_pairs={{0,8},{1,9},{2,10},{3,11},{4,12},{5,13},{6,14},{7,15},{8,0},{9,1},... | collective-permute-start | bytes 98312 | tf_op jit(solution)/shard_map/ppermute | solution.py:260
  77.7 4.9 %collective-permute-start.19 = (f32[64,128]{1,0:T(8,128)S(1)}, f32[64,128]{1,0:T(8,128)S(1)}, u32[]{:S(2)}, u32[]{:S(2)}) collective-permute-start(f32[64,128]{1,0:T(8,128)S(1)} %add_add_fusion.1), channel_id=1, source_target_pairs={{0,4},{1,5},{2,6},{3,7},{4,0},{5,1},{6,2},{7,3},{8,12},{9,13},{10,... | collective-permute-start | bytes 98312 | tf_op jit(solution)/shard_map/ppermute | solution.py:260
